TPU v7x, 256 devices: a whole 4x4x8 slice. The times are simulated.
256 devices in a mesh: date: 64 (over x, z, core), row: 4 (over y).
Axes of the slice: x: 4, y: 4, z: 8, core: 2. Of those that a mesh axis runs over, the one named last changes fastest.
Arguments:
- acquisitions: bfloat16 [256, 2, 512, 2048], P('date', None, 'row'), may hold values from -4 to 4
- date_pairs: int32 [1024, 2], P('date'), may hold values from 0 to 255, as said below
- cycle_maps: int32 [1024, 128, 128], P('date', 'row'), may hold values from 0 to 1
- inverse: float32 [256, 1024], P(None, 'date'), may hold values from -0.046875 to 0.046875
Outputs:
- displacement: float32 [128, 128, 256], P('date', 'row')
Inputs may be any that keep to these rules, and one draw needn't show every extreme that they name: `date_pairs`: pair k's first date lies in dates j * 4 to (j + 1) * 4 - 1 with j = k // 16; its second date is (first + gap) mod 256 with gap from 1 to 4; each aligned block of 16 pairs holds a pair with gap 4.
All inputs are finite; a program needn't handle non-finite values.
Results may differ from a plain program's by a relative error of at most 0.0003.
Values may be sent and summed in bfloat16 or wider, within the bound.
No kernel may reach another device: no remote copies, remote signals or barrier semaphores. Data moves between devices by JAX's collectives and lax.ppermute only.
A program may use at most 64 MiB of HBM per device.

v0:
```python
from functools import partial
import math

import jax
import jax.numpy as jnp
from jax import lax
from jax.sharding import PartitionSpec as P

LOOK_R = 4
LOOK_C = 16


TWO_PI = 2.0 * math.pi


def passed_along(value, axis, steps):
    count = lax.axis_size(axis)
    pairs = [(source, (source + steps) % count) for source in range(count)]
    return lax.ppermute(value, axis, pairs)


def form_pair(images, column_sums, pair_dates):
    reference_image = lax.dynamic_index_in_dim(images, pair_dates[0], 0, keepdims=False).astype(
        jnp.float32
    )
    second_image = lax.dynamic_index_in_dim(images, pair_dates[1], 0, keepdims=False).astype(
        jnp.float32
    )
    real_part = reference_image[0] * second_image[0] + reference_image[1] * second_image[1]
    imag_part = reference_image[1] * second_image[0] - reference_image[0] * second_image[1]
    height, width = real_part.shape
    real_rows = real_part.reshape(height // LOOK_R, LOOK_R, width).sum(axis=1)
    imag_rows = imag_part.reshape(height // LOOK_R, LOOK_R, width).sum(axis=1)
    stacked = jnp.concatenate([real_rows, imag_rows], axis=0)
    looked = jnp.dot(
        stacked, column_sums, precision=lax.Precision.HIGHEST, preferred_element_type=jnp.float32
    )
    half = height // LOOK_R
    return jnp.arctan2(looked[half:], looked[:half])


def body(acquisitions, date_pairs, cycle_maps, inverse):
    date_count = acquisitions.shape[0]
    date_devices = lax.axis_size("date")
    total_dates = date_count * date_devices
    date_base = lax.axis_index("date") * date_count
    following = passed_along(acquisitions, "date", -1)
    extended = jnp.concatenate([acquisitions, following], axis=0)
    first_local = date_pairs[:, 0] - date_base
    second_local = (date_pairs[:, 1] - date_base + total_dates) % total_dates
    local_pairs = jnp.stack([first_local, second_local], axis=1)
    width = acquisitions.shape[3]
    column_index = jnp.arange(width, dtype=jnp.int32) // LOOK_C
    look_index = jnp.arange(width // LOOK_C, dtype=jnp.int32)
    column_sums = (column_index[:, None] == look_index[None, :]).astype(jnp.float32)
    wrapped = lax.map(partial(form_pair, extended, column_sums), local_pairs)
    phase = wrapped - TWO_PI * cycle_maps.astype(jnp.float32)
    pair_count, look_rows, look_cols = phase.shape
    pixel_total = look_rows * lax.axis_size("row") * look_cols
    band_mean = lax.psum(jnp.sum(phase, axis=(1, 2)), "row") / pixel_total
    values = phase - band_mean[:, None, None]
    pixel_rows = values.transpose(0, 2, 1).reshape(pair_count, look_cols * look_rows)
    date_total = inverse.shape[0]
    product = lax.dot_general(
        pixel_rows,
        inverse,
        (((0,), (1,)), ((), ())),
        precision=lax.Precision.HIGHEST,
        preferred_element_type=jnp.float32,
    )
    result = lax.psum_scatter(product, "date", scatter_dimension=0, tiled=True)
    return result.reshape(look_cols // date_devices, look_rows, date_total)


def solution(mesh):
    return jax.shard_map(
        body,
        mesh=mesh,
        in_specs=(
            P("date", None, "row", None),
            P("date", None),
            P("date", "row", None),
            P(None, "date"),
        ),
        out_specs=P("date", "row", None),
        check_vma=False,
    )
```

profile of v0, /device:TPU:6, one launch (start us, length us, event | category | flops | bytes accessed | tf_op | source)
XLA Modules:
  0.0 391.9 jit_solution(520398919884927568)
XLA Ops:
  6.5 5.6 %collective-permute-start = (bf16[4,2,128,2048]{3,2,1,0:T(8,128)(2,1)}, bf16[4,2,128,2048]{3,2,1,0:T(8,128)(2,1)}, u32[]{:S(2)}, u32[]{:S(2)}) collective-permute-start(bf16[4,2,128,2048]{3,2,1,0:T(8,128)(2,1)} %param.6), channel_id=1, source_target_pairs={{0,252},{4,0},{8,4},{12,8},{16,12},{20,16},{24,20},{28,24},{32,28}... | collective-permute-start | bytes 12582920 | tf_op jit(solution)/shard_map/ppermute | solution.py:19
  12.1 0.8 slice_subtract_fusion
  12.9 45.5 %collective-permute-done = bf16[4,2,128,2048]{3,2,1,0:T(8,128)(2,1)} collective-permute-done((bf16[4,2,128,2048]{3,2,1,0:T(8,128)(2,1)}, bf16[4,2,128,2048]{3,2,1,0:T(8,128)(2,1)}, u32[]{:S(2)}, u32[]{:S(2)}) %collective-permute-start) | collective-permute-done | bytes 4194336 | tf_op jit(solution)/shard_map/ppermute | solution.py:19
  58.4 7.4 %pad_maximum_fusion = bf16[8,2,128,2048]{3,2,1,0:T(8,128)(2,1)} fusion(bf16[4,2,128,2048]{3,2,1,0:T(8,128)(2,1)} %collective-permute-done, bf16[4,2,128,2048]{3,2,1,0:T(8,128)(2,1)} %param.6), kind=kLoop, calls=%fused_computation.17 | loop fusion | flops 4194304 | bytes 16777216 | tf_op jit(solution)/shard_map/concatenate | solution.py:48
  65.9 161.2 %while.11 = (s32[]{:T(128)}, f32[16,32,128]{2,1,0:T(8,128)}, s32[16,2]{0,1:T(2,128)S(1)}, bf16[8,2,128,2048]{3,2,1,0:T(8,128)(2,1)}, s32[2048]{0:T(1024)S(1)}, /*index=5*/s32[]{:T(128)}, s32[]{:T(128)}, s32[]{:T(128)}, f32[]{:T(128)}) while((s32[]{:T(128)}, f32[16,32,128]{2,1,0:T(8,128)}, s32[16,2]{0,1:T(2,128)S(1)}, ...), condition=%wide.region_3.4_spmd.clone, body=%wide.region_0.3_spmd.clone.sunk | while | flops 204996608 | bytes 20013780 | solution.py:56
  70.0 2.1 dynamic-slice_convert_fusion.3
  74.4 0.9 fusion.28
  75.3 0.6 fusion.29
  80.1 2.1 dynamic-slice_convert_fusion.3
  84.4 0.9 fusion.28
  90.2 2.1 dynamic-slice_convert_fusion.3
  94.5 0.9 fusion.28
  95.4 0.6 fusion.29
  100.3 2.1 dynamic-slice_convert_fusion.3
  104.6 0.9 fusion.28
  110.3 2.1 dynamic-slice_convert_fusion.3
  114.7 0.9 fusion.28
  120.4 2.1 dynamic-slice_convert_fusion.3
  124.7 0.9 fusion.28
  130.5 2.1 dynamic-slice_convert_fusion.3
  134.8 0.9 fusion.28
  135.7 0.6 fusion.29
  140.6 2.1 dynamic-slice_convert_fusion.3
  144.9 0.9 fusion.28
  150.6 2.1 dynamic-slice_convert_fusion.3
  154.9 0.9 fusion.28
  160.7 2.1 dynamic-slice_convert_fusion.3
  165.0 0.9 fusion.28
  170.8 2.1 dynamic-slice_convert_fusion.3
  175.1 0.9 fusion.28
  176.0 0.7 fusion.29
  180.8 2.1 dynamic-slice_convert_fusion.3
  185.2 0.9 fusion.28
  190.9 2.1 dynamic-slice_convert_fusion.3
  195.2 0.9 fusion.28
  201.0 2.1 dynamic-slice_convert_fusion.3
  205.3 0.9 fusion.28
  206.2 0.6 fusion.29
  211.1 2.1 dynamic-slice_convert_fusion.3
  215.4 0.9 fusion.28
  221.1 2.1 dynamic-slice_convert_fusion.3
  225.5 0.9 fusion.28
  226.4 0.7 fusion.29
  227.0 1.2 fusion.11
  228.2 10.7 %psum.7 = f32[16]{0:T(128)S(1)} all-reduce(f32[16]{0:T(128)S(1)} %fusion.11), channel_id=1, replica_groups=mesh['date'=64,'row'=4] {'row'}, use_global_device_ids=true, to_apply=%region_5.6 | all-reduce | flops 16 | bytes 128 | tf_op jit(solution)/shard_map/psum | solution.py:60
  238.9 1.0 subtract_bitcast_fusion
  240.8 5.0 %fusion.17 = f32[4096,256]{1,0:T(8,128)} fusion(f32[16,4096]{1,0:T(8,128)S(1)} %reshape.54, f32[256,16]{0,1:T(8,128)S(1)} %copy-done), kind=kOutput, calls=%fused_computation.36 | convolution fusion | flops 201326592 | bytes 4472832 | tf_op jit(solution)/shard_map/dot_general | solution.py:64
  245.8 139.2 %reduce-scatter.2.cloned.1.call-done = f32[64,256]{1,0:T(8,128)} async-done(((f32[4096,256]{1,0:T(8,128)}), f32[64,256]{1,0:T(8,128)}) %reduce-scatter.2.cloned.1.call-update) | async-done | bytes 65552 | tf_op jit(solution)/shard_map/reduce_scatter | solution.py:71
  (134 shorter events, 52.5 us)
Async XLA Ops:
  6.5 234.3 %copy-start = (f32[256,16]{0,1:T(8,128)S(1)}, f32[256,16]{0,1:T(8,128)}, u32[]{:S(2)}) copy-start(f32[256,16]{0,1:T(8,128)} %param.9) | copy-start | bytes 49156
  6.5 378.5 %reduce-scatter.2.cloned.1.call-start = ((), (), s32[]{:S(2)}) async-start(), calls=%async_computation.1 | async-start | bytes 4259840 | tf_op jit(solution)/shard_map/reduce_scatter | solution.py:71
  6.5 51.9 %collective-permute-start = (bf16[4,2,128,2048]{3,2,1,0:T(8,128)(2,1)}, bf16[4,2,128,2048]{3,2,1,0:T(8,128)(2,1)}, u32[]{:S(2)}, u32[]{:S(2)}) collective-permute-start(bf16[4,2,128,2048]{3,2,1,0:T(8,128)(2,1)} %param.6), channel_id=1, source_target_pairs={{0,252},{4,0},{8,4},{12,8},{16,12},{20,16},{24,20},{28,24},{32,28}... | collective-permute-start | bytes 12582920 | tf_op jit(solution)/shard_map/ppermute | solution.py:19
  65.8 161.2 %copy-start.1 = (s32[16,32,128]{2,1,0:T(8,128)S(1)}, s32[16,32,128]{2,1,0:T(8,128)}, u32[]{:S(2)}) copy-start(s32[16,32,128]{2,1,0:T(8,128)} %param.8) | copy-start | bytes 786436
Sparse Core Ops, SparseCore 0:
  245.9 139.0 reduce-scatter.1
where the time goes:
time: 394 us; the launch traced here: 392 us
  waiting for transfers between devices  185 us (47%)
  other arithmetic  69.1 us (18%)
  loops' own time  58.2 us (15%)
  local copies, waits for them, and re-layouts  30.6 us (8%)
  matrix products  19.4 us (5%)
  between operations  13.4 us (3%)
  blocking collectives  10.7 us (3%)
  starting transfers between devices  5.56 us (1%)
    reduce_scatter x1, waiting for transfers between devices, body(): result = lax.psum_scatter(product, 'date', scatter_dimension=0, tiled=True)  139 us
    another operation x1, loops' own time, body(): wrapped = lax.map(partial(form_pair, extended, column_sums), local_pairs)  58.2 us
    ppermute x1, waiting for transfers between devices, passed_along(): return lax.ppermute(value, axis, pairs)  45.5 us
    convert_element_type x16, other arithmetic, form_pair(): lax.dynamic_index_in_dim(images, pair_dates[0], 0, keepdims=False)  33 us
    dot_general x16, matrix products, form_pair(): jnp.dot(stacked, column_sums, precision=lax.Precision.HIGHEST, preferred_...  14.4 us
    psum x1, blocking collectives, body(): band_mean = lax.psum(jnp.sum(phase, axis=(1, 2)), 'row') / pixel_total  10.7 us
    dynamic_update_slice x16, local copies, waits for them, and re-layouts, body(): wrapped = lax.map(partial(form_pair, extended, column_sums), local_pairs)  10.3 us
    reduce_sum x16, other arithmetic, form_pair(): real_rows = real_part.reshape(height // LOOK_R, LOOK_R, width).sum(axis=1)  10.1 us
  transfers between devices with their start and end apart: 2, of which 2 were waited for; matrix products, arithmetic and copies ran while one was open for 0% of the time, Pallas kernels for 0%

commit v1 on v0

v1 whole, which is shorter than its diff:
```python
from functools import partial
import math

import jax
import jax.numpy as jnp
from jax import lax
from jax.experimental import pallas as pl
from jax.experimental.pallas import tpu as pltpu
from jax.sharding import PartitionSpec as P

LOOK_R = 4
LOOK_C = 16
TWO_PI = 2.0 * math.pi
CHUNKS = 4
STEP = 256
LANES = 128


def passed_along(value, axis, steps):
    count = lax.axis_size(axis)
    pairs = [(source, (source + steps) % count) for source in range(count)]
    return lax.ppermute(value, axis, pairs)


def phase_kernel(pairs_ref, top_own, top_next, low_prev, low_own, cycles, sums_in, *rest):
    payload, sums, images, high, low = rest[-5:]
    group, _, rows, width = top_own.shape
    looks = rows // LOOK_R
    pair_count = pairs_ref.shape[0] // 4
    out_cols = width // LOOK_C

    @pl.when(pl.program_id(0) == 0)
    def _():
        sums[...] = sums_in[...]

    for half, (first, second) in enumerate(((top_own, top_next), (low_prev, low_own))):
        for at, source in enumerate((first, second)):
            for date in range(group):
                for part in range(2):
                    for tile in range(width // LANES):
                        images[half, at * group + date, part, tile] = source[
                            date, part, :, tile * LANES : (tile + 1) * LANES
                        ].astype(jnp.float32)

    for half in range(2):

        @pl.loop(0, pair_count)
        def _(pair, half=half):
            a = pairs_ref[(half * pair_count + pair) * 2]
            b = pairs_ref[(half * pair_count + pair) * 2 + 1]
            for tile in range(width // LANES):
                real = imag = None
                for step in range(LOOK_R):
                    at = pl.ds(step, looks, stride=LOOK_R)
                    a0, a1 = images[half, a, 0, tile, at, :], images[half, a, 1, tile, at, :]
                    b0, b1 = images[half, b, 0, tile, at, :], images[half, b, 1, tile, at, :]
                    re, im = a0 * b0 + a1 * b1, a1 * b0 - a0 * b1
                    real, imag = (re, im) if real is None else (real + re, imag + im)
                for part, value in enumerate((real, imag)):
                    base = part * pair_count * 2 * looks + half * looks
                    place = pl.ds(pl.multiple_of(pair * 2 * looks + base, 16), looks)
                    head = value.astype(jnp.bfloat16)
                    high[place, tile * LANES : (tile + 1) * LANES] = head
                    low[place, tile * LANES : (tile + 1) * LANES] = (value - head.astype(jnp.float32)).astype(
                        jnp.bfloat16
                    )

    shape = (out_cols, width)
    picked = lax.broadcasted_iota(jnp.int32, shape, 1) // LOOK_C == lax.broadcasted_iota(jnp.int32, shape, 0)
    picked = jnp.where(picked, 1.0, 0.0).astype(jnp.bfloat16)
    turned = (((1,), (1,)), ((), ()))
    looked = lax.dot_general(picked, high[...], turned, preferred_element_type=jnp.float32)
    looked += lax.dot_general(picked, low[...], turned, preferred_element_type=jnp.float32)
    half_width = looked.shape[1] // 2
    real, imag = looked[:, :half_width], looked[:, half_width:]
    phase = jnp.arctan2(imag, real) - cycles[...]
    total = jnp.sum(phase, axis=0, keepdims=True)
    blocks = half_width // LANES
    for q in range(blocks):
        payload[pl.ds(q, out_cols, stride=blocks), :] = phase[:, q * LANES : (q + 1) * LANES]
        sums[q : q + 1, :] += total[:, q * LANES : (q + 1) * LANES]


def phases(chunk, chunk_width, pairs, acquisitions, following, previous, cycles, sums, payload):
    group, _, height, width = acquisitions.shape
    rows = height // 2
    steps = chunk_width // STEP
    lanes = cycles.shape[1]
    out_cols = STEP // LOOK_C
    block_rows = out_cols * lanes // LANES
    payload_shape = (cycles.shape[0] * lanes // LANES, LANES)
    looks = rows // LOOK_R
    pair_count = lanes // (2 * looks)
    whole = (group, 2, rows, STEP)

    in_specs = [
        pl.BlockSpec(whole, lambda i, p: (0, 0, 0, chunk * steps + i)),
        pl.BlockSpec(whole, lambda i, p: (0, 0, 0, i)),
        pl.BlockSpec(whole, lambda i, p: (0, 0, 0, i)),
        pl.BlockSpec(whole, lambda i, p: (0, 0, 1, chunk * steps + i)),
        pl.BlockSpec((out_cols, lanes), lambda i, p: (chunk * steps + i, 0)),
        pl.BlockSpec((8, LANES), lambda i, p: (0, 0)),
    ]
    operands = [pairs, acquisitions, following, previous, acquisitions, cycles, sums]
    aliases = {}
    if payload is not None:
        in_specs.append(pl.BlockSpec(memory_space=pl.ANY))
        aliases = {len(operands): 0}
        operands.append(payload)
    return pl.pallas_call(
        phase_kernel,
        grid_spec=pltpu.PrefetchScalarGridSpec(
            num_scalar_prefetch=1,
            grid=(steps,),
            in_specs=in_specs,
            out_specs=[
                pl.BlockSpec((block_rows, LANES), lambda i, p: (chunk * steps + i, 0)),
                pl.BlockSpec((8, LANES), lambda i, p: (0, 0)),
            ],
            scratch_shapes=[
                pltpu.VMEM((2, 2 * group, 2, STEP // LANES, rows, LANES), jnp.float32),
                pltpu.VMEM((2 * lanes, STEP), jnp.bfloat16),
                pltpu.VMEM((2 * lanes, STEP), jnp.bfloat16),
            ],
        ),
        out_shape=[
            jax.ShapeDtypeStruct(payload_shape, jnp.float32),
            jax.ShapeDtypeStruct((8, LANES), jnp.float32),
        ],
        input_output_aliases=aliases,
        compiler_params=pltpu.CompilerParams(vmem_limit_bytes=24 << 20),
        cost_estimate=pl.CostEstimate(
            flops=10 * pair_count * height * chunk_width,
            bytes_accessed=group * 2 * height * chunk_width * 4,
            transcendentals=0,
        ),
        name="phases",
    )(*operands)


def invert_kernel(band_pixels, received, inverse, sums, out, left):
    sources = inverse.shape[0] // 16
    pair_count = 16
    blocks = 4
    per = pair_count // blocks
    rows = LANES // per
    pixels = out.shape[0]

    def aligned(value):
        rolled = pltpu.roll(value, sources - 1, 0)
        lane = lax.broadcasted_iota(jnp.int32, value.shape, 1) % rows
        return jnp.where(lane < rows // 2, value, rolled).T

    left[pixels:, :] = jnp.zeros((left.shape[0] - pixels, left.shape[1]), jnp.float32)
    for q in range(blocks):
        for col in range(pixels // rows):
            turned = aligned(received[pl.ds(col * blocks + q, sources, stride=8), :])
            for at in range(per):
                pair = q * per + at
                left[col * rows : (col + 1) * rows, pair * sources : (pair + 1) * sources] = turned[
                    at * rows : (at + 1) * rows
                ]
        turned = aligned(sums[pl.ds(q, sources, stride=8), :])
        for at in range(per):
            pair = q * per + at
            left[pixels : pixels + 1, pair * sources : (pair + 1) * sources] = jnp.sum(
                turned[at * rows : (at + 1) * rows], axis=0, keepdims=True
            )
    product = jnp.dot(
        left[...], inverse[...], precision=lax.Precision.HIGHEST, preferred_element_type=jnp.float32
    )
    out[...] = product[:pixels] - product[pixels : pixels + 1] * (1.0 / band_pixels)


def invert(received, inverse, sums, pixels, band_pixels):
    total_pairs, dates = inverse.shape
    return pl.pallas_call(
        partial(invert_kernel, band_pixels),
        in_specs=[pl.BlockSpec(memory_space=pltpu.VMEM)] * 3,
        out_specs=pl.BlockSpec(memory_space=pltpu.VMEM),
        out_shape=jax.ShapeDtypeStruct((pixels, dates), jnp.float32),
        scratch_shapes=[
            pltpu.VMEM((pixels + 8, total_pairs), jnp.float32),
        ],
        compiler_params=pltpu.CompilerParams(vmem_limit_bytes=24 << 20),
        name="invert",
    )(received, inverse, sums)


def body(acquisitions, date_pairs, cycle_maps, inverse):
    group, _, height, width = acquisitions.shape
    devices = lax.axis_size("date")
    total_dates = group * devices
    pair_count, look_rows, look_cols = cycle_maps.shape
    rows = height // 2
    half = look_rows // 2

    base = lax.axis_index("date") * group
    local = jnp.stack([date_pairs[:, 0] - base, (date_pairs[:, 1] - base + total_dates) % total_dates], axis=1)
    pairs = jnp.concatenate([local, passed_along(local, "date", 1)], axis=0).reshape(-1)

    low_cycles = passed_along(cycle_maps[:, half:].astype(jnp.bfloat16), "date", 1)
    cycles = jnp.concatenate(
        [cycle_maps[:, :half].astype(jnp.float32), low_cycles.astype(jnp.float32)], axis=1
    )
    cycles = (TWO_PI * cycles).reshape(pair_count * look_rows, look_cols).T

    whole_inverse = lax.all_gather(inverse.T, "date", axis=1).reshape(-1, total_dates)

    chunk_width = width // CHUNKS
    following, previous = [], []
    for chunk in range(CHUNKS):
        cols = slice(chunk * chunk_width, (chunk + 1) * chunk_width)
        following.append(passed_along(acquisitions[:, :, :rows, cols], "date", -1))
        previous.append(passed_along(acquisitions[:, :, rows:, cols], "date", 1))

    payload, sums = None, jnp.zeros((8, LANES), jnp.float32)
    for chunk in range(CHUNKS):
        payload, sums = phases(
            chunk, chunk_width, pairs, acquisitions, following[chunk], previous[chunk], cycles, sums, payload
        )

    received = lax.all_to_all(
        payload.reshape(devices, -1, LANES), "date", split_axis=0, concat_axis=0, tiled=True
    ).reshape(payload.shape)
    sums = lax.psum(sums, "row")
    sums = lax.all_gather(sums, "date", axis=0, tiled=True)
    out_cols = look_cols // devices
    band_pixels = look_rows * look_cols * lax.axis_size("row")
    result = invert(received, whole_inverse, sums, out_cols * look_rows, band_pixels)
    return result.reshape(out_cols, look_rows, total_dates)


def solution(mesh):
    return jax.shard_map(
        body,
        mesh=mesh,
        in_specs=(
            P("date", None, "row", None),
            P("date", None),
            P("date", "row", None),
            P(None, "date"),
        ),
        out_specs=P("date", "row", None),
        check_vma=False,
    )
```

time: 394 us -> 141 us (0.36)
  waiting for transfers between devices: 185 us -> 8.18 us
  other arithmetic: 69.1 us -> 0.88 us
  loops' own time: 58.2 us -> 0 us
  blocking collectives: 10.7 us -> 54.6 us
  starting transfers between devices: 5.56 us -> 30.4 us
  Pallas kernels: 0 us -> 21.7 us
  local copies, waits for them, and re-layouts: 30.6 us -> 8.91 us
  matrix products: 19.4 us -> 0 us
    reduce_scatter x1 -> x0, waiting for transfers between devices: 139 us -> none  [body(): result = lax.psum_scatter(product, 'date', scatter_dimension=0, tiled=True)]
    another operation x1 -> x0, loops' own time: 58.2 us -> none  [body(): wrapped = lax.map(partial(form_pair, extended, column_sums), local_pairs)]
    all_gather x0 -> x1, blocking collectives: none -> 43.8 us  [body(): sums = lax.all_gather(sums, 'date', axis=0, tiled=True)]
    ppermute x1 -> x10, waiting for transfers between devices: 45.5 us -> 7.46 us  [passed_along(): return lax.ppermute(value, axis, pairs)]
    convert_element_type x16 -> x2, other arithmetic: 33 us -> 0.03 us  [the longest x1 0.02 us: body(): cycle_maps[:, :half].astype(jnp.float32)]
    pallas_call x0 -> x5, Pallas kernels: none -> 21.7 us  [the longest x4 20.1 us: phases(): pl.pallas_call(phase_kernel, grid_spec=pltpu.PrefetchScalarGridSpec(num_s...]
    reduce_sum x33 -> x0, other arithmetic: 21.4 us -> none  [the longest x16 10.1 us: form_pair(): real_rows = real_part.reshape(height // LOOK_R, LOOK_R, width).sum(axis=1)]
    dot_general x17 -> x0, matrix products: 19.4 us -> none  [the longest x16 14.4 us: form_pair(): jnp.dot(stacked, column_sums, precision=lax.Precision.HIGHEST, preferred_...]
  transfers between devices with their start and end apart: 2 -> 12, of which waited for: 2 -> 1; matrix products, arithmetic and copies ran while one was open for 0% -> 5% of each run, Pallas kernels for 0% -> 15%
where the time goes in v1:
time: 141 us; the launch traced here: 138 us
  blocking collectives  54.6 us (39%)
  starting transfers between devices  30.4 us (22%)
  Pallas kernels  21.7 us (15%)
  between operations  13.5 us (10%)
  local copies, waits for them, and re-layouts  8.91 us (6%)
  waiting for transfers between devices  8.18 us (6%)
    all_gather x1, blocking collectives, body(): sums = lax.all_gather(sums, 'date', axis=0, tiled=True)  43.8 us
    pallas_call x4, Pallas kernels, phases(): pl.pallas_call(phase_kernel, grid_spec=pltpu.PrefetchScalarGridSpec(num_s...  20.1 us
    ppermute x10, starting transfers between devices, passed_along(): return lax.ppermute(value, axis, pairs)  17.3 us
    all_to_all x1, starting transfers between devices, body(): lax.all_to_all(payload.reshape(devices, -1, LANES), 'date', split_axis=0,...  13.1 us
    psum x1, blocking collectives, body(): sums = lax.psum(sums, 'row')  10.8 us
    ppermute x10, waiting for transfers between devices, passed_along(): return lax.ppermute(value, axis, pairs)  7.46 us
    slice x1, local copies, waits for them, and re-layouts, body(): previous.append(passed_along(acquisitions[:, :, rows:, cols], 'date', 1))  4.06 us
  transfers between devices with their start and end apart: 12, of which 1 were waited for; matrix products, arithmetic and copies ran while one was open for 5% of the time, Pallas kernels for 15%

profile of v1, /device:TPU:6, one launch (start us, length us, event | category | flops | bytes accessed | tf_op | source)
XLA Modules:
  0.0 138.2 jit_solution(11039119585510273883)
XLA Ops:
  6.5 0.0 all-gather.3.cloned.1.call-start
  6.5 0.7 all-gather.3.cloned.1.call-update
  7.3 0.0 copy-start.1
  7.3 0.0 copy-start.2
  7.3 4.1 %fusion.1 = (bf16[4,2,64,512]{3,2,1,0:T(8,128)(2,1)S(1)}, bf16[4,2,64,512]{3,2,1,0:T(8,128)(2,1)}, bf16[4,2,64,512]{3,2,1,0:T(8,128)(2,1)}, bf16[4,2,64,512]{3,2...) fusion(bf16[4,2,128,2048]{3,2,1,0:T(8,128)(2,1)} %low_own.7), kind=kLoop, calls=%fused_computation.10 | loop fusion | bytes 8388608 | tf_op jit(solution)/shard_map/slice | solution.py:215
  11.3 5.6 %collective-permute-start.8 = (bf16[4,2,64,512]{3,2,1,0:T(8,128)(2,1)}, bf16[4,2,64,512]{3,2,1,0:T(8,128)(2,1)S(1)}, u32[]{:S(2)}, u32[]{:S(2)}) collective-permute-start(bf16[4,2,64,512]{3,2,1,0:T(8,128)(2,1)} %get-tuple-element.22), channel_id=1, source_target_pairs={{0,252},{4,0},{8,4},{12,8},{16,12},{20,16},{24,20},{28,24},{32,28}... | collective-permute-start | bytes 1572872 | tf_op jit(solution)/shard_map/ppermute | solution.py:22
  16.9 0.0 collective-permute-start.9
  16.9 3.9 %collective-permute-start.6 = (bf16[4,2,64,512]{3,2,1,0:T(8,128)(2,1)}, bf16[4,2,64,512]{3,2,1,0:T(8,128)(2,1)S(1)}, u32[]{:S(2)}, u32[]{:S(2)}) collective-permute-start(bf16[4,2,64,512]{3,2,1,0:T(8,128)(2,1)} %get-tuple-element.24), channel_id=1, source_target_pairs={{0,252},{4,0},{8,4},{12,8},{16,12},{20,16},{24,20},{28,24},{32,28}... | collective-permute-start | bytes 1572872 | tf_op jit(solution)/shard_map/ppermute | solution.py:22
  20.8 0.0 copy-done.1
  20.8 0.1 collective-permute-start.3
  20.9 0.0 copy-done.2
  20.9 0.1 collective-permute-start
  21.0 7.4 %collective-permute-done = s32[16,2]{0,1:T(2,128)S(1)} collective-permute-done((s32[16,2]{0,1:T(2,128)S(1)}, s32[16,2]{0,1:T(2,128)S(1)}, u32[]{:S(2)}, u32[]{:S(2)}) %collective-permute-start) | collective-permute-done | bytes 160 | tf_op jit(solution)/shard_map/ppermute | solution.py:22
  28.4 0.0 collective-permute-start.7
  28.5 0.0 collective-permute-done.3
  28.5 3.9 %collective-permute-start.4 = (bf16[4,2,64,512]{3,2,1,0:T(8,128)(2,1)}, bf16[4,2,64,512]{3,2,1,0:T(8,128)(2,1)S(1)}, u32[]{:S(2)}, u32[]{:S(2)}) collective-permute-start(bf16[4,2,64,512]{3,2,1,0:T(8,128)(2,1)} %get-tuple-element.26), channel_id=1, source_target_pairs={{0,252},{4,0},{8,4},{12,8},{16,12},{20,16},{24,20},{28,24},{32,28}... | collective-permute-start | bytes 1572872 | tf_op jit(solution)/shard_map/ppermute | solution.py:22
  32.3 0.0 collective-permute-done.8.top_next
  32.3 0.0 collective-permute-start.5
  32.3 0.0 collective-permute-done.9.low_prev
  32.3 3.9 %collective-permute-start.1 = (bf16[4,2,64,512]{3,2,1,0:T(8,128)(2,1)}, bf16[4,2,64,512]{3,2,1,0:T(8,128)(2,1)S(1)}, u32[]{:S(2)}, u32[]{:S(2)}) collective-permute-start(bf16[4,2,64,512]{3,2,1,0:T(8,128)(2,1)} %get-tuple-element.28), channel_id=1, source_target_pairs={{0,252},{4,0},{8,4},{12,8},{16,12},{20,16},{24,20},{28,24},{32,28}... | collective-permute-start | bytes 1572872 | tf_op jit(solution)/shard_map/ppermute | solution.py:22
  36.2 0.0 collective-permute-done.6.top_next
  36.2 0.0 collective-permute-start.2
  36.2 0.1 pad_add_fusion.1
  36.3 0.1 copy.10
  36.3 0.1 reshape.19.pairs_ref
  36.5 0.8 maximum_multiply_fusion
  37.2 1.1 copy.11
  38.3 0.0 copy-start
  38.3 2.2 %copy-done = bf16[4,2,128,2048]{3,2,1,0:T(8,128)(2,1)S(1)} copy-done((bf16[4,2,128,2048]{3,2,1,0:T(8,128)(2,1)S(1)}, bf16[4,2,128,2048]{3,2,1,0:T(8,128)(2,1)}, u32[]{:S(2)}) %copy-start) | copy-done | bytes 4194328
  40.5 4.7 %phases.4 = (f32[512,128]{1,0:T(8,128)}, f32[8,128]{1,0:T(8,128)S(1)}) custom-call(s32[64]{0:T(128)S(1)} %reshape.19.pairs_ref, bf16[4,2,128,2048]{3,2,1,0:T(8,128)(2,1)S(1)} %copy-done, bf16[4,2,64,512]{3,2,1,0:T(8,128)(2,1)S(1)} %collective-permute-done.8.top_next, bf16[4,2,64,512]{3,2,1,0:T(8,128)(2,1)S(1)} %collective-permute-done.9.low_prev, ...), custom_call_target="tpu_custom_call" | custom-call | flops 10485760 | bytes 2097152 | tf_op jit(solution)/shard_map/phases/pallas_call | solution.py:110
  45.2 0.0 collective-permute-done.7.low_prev
  45.2 4.7 %phases.5 = (f32[512,128]{1,0:T(8,128)}, f32[8,128]{1,0:T(8,128)S(1)}) custom-call(s32[64]{0:T(128)S(1)} %reshape.19.pairs_ref, bf16[4,2,128,2048]{3,2,1,0:T(8,128)(2,1)S(1)} %copy-done, bf16[4,2,64,512]{3,2,1,0:T(8,128)(2,1)S(1)} %collective-permute-done.6.top_next, ...), custom_call_target="tpu_custom_call", output_to_operand_aliasing={{0}: (7, {})} | custom-call | flops 10485760 | bytes 2097152 | tf_op jit(solution)/shard_map/phases/pallas_call | solution.py:110
  49.8 0.0 collective-permute-done.4.top_next
  49.8 0.0 collective-permute-done.5.low_prev
  49.8 5.4 %phases.6 = (f32[512,128]{1,0:T(8,128)}, f32[8,128]{1,0:T(8,128)S(1)}) custom-call(s32[64]{0:T(128)S(1)} %reshape.19.pairs_ref, bf16[4,2,128,2048]{3,2,1,0:T(8,128)(2,1)S(1)} %copy-done, bf16[4,2,64,512]{3,2,1,0:T(8,128)(2,1)S(1)} %collective-permute-done.4.top_next, ...), custom_call_target="tpu_custom_call", output_to_operand_aliasing={{0}: (7, {})} | custom-call | flops 10485760 | bytes 2097152 | tf_op jit(solution)/shard_map/phases/pallas_call | solution.py:110
  55.2 0.0 collective-permute-done.1.top_next
  55.2 0.0 collective-permute-done.2.low_prev
  55.2 5.4 %phases.7 = (f32[512,128]{1,0:T(8,128)}, f32[8,128]{1,0:T(8,128)S(1)}) custom-call(s32[64]{0:T(128)S(1)} %reshape.19.pairs_ref, bf16[4,2,128,2048]{3,2,1,0:T(8,128)(2,1)S(1)} %copy-done, bf16[4,2,64,512]{3,2,1,0:T(8,128)(2,1)S(1)} %collective-permute-done.1.top_next, ...), custom_call_target="tpu_custom_call", output_to_operand_aliasing={{0}: (7, {})} | custom-call | flops 10485760 | bytes 2097152 | tf_op jit(solution)/shard_map/phases/pallas_call | solution.py:110
  60.6 13.1 %all-to-all-start = ((f32[64,8,128]{2,1,0:T(8,128)}), f32[64,8,128]{2,1,0:T(8,128)S(1)}, u32[]{:S(2)}, u32[]{:S(2)}) async-start(f32[64,8,128]{2,1,0:T(8,128)} %bitcast.2), calls=%async_computation | async-start | bytes 524288 | tf_op jit(solution)/shard_map/all_to_all | solution.py:223
  73.8 10.8 %psum.7 = f32[8,128]{1,0:T(8,128)S(1)} all-reduce(f32[8,128]{1,0:T(8,128)S(1)} %get-tuple-element.20), channel_id=1, replica_groups=mesh['date'=64,'row'=4] {'row'}, use_global_device_ids=true, to_apply=%region_0.1 | all-reduce | flops 1024 | bytes 8192 | tf_op jit(solution)/shard_map/psum | solution.py:226
  84.5 43.8 %all_gather.11.sums = f32[512,128]{1,0:T(8,128)S(1)} all-gather(f32[8,128]{1,0:T(8,128)S(1)} %psum.7), channel_id=1, replica_groups=mesh['date'=64,'row'=4] {'date'}, dimensions={0}, use_global_device_ids=true | all-gather | bytes 266240 | tf_op jit(solution)/shard_map/all_gather | solution.py:227
  128.4 0.0 all-gather.3.cloned.1.call-done
  128.4 1.4 %reshape.22.inverse = f32[1024,256]{1,0:T(8,128)S(1)} reshape(f32[16,16384]{1,0:T(8,128)} %all-gather.3.cloned.1.call-done) | data formatting | bytes 2097152 | tf_op jit(solution)/shard_map/reshape | solution.py:208
  129.8 0.0 all-to-all-done
  129.8 1.5 %invert.1 = f32[64,256]{1,0:T(8,128)} custom-call(f32[512,128]{1,0:T(8,128)S(1)} %bitcast.10, f32[1024,256]{1,0:T(8,128)S(1)} %reshape.22.inverse, f32[512,128]{1,0:T(8,128)S(1)} %all_gather.11.sums), custom_call_target="tpu_custom_call" | custom-call | tf_op jit(solution)/shard_map/invert/pallas_call | solution.py:177
  (5 shorter events, 0.1 us)
Async XLA Ops:
  6.5 121.8 %all-gather.3.cloned.1.call-start = ((), (), s32[]{:S(2)}) async-start(), calls=%async_computation.1 | async-start | bytes 1064960 | tf_op jit(solution)/shard_map/all_gather | solution.py:208
  7.3 13.5 %copy-start.1 = (s32[16,32,128]{2,1,0:T(8,128)S(1)}, s32[16,32,128]{2,1,0:T(8,128)}, u32[]{:S(2)}) copy-start(s32[16,32,128]{2,1,0:T(8,128)} %param.6) | copy-start | bytes 786436
  7.3 13.6 %copy-start.2 = (s32[16,2]{0,1:T(2,128)S(1)}, s32[16,2]{0,1:T(2,128)}, u32[]{:S(2)}) copy-start(s32[16,2]{0,1:T(2,128)} %param.5) | copy-start | bytes 388
  11.3 21.0 %collective-permute-start.8 = (bf16[4,2,64,512]{3,2,1,0:T(8,128)(2,1)}, bf16[4,2,64,512]{3,2,1,0:T(8,128)(2,1)S(1)}, u32[]{:S(2)}, u32[]{:S(2)}) collective-permute-start(bf16[4,2,64,512]{3,2,1,0:T(8,128)(2,1)} %get-tuple-element.22), channel_id=1, source_target_pairs={{0,252},{4,0},{8,4},{12,8},{16,12},{20,16},{24,20},{28,24},{32,28}... | collective-permute-start | bytes 1572872 | tf_op jit(solution)/shard_map/ppermute | solution.py:22
  16.9 15.4 %collective-permute-start.9 = (bf16[4,2,64,512]{3,2,1,0:T(8,128)(2,1)S(1)}, bf16[4,2,64,512]{3,2,1,0:T(8,128)(2,1)S(1)}, u32[]{:S(2)}, u32[]{:S(2)}) collective-permute-start(bf16[4,2,64,512]{3,2,1,0:T(8,128)(2,1)S(1)} %get-tuple-element.21), channel_id=1, source_target_pairs={{0,4},{4,8},{8,12},{12,16},{16,20},{20,24},{24,28},{28,32},{32,36}... | collective-permute-start | bytes 1572872 | tf_op jit(solution)/shard_map/ppermute | solution.py:22
  16.9 19.3 %collective-permute-start.6 = (bf16[4,2,64,512]{3,2,1,0:T(8,128)(2,1)}, bf16[4,2,64,512]{3,2,1,0:T(8,128)(2,1)S(1)}, u32[]{:S(2)}, u32[]{:S(2)}) collective-permute-start(bf16[4,2,64,512]{3,2,1,0:T(8,128)(2,1)} %get-tuple-element.24), channel_id=1, source_target_pairs={{0,252},{4,0},{8,4},{12,8},{16,12},{20,16},{24,20},{28,24},{32,28}... | collective-permute-start | bytes 1572872 | tf_op jit(solution)/shard_map/ppermute | solution.py:22
  20.8 7.7 %collective-permute-start.3 = (bf16[16,16,128]{2,1,0:T(8,128)(2,1)S(1)}, bf16[16,16,128]{2,1,0:T(8,128)(2,1)S(1)}, u32[]{:S(2)}, u32[]{:S(2)}) collective-permute-start(bf16[16,16,128]{2,1,0:T(8,128)(2,1)S(1)} %get-tuple-element.30), channel_id=1, source_target_pairs={{0,4},{4,8},{8,12},{12,16},{16,20},{20,24},{24,28},{28,32},{32,36}... | collective-permute-start | bytes 196616 | tf_op jit(solution)/shard_map/ppermute | solution.py:22
  20.9 7.5 %collective-permute-start = (s32[16,2]{0,1:T(2,128)S(1)}, s32[16,2]{0,1:T(2,128)S(1)}, u32[]{:S(2)}, u32[]{:S(2)}) collective-permute-start(s32[16,2]{0,1:T(2,128)S(1)} %pad_add_fusion), channel_id=1, source_target_pairs={{0,4},{4,8},{8,12},{12,16},{16,20},{20,24},{24,28},{28,32},{32,36}... | collective-permute-start | bytes 392 | tf_op jit(solution)/shard_map/ppermute | solution.py:22
  28.4 16.7 %collective-permute-start.7 = (bf16[4,2,64,512]{3,2,1,0:T(8,128)(2,1)}, bf16[4,2,64,512]{3,2,1,0:T(8,128)(2,1)S(1)}, u32[]{:S(2)}, u32[]{:S(2)}) collective-permute-start(bf16[4,2,64,512]{3,2,1,0:T(8,128)(2,1)} %get-tuple-element.23), channel_id=1, source_target_pairs={{0,4},{4,8},{8,12},{12,16},{16,20},{20,24},{24,28},{28,32},{32,36}... | collective-permute-start | bytes 1572872 | tf_op jit(solution)/shard_map/ppermute | solution.py:22
  28.5 21.4 %collective-permute-start.4 = (bf16[4,2,64,512]{3,2,1,0:T(8,128)(2,1)}, bf16[4,2,64,512]{3,2,1,0:T(8,128)(2,1)S(1)}, u32[]{:S(2)}, u32[]{:S(2)}) collective-permute-start(bf16[4,2,64,512]{3,2,1,0:T(8,128)(2,1)} %get-tuple-element.26), channel_id=1, source_target_pairs={{0,252},{4,0},{8,4},{12,8},{16,12},{20,16},{24,20},{28,24},{32,28}... | collective-permute-start | bytes 1572872 | tf_op jit(solution)/shard_map/ppermute | solution.py:22
  32.3 17.5 %collective-permute-start.5 = (bf16[4,2,64,512]{3,2,1,0:T(8,128)(2,1)}, bf16[4,2,64,512]{3,2,1,0:T(8,128)(2,1)}, u32[]{:S(2)}, u32[]{:S(2)}) collective-permute-start(bf16[4,2,64,512]{3,2,1,0:T(8,128)(2,1)} %get-tuple-element.25), channel_id=1, source_target_pairs={{0,4},{4,8},{8,12},{12,16},{16,20},{20,24},{24,28},{28,32},{32,36}... | collective-permute-start | bytes 1572872 | tf_op jit(solution)/shard_map/ppermute | solution.py:22
  32.3 22.9 %collective-permute-start.1 = (bf16[4,2,64,512]{3,2,1,0:T(8,128)(2,1)}, bf16[4,2,64,512]{3,2,1,0:T(8,128)(2,1)S(1)}, u32[]{:S(2)}, u32[]{:S(2)}) collective-permute-start(bf16[4,2,64,512]{3,2,1,0:T(8,128)(2,1)} %get-tuple-element.28), channel_id=1, source_target_pairs={{0,252},{4,0},{8,4},{12,8},{16,12},{20,16},{24,20},{28,24},{32,28}... | collective-permute-start | bytes 1572872 | tf_op jit(solution)/shard_map/ppermute | solution.py:22
  36.2 19.1 %collective-permute-start.2 = (bf16[4,2,64,512]{3,2,1,0:T(8,128)(2,1)}, bf16[4,2,64,512]{3,2,1,0:T(8,128)(2,1)}, u32[]{:S(2)}, u32[]{:S(2)}) collective-permute-start(bf16[4,2,64,512]{3,2,1,0:T(8,128)(2,1)} %get-tuple-element.27), channel_id=1, source_target_pairs={{0,4},{4,8},{8,12},{12,16},{16,20},{20,24},{24,28},{28,32},{32,36}... | collective-permute-start | bytes 1572872 | tf_op jit(solution)/shard_map/ppermute | solution.py:22
  38.3 2.2 %copy-start = (bf16[4,2,128,2048]{3,2,1,0:T(8,128)(2,1)S(1)}, bf16[4,2,128,2048]{3,2,1,0:T(8,128)(2,1)}, u32[]{:S(2)}) copy-start(bf16[4,2,128,2048]{3,2,1,0:T(8,128)(2,1)} %low_own.7) | copy-start | bytes 12582916
  60.6 69.1 %all-to-all-start = ((f32[64,8,128]{2,1,0:T(8,128)}), f32[64,8,128]{2,1,0:T(8,128)S(1)}, u32[]{:S(2)}, u32[]{:S(2)}) async-start(f32[64,8,128]{2,1,0:T(8,128)} %bitcast.2), calls=%async_computation | async-start | bytes 524288 | tf_op jit(solution)/shard_map/all_to_all | solution.py:223
Sparse Core Ops, SparseCore 0:
  9.9 74.8 all-gather.2

commit v2 on v1

v2 whole, which is shorter than its diff:
```python
from functools import partial
import math

import jax
import jax.numpy as jnp
from jax import lax
from jax.experimental import pallas as pl
from jax.experimental.pallas import tpu as pltpu
from jax.sharding import PartitionSpec as P

LOOK_R = 4
LOOK_C = 16
TWO_PI = 2.0 * math.pi
CODES = 32767.0 / TWO_PI
CUTS = (0, 1280, 2048)
STEP = 256
LANES = 128
SUM_ROWS = (2, 3, 6, 7)


def passed_along(value, axis, steps):
    count = lax.axis_size(axis)
    pairs = [(source, (source + steps) % count) for source in range(count)]
    return lax.ppermute(value, axis, pairs)


def phase_kernel(first_step, steps, combos_ref, top_own, top_next, low_prev, low_own, cycles, *rest):
    payload, sums, images, products, high, low = rest[-6:]
    group, _, rows, width = top_own.shape
    looks = rows // LOOK_R
    pair_count = combos_ref.shape[0] // 2
    out_cols = width // LOOK_C
    tiles = width // LANES
    sets = looks // 8
    step_at = pl.program_id(0)

    @pl.when(step_at == 0)
    def _():
        if first_step:
            earlier, earlier_sums = rest[0], rest[1]
            done = first_step * out_cols * 4
            payload[:done, :] = earlier[:done, :]
            sums[...] = earlier_sums[...]
        else:
            sums[...] = jnp.zeros_like(sums)

    for half, (first, second) in enumerate(((top_own, top_next), (low_prev, low_own))):
        for at, source in enumerate((first, second)):
            for date in range(group):
                for part in range(2):
                    for tile in range(tiles):
                        images[half, at * group + date, part, tile] = source[
                            date, part, :, tile * LANES : (tile + 1) * LANES
                        ].astype(jnp.float32)

    @pl.loop(0, 2 * tiles * sets)
    def _(index):
        half, tile, block = index // (tiles * sets), index // sets % tiles, index % sets
        real, imag = [None] * (group * group), [None] * (group * group)
        for step in range(LOOK_R):
            at = pl.ds(block * 8 * LOOK_R + step, 8, stride=LOOK_R)
            parts = [[images[half, date, part, tile, at, :] for part in range(2)] for date in range(2 * group)]
            for date in range(group):
                a0, a1 = parts[date]
                for gap in range(group):
                    b0, b1 = parts[date + gap + 1]
                    combo = date * group + gap
                    re, im = a0 * b0 + a1 * b1, a1 * b0 - a0 * b1
                    real[combo] = re if step == 0 else real[combo] + re
                    imag[combo] = im if step == 0 else imag[combo] + im
        place = pl.ds(pl.multiple_of(block * 8, 8), 8)
        for combo in range(group * group):
            products[half, combo, 0, tile, place, :] = real[combo]
            products[half, combo, 1, tile, place, :] = imag[combo]

    for half in range(2):

        @pl.loop(0, pair_count)
        def _(pair, half=half):
            combo = combos_ref[half * pair_count + pair]
            for part in range(2):
                base = part * pair_count * 2 * looks + half * looks
                place = pl.ds(pl.multiple_of(pair * 2 * looks + base, 16), looks)
                for tile in range(tiles):
                    value = products[half, combo, part, tile]
                    head = value.astype(jnp.bfloat16)
                    high[place, tile * LANES : (tile + 1) * LANES] = head
                    low[place, tile * LANES : (tile + 1) * LANES] = (value - head.astype(jnp.float32)).astype(
                        jnp.bfloat16
                    )

    shape = (out_cols, width)
    picked = lax.broadcasted_iota(jnp.int32, shape, 1) // LOOK_C == lax.broadcasted_iota(jnp.int32, shape, 0)
    picked = jnp.where(picked, 1.0, 0.0).astype(jnp.bfloat16)
    turned = (((1,), (1,)), ((), ()))
    looked = lax.dot_general(picked, high[...], turned, preferred_element_type=jnp.float32)
    looked += lax.dot_general(picked, low[...], turned, preferred_element_type=jnp.float32)
    half_width = looked.shape[1] // 2
    real, imag = looked[:, :half_width], looked[:, half_width:]
    imag = jnp.where(imag == 0.0, 0.0, imag)
    phase = jnp.arctan2(imag, real) - cycles[...]
    codes = jnp.round((phase + math.pi) * CODES)
    blocks = half_width // LANES
    total = jnp.sum(codes, axis=0, keepdims=True).astype(jnp.int32)
    codes = codes.astype(jnp.int32)
    for q in range(blocks):
        sums[q : q + 1, :] += total[:, q * LANES : (q + 1) * LANES]
    base = (step_at + first_step) * (out_cols * 4)
    for word in range(blocks // 2):
        left = codes[:, 2 * word * LANES : (2 * word + 1) * LANES]
        right = codes[:, (2 * word + 1) * LANES : (2 * word + 2) * LANES]
        payload[pl.ds(base + word, out_cols, stride=4), :] = (left << 16) | (right & 0xFFFF)

    if (first_step + steps) * out_cols * 4 == payload.shape[0]:

        @pl.when(step_at == steps - 1)
        def _():
            for q in range(blocks):
                count = payload.shape[0] // 8
                payload[pl.ds(SUM_ROWS[q], count, stride=8), :] = jnp.broadcast_to(
                    sums[q : q + 1, :], (count, LANES)
                )


def phases(start, stop, combos, acquisitions, following, previous, cycles, earlier):
    group, _, height, width = acquisitions.shape
    rows = height // 2
    first_step, steps = start // STEP, (stop - start) // STEP
    lanes = cycles.shape[1]
    out_cols = STEP // LOOK_C
    payload_shape = (cycles.shape[0] * lanes // LANES, LANES)
    looks = rows // LOOK_R
    tiles = STEP // LANES
    whole = (group, 2, rows, STEP)

    in_specs = [
        pl.BlockSpec(whole, lambda i, p: (0, 0, 0, first_step + i)),
        pl.BlockSpec(whole, lambda i, p: (0, 0, 0, i)),
        pl.BlockSpec(whole, lambda i, p: (0, 0, 0, i)),
        pl.BlockSpec(whole, lambda i, p: (0, 0, 1, first_step + i)),
        pl.BlockSpec((out_cols, lanes), lambda i, p: (first_step + i, 0)),
    ]
    outs = [
        pl.BlockSpec(payload_shape, lambda i, p: (0, 0)),
        pl.BlockSpec((8, LANES), lambda i, p: (0, 0)),
    ]
    operands = [combos, acquisitions, following, previous, acquisitions, cycles, *earlier]
    return pl.pallas_call(
        partial(phase_kernel, first_step, steps),
        grid_spec=pltpu.PrefetchScalarGridSpec(
            num_scalar_prefetch=1,
            grid=(steps,),
            in_specs=in_specs + outs[: len(earlier)],
            out_specs=outs,
            scratch_shapes=[
                pltpu.VMEM((2, 2 * group, 2, tiles, rows, LANES), jnp.float32),
                pltpu.VMEM((2, group * group, 2, tiles, looks, LANES), jnp.float32),
                pltpu.VMEM((2 * lanes, STEP), jnp.bfloat16),
                pltpu.VMEM((2 * lanes, STEP), jnp.bfloat16),
            ],
        ),
        out_shape=[
            jax.ShapeDtypeStruct(payload_shape, jnp.int32),
            jax.ShapeDtypeStruct((8, LANES), jnp.int32),
        ],
        compiler_params=pltpu.CompilerParams(vmem_limit_bytes=24 << 20),
        cost_estimate=pl.CostEstimate(
            flops=8 * group * group * height * (stop - start),
            bytes_accessed=group * 2 * height * (stop - start) * 4,
            transcendentals=0,
        ),
        name="phases",
    )(*operands)


def placed_kernel(row_ref, *refs):
    *pieces, out = refs
    per, sources, _ = pieces[0].shape
    for offset, piece in enumerate(pieces):
        owner = lax.rem(row_ref[0] - offset + len(pieces), len(pieces))
        for at in range(per):
            start = pl.multiple_of((owner * per + at) * sources, 8)
            out[pl.ds(start, sources), :] = piece[at]


def whole_inverse(inverse):
    devices, row_count = lax.axis_size("date"), lax.axis_size("row")
    dates, pair_count = inverse.shape
    per = pair_count // row_count
    mine = lax.dynamic_slice_in_dim(inverse.T, lax.axis_index("row") * per, per, axis=0)
    sent = jnp.broadcast_to(mine.reshape(1, 2, per * dates // 2), (devices // 2, 2, per * dates // 2))
    sent = sent.reshape(devices, per * dates // (2 * LANES), LANES)
    got = lax.all_to_all(sent, "date", split_axis=0, concat_axis=0, tiled=True)
    got = got.reshape(devices, per // 2, dates).transpose(1, 0, 2)
    other = lax.ppermute(got, "date", [(at, at ^ 1) for at in range(devices)])
    odd = lax.axis_index("date") % 2
    got = jnp.concatenate([jnp.where(odd == 0, got, other), jnp.where(odd == 0, other, got)], axis=0)
    pieces = [got] + [passed_along(got, "row", step) for step in range(1, row_count)]
    return pl.pallas_call(
        placed_kernel,
        in_specs=[pl.BlockSpec(memory_space=pltpu.SMEM)] + [pl.BlockSpec(memory_space=pltpu.VMEM)] * row_count,
        out_specs=pl.BlockSpec(memory_space=pltpu.VMEM),
        out_shape=jax.ShapeDtypeStruct((pair_count * devices, dates), jnp.float32),
        name="placed",
    )(lax.axis_index("row").reshape(1), *pieces)


def invert_kernel(band_pixels, received, inverse, out, bias, left):
    pair_count, blocks = 16, 4
    sources = inverse.shape[0] // pair_count
    per = pair_count // blocks
    rows = LANES // per
    pixels = out.shape[0]

    def aligned(words):
        value = words.astype(jnp.float32)
        rolled = pltpu.roll(value, sources - 1, 0)
        lane = lax.broadcasted_iota(jnp.int32, value.shape, 1) % rows
        return jnp.where(lane < rows // 2, value, rolled).T

    left[pixels:, :] = jnp.zeros((left.shape[0] - pixels, left.shape[1]), jnp.float32)
    for col in range(pixels // rows):
        for word in range(blocks // 2):
            words = received[pl.ds(col * 4 + word, sources, stride=8), :]
            for side, value in enumerate((words >> 16, (words << 16) >> 16)):
                turned = aligned(value)
                for at in range(per):
                    pair = (2 * word + side) * per + at
                    left[col * rows : (col + 1) * rows, pair * sources : (pair + 1) * sources] = turned[
                        at * rows : (at + 1) * rows
                    ]
    for q in range(blocks):
        turned = aligned(received[pl.ds(SUM_ROWS[q], sources, stride=8), :])
        for at in range(per):
            pair = q * per + at
            left[pixels : pixels + 1, pair * sources : (pair + 1) * sources] = jnp.sum(
                turned[at * rows : (at + 1) * rows], axis=0, keepdims=True
            )
    product = jnp.dot(
        left[...], inverse[...], precision=lax.Precision.HIGHEST, preferred_element_type=jnp.float32
    )
    out[...] = product[:pixels] * (1.0 / CODES)
    bias[...] = product[pixels:] * (1.0 / (CODES * band_pixels))


def invert(received, inverse, pixels, band_pixels):
    total_pairs, dates = inverse.shape
    return pl.pallas_call(
        partial(invert_kernel, band_pixels),
        in_specs=[pl.BlockSpec(memory_space=pltpu.VMEM)] * 2,
        out_specs=[pl.BlockSpec(memory_space=pltpu.VMEM)] * 2,
        out_shape=[
            jax.ShapeDtypeStruct((pixels, dates), jnp.float32),
            jax.ShapeDtypeStruct((8, dates), jnp.float32),
        ],
        scratch_shapes=[pltpu.VMEM((pixels + 8, total_pairs), jnp.float32)],
        compiler_params=pltpu.CompilerParams(vmem_limit_bytes=24 << 20),
        name="invert",
    )(received, inverse)


def body(acquisitions, date_pairs, cycle_maps, inverse):
    group, _, height, width = acquisitions.shape
    devices = lax.axis_size("date")
    total_dates = group * devices
    pair_count, look_rows, look_cols = cycle_maps.shape
    rows = height // 2
    half = look_rows // 2

    sliced = [
        (acquisitions[:, :, :rows, start:stop], acquisitions[:, :, rows:, start:stop])
        for start, stop in zip(CUTS[:-1], CUTS[1:])
    ]
    sliced, date_pairs, cycle_maps, inverse = lax.optimization_barrier((sliced, date_pairs, cycle_maps, inverse))
    following = [passed_along(upper, "date", -1) for upper, _ in sliced]
    previous = [passed_along(lower, "date", 1) for _, lower in sliced]

    base = lax.axis_index("date") * group
    gaps = (date_pairs[:, 1] - date_pairs[:, 0] + total_dates) % total_dates
    combos = (date_pairs[:, 0] - base) * group + gaps - 1
    named = jnp.broadcast_to(combos[:, None, None], (pair_count, half, look_cols))
    low_data = jnp.stack([cycle_maps[:, half:], named]).astype(jnp.bfloat16)
    low_data = passed_along(low_data, "date", 1)
    combos = jnp.concatenate([combos, low_data[1, :, 0, 0].astype(jnp.int32)])
    cycles = jnp.concatenate([cycle_maps[:, :half].astype(jnp.float32), low_data[0].astype(jnp.float32)], axis=1)
    cycles = (TWO_PI * cycles).reshape(pair_count * look_rows, look_cols).T

    inverse = whole_inverse(inverse)

    earlier = ()
    for chunk, (start, stop) in enumerate(zip(CUTS[:-1], CUTS[1:])):
        earlier = phases(
            start, stop, combos, acquisitions, following[chunk], previous[chunk], cycles, earlier
        )

    payload = earlier[0]
    received = lax.all_to_all(
        payload.reshape(devices, -1, LANES), "date", split_axis=0, concat_axis=0, tiled=True
    ).reshape(payload.shape)
    out_cols = look_cols // devices
    row_count = lax.axis_size("row")
    result, bias = invert(received, inverse, out_cols * look_rows, look_rows * look_cols * row_count)
    for step in range(1, row_count):
        result = result - passed_along(bias, "row", step)[:1]
    result = result - bias[:1]
    return result.reshape(out_cols, look_rows, total_dates)


def solution(mesh):
    return jax.shard_map(
        body,
        mesh=mesh,
        in_specs=(
            P("date", None, "row", None),
            P("date", None),
            P("date", "row", None),
            P(None, "date"),
        ),
        out_specs=P("date", "row", None),
        check_vma=False,
    )
```

time: 141 us -> 105 us (0.74); the launches traced: 138 us -> 104 us
  blocking collectives: 54.6 us -> 0 us
  waiting for transfers between devices: 8.18 us -> 30.7 us
  between operations: 13.5 us -> 0.21 us
  starting transfers between devices: 30.4 us -> 38.7 us
  local copies, waits for them, and re-layouts: 8.91 us -> 11.6 us
  other arithmetic: 0.88 us -> 2.98 us
  Pallas kernels: 21.7 us -> 19.9 us
    all_gather x1 -> x0, blocking collectives: 43.8 us -> none  [body(): sums = lax.all_gather(sums, 'date', axis=0, tiled=True)]
    ppermute x10 -> x11, waiting for transfers between devices: 7.46 us -> 29.7 us  [passed_along(): return lax.ppermute(value, axis, pairs)]
    all_to_all x0 -> x1, starting transfers between devices: none -> 11.1 us  [whole_inverse(): got = lax.all_to_all(sent, 'date', split_axis=0, concat_axis=0, tiled=True)]
    psum x1 -> x0, blocking collectives: 10.8 us -> none  [body(): sums = lax.psum(sums, 'row')]
    all_to_all x1, starting transfers between devices: 13.1 us -> 8.03 us  [body(): lax.all_to_all(payload.reshape(devices, -1, LANES), 'date', split_axis=0,...]
    slice x1 -> x6, local copies, waits for them, and re-layouts: 4.06 us -> 6.24 us  [the longest x2 6.23 us: body(): acquisitions[:, :, rows:, start:stop]]
    ppermute x10 -> x11, starting transfers between devices: 17.3 us -> 19.4 us  [passed_along(): return lax.ppermute(value, axis, pairs)]
    unnamed x6 -> x18, local copies, waits for them, and re-layouts: 2.19 us -> 4.21 us
  transfers between devices with their start and end apart: 12 -> 14, of which waited for: 1 -> 6; matrix products, arithmetic and copies ran while one was open for 5% -> 3% of each run, Pallas kernels for 15% -> 18%
where the time goes in v2:
time: 105 us; the launch traced here: 104 us
  starting transfers between devices  38.7 us (37%)
  waiting for transfers between devices  30.7 us (29%)
  Pallas kernels  19.9 us (19%)
  local copies, waits for them, and re-layouts  11.6 us (11%)
  other arithmetic  2.98 us (3%)
    ppermute x11, waiting for transfers between devices, passed_along(): return lax.ppermute(value, axis, pairs)  29.7 us
    ppermute x11, starting transfers between devices, passed_along(): return lax.ppermute(value, axis, pairs)  19.4 us
    pallas_call x2, Pallas kernels, phases(): pl.pallas_call(partial(phase_kernel, first_step, steps), grid_spec=pltpu....  16.7 us
    all_to_all x1, starting transfers between devices, whole_inverse(): got = lax.all_to_all(sent, 'date', split_axis=0, concat_axis=0, tiled=True)  11.1 us
    all_to_all x1, starting transfers between devices, body(): lax.all_to_all(payload.reshape(devices, -1, LANES), 'date', split_axis=0,...  8.03 us
    slice x2, local copies, waits for them, and re-layouts, body(): acquisitions[:, :, rows:, start:stop]  6.23 us
    unnamed x18, local copies, waits for them, and re-layouts  4.21 us
    pallas_call x1, Pallas kernels, whole_inverse(): pl.pallas_call(placed_kernel, in_specs=[pl.BlockSpec(memory_space=pltpu.S...  2.25 us
  transfers between devices with their start and end apart: 14, of which 6 were waited for; matrix products, arithmetic and copies ran while one was open for 3% of the time, Pallas kernels for 18%

profile of v2, /device:TPU:6, one launch (start us, length us, event | category | flops | bytes accessed | tf_op | source)
XLA Modules:
  0.0 104.1 jit_solution(8713654610560621587)
XLA Ops:
  0.0 0.0 copy-start
  0.0 3.5 %fusion.9 = (bf16[4,2,64,1280]{3,2,1,0:T(8,128)(2,1)}, bf16[4,2,64,1280]{3,2,1,0:T(8,128)(2,1)}) fusion(bf16[4,2,128,2048]{3,2,1,0:T(8,128)(2,1)} %low_own.3), kind=kLoop, calls=%fused_computation.24 | loop fusion | bytes 5242880 | tf_op jit(solution)/shard_map/slice | solution.py:271
  3.5 2.7 %fusion.8 = (bf16[4,2,64,768]{3,2,1,0:T(8,128)(2,1)}, bf16[4,2,64,768]{3,2,1,0:T(8,128)(2,1)}) fusion(bf16[4,2,128,2048]{3,2,1,0:T(8,128)(2,1)} %low_own.3), kind=kLoop, calls=%fused_computation.23 | loop fusion | bytes 3145728 | tf_op jit(solution)/shard_map/slice | solution.py:271
  6.2 5.6 %collective-permute-start.3 = (bf16[4,2,64,1280]{3,2,1,0:T(8,128)(2,1)}, bf16[4,2,64,1280]{3,2,1,0:T(8,128)(2,1)S(1)}, u32[]{:S(2)}, u32[]{:S(2)}) collective-permute-start(bf16[4,2,64,1280]{3,2,1,0:T(8,128)(2,1)} %get-tuple-element.21), channel_id=1, source_target_pairs={{0,252},{4,0},{8,4},{12,8},{16,12},{20,16},{24,20},{28,24},{32,28}... | collective-permute-start | bytes 3932168 | tf_op jit(solution)/shard_map/ppermute | solution.py:24
  11.8 0.0 collective-permute-start.4
  11.8 3.9 %collective-permute-start.1 = (bf16[4,2,64,768]{3,2,1,0:T(8,128)(2,1)}, bf16[4,2,64,768]{3,2,1,0:T(8,128)(2,1)}, u32[]{:S(2)}, u32[]{:S(2)}) collective-permute-start(bf16[4,2,64,768]{3,2,1,0:T(8,128)(2,1)} %get-tuple-element.19), channel_id=1, source_target_pairs={{0,252},{4,0},{8,4},{12,8},{16,12},{20,16},{24,20},{28,24},{32,28}... | collective-permute-start | bytes 2359304 | tf_op jit(solution)/shard_map/ppermute | solution.py:24
  15.7 0.0 collective-permute-start.2
  15.7 0.5 fusion.6
  16.2 0.0 copy-done.7
  16.2 0.1 stack_broadcast_in_dim.2
  16.3 0.1 collective-permute-start
  16.5 0.8 reshape.47
  17.3 11.1 %all-to-all-start.1 = ((f32[64,4,128]{2,1,0:T(4,128)}), f32[64,4,128]{2,1,0:T(4,128)S(1)}, u32[]{:S(2)}, u32[]{:S(2)}) async-start(f32[64,4,128]{2,1,0:T(4,128)} %reshape.47), calls=%async_computation.1 | async-start | bytes 262144 | tf_op jit(solution)/shard_map/all_to_all | solution.py:193
  28.4 14.9 %collective-permute-done = bf16[2,16,16,128]{3,2,1,0:T(8,128)(2,1)S(1)} collective-permute-done((bf16[2,16,16,128]{3,2,1,0:T(8,128)(2,1)S(1)}, bf16[2,16,16,128]{3,2,1,0:T(8,128)(2,1)S(1)}, u32[]{:S(2)}, u32[]{:S(2)}) %collective-permute-start) | collective-permute-done | bytes 131104 | tf_op jit(solution)/shard_map/ppermute | solution.py:24
  43.3 1.1 %all-to-all-done.1 = f32[64,4,128]{2,1,0:T(4,128)S(1)} async-done(((f32[64,4,128]{2,1,0:T(4,128)}), f32[64,4,128]{2,1,0:T(4,128)S(1)}, u32[]{:S(2)}, u32[]{:S(2)}) %all-to-all-start.1) | async-done | bytes 131104 | tf_op jit(solution)/shard_map/all_to_all | solution.py:193
  44.4 0.1 reshape.48
  44.5 0.2 collective-permute-start.5
  44.7 1.0 fusion.2
  45.7 0.1 copy.6
  45.8 0.7 pad_add_fusion.combos_ref
  46.6 0.0 collective-permute-done.3.top_next
  46.6 0.0 collective-permute-done.4.low_prev
  46.6 2.2 %copy-done.1 = bf16[4,2,128,2048]{3,2,1,0:T(8,128)(2,1)S(1)} copy-done((bf16[4,2,128,2048]{3,2,1,0:T(8,128)(2,1)S(1)}, bf16[4,2,128,2048]{3,2,1,0:T(8,128)(2,1)}, u32[]{:S(2)}) %copy-start.1) | copy-done | bytes 4194328
  48.8 9.3 %phases.2 = (s32[512,128]{1,0:T(8,128)S(1)}, s32[8,128]{1,0:T(8,128)S(1)}) custom-call(s32[32]{0:T(128)S(1)} %pad_add_fusion.combos_ref, bf16[4,2,128,2048]{3,2,1,0:T(8,128)(2,1)S(1)} %copy-done.1, bf16[4,2,64,1280]{3,2,1,0:T(8,128)(2,1)S(1)} %collective-permute-done.3.top_next, bf16[4,2,64,1280]{3,2,1,0:T(8,128)(2,1)S(1)} %collective-permute-done.4.low_prev, ...), custom_call_target="tpu_custom_call" | custom-call | flops 20971520 | bytes 5242880 | tf_op jit(solution)/shard_map/phases/pallas_call | solution.py:148
  58.1 0.0 collective-permute-done.1.top_next
  58.1 0.0 collective-permute-done.2.low_prev
  58.1 7.4 %phases.3 = (s32[512,128]{1,0:T(8,128)}, s32[8,128]{1,0:T(8,128)}) custom-call(s32[32]{0:T(128)S(1)} %pad_add_fusion.combos_ref, bf16[4,2,128,2048]{3,2,1,0:T(8,128)(2,1)S(1)} %copy-done.1, bf16[4,2,64,768]{3,2,1,0:T(8,128)(2,1)} %collective-permute-done.1.top_next, bf16[4,2,64,768]{3,2,1,0:T(8,128)(2,1)} %collective-permute-done.2.low_prev, ...), custom_call_target="tpu_custom_call" | custom-call | flops 12582912 | bytes 3145728 | tf_op jit(solution)/shard_map/phases/pallas_call | solution.py:148
  65.5 8.0 %all-to-all-start = ((s32[64,8,128]{2,1,0:T(8,128)}), s32[64,8,128]{2,1,0:T(8,128)S(1)}, u32[]{:S(2)}, u32[]{:S(2)}) async-start(s32[64,8,128]{2,1,0:T(8,128)} %bitcast.6), calls=%async_computation | async-start | bytes 524288 | tf_op jit(solution)/shard_map/all_to_all | solution.py:297
  73.5 0.0 collective-permute-done.5
  73.6 1.7 %collective-permute-start.6 = (f32[4,64,256]{2,1,0:T(8,128)S(1)}, f32[4,64,256]{2,1,0:T(8,128)S(1)}, u32[]{:S(2)}, u32[]{:S(2)}) collective-permute-start(f32[4,64,256]{2,1,0:T(8,128)S(1)} %pad_maximum_fusion.refs_0_), channel_id=1, source_target_pairs={{0,1},{1,2},{2,3},{3,0},{4,5},{5,6},{6,7},{7,4},{8,9},{9,10},{10,1... | collective-permute-start | bytes 786440 | tf_op jit(solution)/shard_map/ppermute | solution.py:24
  75.3 2.9 %collective-permute-start.7 = (f32[4,64,256]{2,1,0:T(8,128)S(1)}, f32[4,64,256]{2,1,0:T(8,128)S(1)}, u32[]{:S(2)}, u32[]{:S(2)}) collective-permute-start(f32[4,64,256]{2,1,0:T(8,128)S(1)} %pad_maximum_fusion.refs_0_), channel_id=1, source_target_pairs={{0,2},{1,3},{2,0},{3,1},{4,6},{5,7},{6,4},{7,5},{8,10},{9,11},{10,... | collective-permute-start | bytes 786440 | tf_op jit(solution)/shard_map/ppermute | solution.py:24
  78.2 1.3 %collective-permute-start.8 = (f32[4,64,256]{2,1,0:T(8,128)S(1)}, f32[4,64,256]{2,1,0:T(8,128)S(1)}, u32[]{:S(2)}, u32[]{:S(2)}) collective-permute-start(f32[4,64,256]{2,1,0:T(8,128)S(1)} %pad_maximum_fusion.refs_0_), channel_id=1, source_target_pairs={{0,3},{1,0},{2,1},{3,2},{4,7},{5,4},{6,5},{7,6},{8,11},{9,8},{10,9... | collective-permute-start | bytes 786440 | tf_op jit(solution)/shard_map/ppermute | solution.py:24
  79.5 3.8 %collective-permute-done.6.refs_1_ = f32[4,64,256]{2,1,0:T(8,128)S(1)} collective-permute-done((f32[4,64,256]{2,1,0:T(8,128)S(1)}, f32[4,64,256]{2,1,0:T(8,128)S(1)}, u32[]{:S(2)}, u32[]{:S(2)}) %collective-permute-start.6) | collective-permute-done | bytes 262176 | tf_op jit(solution)/shard_map/ppermute | solution.py:24
  83.3 6.8 %collective-permute-done.7.refs_2_ = f32[4,64,256]{2,1,0:T(8,128)S(1)} collective-permute-done((f32[4,64,256]{2,1,0:T(8,128)S(1)}, f32[4,64,256]{2,1,0:T(8,128)S(1)}, u32[]{:S(2)}, u32[]{:S(2)}) %collective-permute-start.7) | collective-permute-done | bytes 262176 | tf_op jit(solution)/shard_map/ppermute | solution.py:24
  90.1 0.0 collective-permute-done.8.refs_3_
  90.2 0.7 copy-done.5
  90.8 0.1 copy-done.6
  90.9 2.2 %placed.1.inverse = f32[1024,256]{1,0:T(8,128)} custom-call(s32[1]{0:T(128)} %bitcast.8.row_ref, f32[4,64,256]{2,1,0:T(8,128)} %copy-done.3, f32[4,64,256]{2,1,0:T(8,128)} %copy-done.4, f32[4,64,256]{2,1,0:T(8,128)} %copy-done.5, f32[4,64,256]{2,1,0:T(8,128)} %copy-done.6), custom_call_target="tpu_custom_call" | custom-call | tf_op jit(solution)/shard_map/placed/pallas_call | solution.py:199
  93.2 0.0 all-to-all-done
  93.2 1.2 %copy-done.2 = f32[1024,256]{1,0:T(8,128)S(1)} copy-done((f32[1024,256]{1,0:T(8,128)S(1)}, f32[1024,256]{1,0:T(8,128)}, u32[]{:S(2)}) %copy-start.2) | copy-done | bytes 1048600
  94.4 0.9 invert.1
  95.3 2.2 %collective-permute-start.11 = (f32[8,256]{1,0:T(8,128)S(1)}, f32[8,256]{1,0:T(8,128)S(1)}, u32[]{:S(2)}, u32[]{:S(2)}) collective-permute-start(f32[8,256]{1,0:T(8,128)S(1)} %get-tuple-element.28), channel_id=1, source_target_pairs={{0,3},{1,0},{2,1},{3,2},{4,7},{5,4},{6,5},{7,6},{8,11},{9,8},{10,9... | collective-permute-start | bytes 24584 | tf_op jit(solution)/shard_map/ppermute | solution.py:24
  97.5 1.1 %collective-permute-start.10 = (f32[8,256]{1,0:T(8,128)S(1)}, f32[8,256]{1,0:T(8,128)S(1)}, u32[]{:S(2)}, u32[]{:S(2)}) collective-permute-start(f32[8,256]{1,0:T(8,128)S(1)} %get-tuple-element.28), channel_id=1, source_target_pairs={{0,2},{1,3},{2,0},{3,1},{4,6},{5,7},{6,4},{7,5},{8,10},{9,11},{10,... | collective-permute-start | bytes 24584 | tf_op jit(solution)/shard_map/ppermute | solution.py:24
  98.6 0.7 collective-permute-start.9
  99.3 0.0 collective-permute-done.11
  99.3 3.3 %collective-permute-done.10 = f32[8,256]{1,0:T(8,128)S(1)} collective-permute-done((f32[8,256]{1,0:T(8,128)S(1)}, f32[8,256]{1,0:T(8,128)S(1)}, u32[]{:S(2)}, u32[]{:S(2)}) %collective-permute-start.10) | collective-permute-done | bytes 8224 | tf_op jit(solution)/shard_map/ppermute | solution.py:24
  102.6 0.8 collective-permute-done.9
  103.5 0.6 subtract_subtract_fusion
  (26 shorter events, 0.2 us)
Async XLA Ops:
  0.0 16.4 %copy-start = (f32[256,16]{0,1:T(8,128)S(1)}, f32[256,16]{0,1:T(8,128)}, u32[]{:S(2)}) copy-start(f32[256,16]{0,1:T(8,128)} %param.7) | copy-start | bytes 49156
  3.5 12.2 %copy-start.8 = (s32[16,2]{0,1:T(2,128)S(1)}, s32[16,2]{0,1:T(2,128)}, u32[]{:S(2)}) copy-start(s32[16,2]{0,1:T(2,128)} %param.5) | copy-start | bytes 388
  3.5 12.7 %copy-start.7 = (s32[16,32,128]{2,1,0:T(8,128)S(1)}, s32[16,32,128]{2,1,0:T(8,128)}, u32[]{:S(2)}) copy-start(s32[16,32,128]{2,1,0:T(8,128)} %param.6) | copy-start | bytes 786436
  6.2 40.3 %collective-permute-start.3 = (bf16[4,2,64,1280]{3,2,1,0:T(8,128)(2,1)}, bf16[4,2,64,1280]{3,2,1,0:T(8,128)(2,1)S(1)}, u32[]{:S(2)}, u32[]{:S(2)}) collective-permute-start(bf16[4,2,64,1280]{3,2,1,0:T(8,128)(2,1)} %get-tuple-element.21), channel_id=1, source_target_pairs={{0,252},{4,0},{8,4},{12,8},{16,12},{20,16},{24,20},{28,24},{32,28}... | collective-permute-start | bytes 3932168 | tf_op jit(solution)/shard_map/ppermute | solution.py:24
  11.8 34.8 %collective-permute-start.4 = (bf16[4,2,64,1280]{3,2,1,0:T(8,128)(2,1)}, bf16[4,2,64,1280]{3,2,1,0:T(8,128)(2,1)S(1)}, u32[]{:S(2)}, u32[]{:S(2)}) collective-permute-start(bf16[4,2,64,1280]{3,2,1,0:T(8,128)(2,1)} %get-tuple-element.22), channel_id=1, source_target_pairs={{0,4},{4,8},{8,12},{12,16},{16,20},{20,24},{24,28},{28,32},{32,36}... | collective-permute-start | bytes 3932168 | tf_op jit(solution)/shard_map/ppermute | solution.py:24
  11.8 46.3 %collective-permute-start.1 = (bf16[4,2,64,768]{3,2,1,0:T(8,128)(2,1)}, bf16[4,2,64,768]{3,2,1,0:T(8,128)(2,1)}, u32[]{:S(2)}, u32[]{:S(2)}) collective-permute-start(bf16[4,2,64,768]{3,2,1,0:T(8,128)(2,1)} %get-tuple-element.19), channel_id=1, source_target_pairs={{0,252},{4,0},{8,4},{12,8},{16,12},{20,16},{24,20},{28,24},{32,28}... | collective-permute-start | bytes 2359304 | tf_op jit(solution)/shard_map/ppermute | solution.py:24
  15.7 42.4 %collective-permute-start.2 = (bf16[4,2,64,768]{3,2,1,0:T(8,128)(2,1)}, bf16[4,2,64,768]{3,2,1,0:T(8,128)(2,1)}, u32[]{:S(2)}, u32[]{:S(2)}) collective-permute-start(bf16[4,2,64,768]{3,2,1,0:T(8,128)(2,1)} %get-tuple-element.20), channel_id=1, source_target_pairs={{0,4},{4,8},{8,12},{12,16},{16,20},{20,24},{24,28},{28,32},{32,36}... | collective-permute-start | bytes 2359304 | tf_op jit(solution)/shard_map/ppermute | solution.py:24
  16.3 26.9 %collective-permute-start = (bf16[2,16,16,128]{3,2,1,0:T(8,128)(2,1)S(1)}, bf16[2,16,16,128]{3,2,1,0:T(8,128)(2,1)S(1)}, u32[]{:S(2)}, u32[]{:S(2)}) collective-permute-start(bf16[2,16,16,128]{3,2,1,0:T(8,128)(2,1)S(1)} %pad_maximum_fusion.1), channel_id=1, source_target_pairs={{0,4},{4,8},{8,12},{12,16},{16,20},{20,24},{24,28},{28,32},{32,36}... | collective-permute-start | bytes 393224 | tf_op jit(solution)/shard_map/ppermute | solution.py:24
  17.3 27.1 %all-to-all-start.1 = ((f32[64,4,128]{2,1,0:T(4,128)}), f32[64,4,128]{2,1,0:T(4,128)S(1)}, u32[]{:S(2)}, u32[]{:S(2)}) async-start(f32[64,4,128]{2,1,0:T(4,128)} %reshape.47), calls=%async_computation.1 | async-start | bytes 262144 | tf_op jit(solution)/shard_map/all_to_all | solution.py:193
  44.5 29.0 %collective-permute-start.5 = (f32[2,64,256]{2,1,0:T(8,128)S(1)}, f32[2,64,256]{2,1,0:T(8,128)S(1)}, u32[]{:S(2)}, u32[]{:S(2)}) collective-permute-start(f32[2,64,256]{2,1,0:T(8,128)S(1)} %bitcast.40), channel_id=1, source_target_pairs={{0,4},{4,0},{8,12},{12,8},{16,20},{20,16},{24,28},{28,24},{32,36},... | collective-permute-start | bytes 393224 | tf_op jit(solution)/shard_map/ppermute | solution.py:195
  46.6 2.2 %copy-start.1 = (bf16[4,2,128,2048]{3,2,1,0:T(8,128)(2,1)S(1)}, bf16[4,2,128,2048]{3,2,1,0:T(8,128)(2,1)}, u32[]{:S(2)}) copy-start(bf16[4,2,128,2048]{3,2,1,0:T(8,128)(2,1)} %low_own.3) | copy-start | bytes 12582916
  65.5 27.7 %all-to-all-start = ((s32[64,8,128]{2,1,0:T(8,128)}), s32[64,8,128]{2,1,0:T(8,128)S(1)}, u32[]{:S(2)}, u32[]{:S(2)}) async-start(s32[64,8,128]{2,1,0:T(8,128)} %bitcast.6), calls=%async_computation | async-start | bytes 524288 | tf_op jit(solution)/shard_map/all_to_all | solution.py:297
  73.6 16.5 %copy-start.3 = (f32[4,64,256]{2,1,0:T(8,128)}, f32[4,64,256]{2,1,0:T(8,128)S(1)}, u32[]{:S(2)}) copy-start(f32[4,64,256]{2,1,0:T(8,128)S(1)} %pad_maximum_fusion.refs_0_) | copy-start | bytes 786436
  73.6 9.7 %collective-permute-start.6 = (f32[4,64,256]{2,1,0:T(8,128)S(1)}, f32[4,64,256]{2,1,0:T(8,128)S(1)}, u32[]{:S(2)}, u32[]{:S(2)}) collective-permute-start(f32[4,64,256]{2,1,0:T(8,128)S(1)} %pad_maximum_fusion.refs_0_), channel_id=1, source_target_pairs={{0,1},{1,2},{2,3},{3,0},{4,5},{5,6},{6,7},{7,4},{8,9},{9,10},{10,1... | collective-permute-start | bytes 786440 | tf_op jit(solution)/shard_map/ppermute | solution.py:24
  75.3 14.9 %collective-permute-start.7 = (f32[4,64,256]{2,1,0:T(8,128)S(1)}, f32[4,64,256]{2,1,0:T(8,128)S(1)}, u32[]{:S(2)}, u32[]{:S(2)}) collective-permute-start(f32[4,64,256]{2,1,0:T(8,128)S(1)} %pad_maximum_fusion.refs_0_), channel_id=1, source_target_pairs={{0,2},{1,3},{2,0},{3,1},{4,6},{5,7},{6,4},{7,5},{8,10},{9,11},{10,... | collective-permute-start | bytes 786440 | tf_op jit(solution)/shard_map/ppermute | solution.py:24
  78.2 12.0 %collective-permute-start.8 = (f32[4,64,256]{2,1,0:T(8,128)S(1)}, f32[4,64,256]{2,1,0:T(8,128)S(1)}, u32[]{:S(2)}, u32[]{:S(2)}) collective-permute-start(f32[4,64,256]{2,1,0:T(8,128)S(1)} %pad_maximum_fusion.refs_0_), channel_id=1, source_target_pairs={{0,3},{1,0},{2,1},{3,2},{4,7},{5,4},{6,5},{7,6},{8,11},{9,8},{10,9... | collective-permute-start | bytes 786440 | tf_op jit(solution)/shard_map/ppermute | solution.py:24
  83.3 6.8 %copy-start.4 = (f32[4,64,256]{2,1,0:T(8,128)}, f32[4,64,256]{2,1,0:T(8,128)S(1)}, u32[]{:S(2)}) copy-start(f32[4,64,256]{2,1,0:T(8,128)S(1)} %collective-permute-done.6.refs_1_) | copy-start | bytes 786436
  90.1 0.7 copy-start.5
  90.1 0.8 copy-start.6
  93.2 1.2 %copy-start.2 = (f32[1024,256]{1,0:T(8,128)S(1)}, f32[1024,256]{1,0:T(8,128)}, u32[]{:S(2)}) copy-start(f32[1024,256]{1,0:T(8,128)} %placed.1.inverse) | copy-start | bytes 3145732
  95.3 4.0 %collective-permute-start.11 = (f32[8,256]{1,0:T(8,128)S(1)}, f32[8,256]{1,0:T(8,128)S(1)}, u32[]{:S(2)}, u32[]{:S(2)}) collective-permute-start(f32[8,256]{1,0:T(8,128)S(1)} %get-tuple-element.28), channel_id=1, source_target_pairs={{0,3},{1,0},{2,1},{3,2},{4,7},{5,4},{6,5},{7,6},{8,11},{9,8},{10,9... | collective-permute-start | bytes 24584 | tf_op jit(solution)/shard_map/ppermute | solution.py:24
  97.5 5.2 %collective-permute-start.10 = (f32[8,256]{1,0:T(8,128)S(1)}, f32[8,256]{1,0:T(8,128)S(1)}, u32[]{:S(2)}, u32[]{:S(2)}) collective-permute-start(f32[8,256]{1,0:T(8,128)S(1)} %get-tuple-element.28), channel_id=1, source_target_pairs={{0,2},{1,3},{2,0},{3,1},{4,6},{5,7},{6,4},{7,5},{8,10},{9,11},{10,... | collective-permute-start | bytes 24584 | tf_op jit(solution)/shard_map/ppermute | solution.py:24
  98.6 4.9 %collective-permute-start.9 = (f32[8,256]{1,0:T(8,128)S(1)}, f32[8,256]{1,0:T(8,128)S(1)}, u32[]{:S(2)}, u32[]{:S(2)}) collective-permute-start(f32[8,256]{1,0:T(8,128)S(1)} %get-tuple-element.28), channel_id=1, source_target_pairs={{0,1},{1,2},{2,3},{3,0},{4,5},{5,6},{6,7},{7,4},{8,9},{9,10},{10,1... | collective-permute-start | bytes 24584 | tf_op jit(solution)/shard_map/ppermute | solution.py:24

commit v3 on v2

v3 whole, which is shorter than its diff:
```python
from functools import partial
import math

import jax
import jax.numpy as jnp
from jax import lax
from jax.experimental import pallas as pl
from jax.experimental.pallas import tpu as pltpu
from jax.sharding import PartitionSpec as P

LOOK_R = 4
LOOK_C = 16
TWO_PI = 2.0 * math.pi
CODES = 32767.0 / TWO_PI
INNER = ((0, 1024), (1024, 2048))
OUTER = ((0, 1024), (1024, 2048))
ORDER = ((0, 0), (0, 1), (1, 0), (1, 1))
STEP = 512
MESSAGE = 5
LANES = 128


def passed_along(value, axis, steps):
    count = lax.axis_size(axis)
    pairs = [(source, (source + steps) % count) for source in range(count)]
    return lax.ppermute(value, axis, pairs)


def phase_kernel(slot, first_step, steps, final, scalars, own, other, cycles, *rest):
    payload, sums, images, products, high, low, words = rest[-7:]
    rest = rest[:-7]
    group, _, rows, width = own.shape
    looks = rows // LOOK_R
    pair_count = group * group
    out_cols = width // LOOK_C
    tiles = width // LANES
    sets = looks // 8
    half, own_at = scalars[0], scalars[2]
    step_at = pl.program_id(0)

    @pl.when(step_at == 0)
    def _():
        if len(rest) > 1:
            payload[...] = rest[1][...]
            sums[...] = rest[2][...]
        else:
            sums[...] = jnp.zeros_like(sums)

    @pl.loop(0, 2 * group)
    def _(index):
        date, part = index // 2, index % 2
        for source, start in ((own, own_at), (other, group - own_at)):
            for tile in range(tiles):
                images[start + date, part, tile] = source[
                    date, part, :, tile * LANES : (tile + 1) * LANES
                ].astype(jnp.float32)

    @pl.loop(0, tiles * sets)
    def _(index):
        tile, block = index // sets, index % sets
        real, imag = [None] * pair_count, [None] * pair_count
        for step in range(LOOK_R):
            at = pl.ds(block * 8 * LOOK_R + step, 8, stride=LOOK_R)
            parts = [[images[date, part, tile, at, :] for part in range(2)] for date in range(2 * group)]
            for date in range(group):
                a0, a1 = parts[date]
                for gap in range(group):
                    b0, b1 = parts[date + gap + 1]
                    combo = date * group + gap
                    re, im = a0 * b0 + a1 * b1, a1 * b0 - a0 * b1
                    real[combo] = re if step == 0 else real[combo] + re
                    imag[combo] = im if step == 0 else imag[combo] + im
        place = pl.ds(pl.multiple_of(block * 8, 8), 8)
        for combo in range(pair_count):
            products[combo, 0, tile, place, :] = real[combo]
            products[combo, 1, tile, place, :] = imag[combo]

    @pl.loop(0, pair_count)
    def _(pair):
        combo = scalars[4 + pair]
        for part in range(2):
            place = pl.ds(pl.multiple_of((part * pair_count + pair) * looks, 16), looks)
            for tile in range(tiles):
                value = products[combo, part, tile]
                head = value.astype(jnp.bfloat16)
                high[place, tile * LANES : (tile + 1) * LANES] = head
                low[place, tile * LANES : (tile + 1) * LANES] = (value - head.astype(jnp.float32)).astype(
                    jnp.bfloat16
                )

    shape = (out_cols, width)
    picked = lax.broadcasted_iota(jnp.int32, shape, 1) // LOOK_C == lax.broadcasted_iota(jnp.int32, shape, 0)
    picked = jnp.where(picked, 1.0, 0.0).astype(jnp.bfloat16)
    turned = (((1,), (1,)), ((), ()))
    looked = lax.dot_general(picked, high[...], turned, preferred_element_type=jnp.float32)
    looked += lax.dot_general(picked, low[...], turned, preferred_element_type=jnp.float32)
    half_width = looked.shape[1] // 2
    real, imag = looked[:, :half_width], looked[:, half_width:]
    imag = jnp.where(imag == 0.0, 0.0, imag)
    phase = jnp.arctan2(imag, real) - cycles[...]
    codes = jnp.round((phase + math.pi) * CODES)
    total = jnp.sum(codes, axis=0, keepdims=True).astype(jnp.int32)
    codes = codes.astype(jnp.int32)
    for octet in range(2):
        row = 2 * slot + octet
        sums[row : row + 1, :] += total[:, octet * LANES : (octet + 1) * LANES]
    words[...] = (codes[:, :LANES] << 16) | (codes[:, LANES:] & 0xFFFF)
    base = (step_at + first_step) * (out_cols // 2) * MESSAGE
    for col in range(2):
        place = pl.ds(base + 2 * col + half, out_cols // 2, stride=MESSAGE)
        payload[place, :] = words[pl.ds(col, out_cols // 2, stride=2), :]

    if final:

        @pl.when(step_at == steps - 1)
        def _():
            total = sums[...]
            for step in (8, 4, 2, 1):
                total += pltpu.roll(total, LANES - step, 1)
            lane = lax.broadcasted_iota(jnp.int32, (1, LANES), 1) % looks
            line = rest[0][0:1, :]
            for at in range(2):
                of = half if at == slot else 1 - half
                for octet in range(2):
                    row = 2 * at + octet
                    for side in range(2):
                        lanes_at = 2 * side + octet
                        moved = pltpu.roll(total, lanes_at, 1)[row : row + 1]
                        line = jnp.where((lane == lanes_at) & (of == side), moved, line)
            count = payload.shape[0] // MESSAGE
            payload[pl.ds(4, count, stride=MESSAGE), :] = jnp.broadcast_to(line, (count, LANES))


def phases(slot, start, stop, final, scalars, acquisitions, other, cycles, line, earlier):
    group, _, height, width = acquisitions.shape
    rows = height // 2
    first_step, steps = start // STEP, (stop - start) // STEP
    lanes = cycles.shape[1] // 2
    out_cols = STEP // LOOK_C
    payload_shape = (cycles.shape[0] // 2 * MESSAGE, LANES)
    looks = rows // LOOK_R
    tiles = STEP // LANES

    in_specs = [
        pl.BlockSpec((group, 2, rows, STEP), lambda i, p: (0, 0, p[1], first_step + i)),
        pl.BlockSpec((None, group, 2, rows, STEP), lambda i, p: (p[3], 0, 0, 0, i)),
        pl.BlockSpec((out_cols, lanes), lambda i, p: (first_step + i, p[0])),
        pl.BlockSpec((8, LANES), lambda i, p: (0, 0)),
    ]
    outs = [
        pl.BlockSpec(payload_shape, lambda i, p: (0, 0)),
        pl.BlockSpec((8, LANES), lambda i, p: (0, 0)),
    ]
    return pl.pallas_call(
        partial(phase_kernel, slot, first_step, steps, final),
        grid_spec=pltpu.PrefetchScalarGridSpec(
            num_scalar_prefetch=1,
            grid=(steps,),
            in_specs=in_specs + outs[: len(earlier)],
            out_specs=outs,
            scratch_shapes=[
                pltpu.VMEM((2 * group, 2, tiles, rows, LANES), jnp.float32),
                pltpu.VMEM((group * group, 2, tiles, looks, LANES), jnp.float32),
                pltpu.VMEM((2 * lanes, STEP), jnp.bfloat16),
                pltpu.VMEM((2 * lanes, STEP), jnp.bfloat16),
                pltpu.VMEM((out_cols, LANES), jnp.int32),
            ],
        ),
        out_shape=[
            jax.ShapeDtypeStruct(payload_shape, jnp.int32),
            jax.ShapeDtypeStruct((8, LANES), jnp.int32),
        ],
        compiler_params=pltpu.CompilerParams(vmem_limit_bytes=60 << 20),
        cost_estimate=pl.CostEstimate(
            flops=8 * group * group * rows * (stop - start),
            bytes_accessed=group * 4 * rows * (stop - start) * 2,
            transcendentals=0,
        ),
        name="phases",
    )(scalars, acquisitions, other, cycles, line, *earlier)


def coded_inverse(inverse):
    turned = inverse.T
    peak = jnp.max(jnp.abs(turned), axis=1, keepdims=True)
    exponent = jnp.clip(jnp.floor(jnp.log2(peak)) + 1.0, -100.0, 100.0)
    codes = jnp.round(turned * jnp.exp2(-exponent) * 32767.0).astype(jnp.int32)
    words = (codes[:, :LANES] << 16) | (codes[:, LANES:] & 0xFFFF)
    return words, exponent[:, 0].astype(jnp.int32)


def exponent_line(exponent):
    spread = exponent.reshape(2, -1).T
    spread = jnp.pad(spread, ((0, 0), (4, LANES // spread.shape[0] - 6)))
    return jnp.broadcast_to(spread.reshape(1, LANES), (8, LANES))


def sent_inverse(words):
    devices, row_count = lax.axis_size("date"), lax.axis_size("row")
    per = words.shape[0] // row_count
    mine = lax.dynamic_slice_in_dim(words, lax.axis_index("row") * per, per, axis=0)
    sent = jnp.broadcast_to(mine[None], (devices, per, LANES))
    got = lax.all_to_all(sent, "date", split_axis=0, concat_axis=0, tiled=True)
    return got.transpose(1, 0, 2)


def invert_kernel(band_pixels, received, inverse, out, bias, left, right):
    pair_count = 16
    sources = inverse.shape[0] // pair_count
    looks = LANES * 2 // pair_count
    pixels = out.shape[0]

    def aligned(words, half):
        value = words.astype(jnp.float32)
        return (pltpu.roll(value, sources - 1, 0) if half else value).T

    right[:, :LANES] = (inverse[...] >> 16).astype(jnp.float32)
    right[:, LANES:] = ((inverse[...] << 16) >> 16).astype(jnp.float32)
    line = received[pl.ds(4, sources, stride=MESSAGE), :]
    lines = aligned(line, 0), aligned(line, 1)
    scales = []
    for pair in range(pair_count):
        octet, at = pair // 8, pair % 8 * looks
        scales.append(jnp.exp2(lines[0][at + 4 + octet : at + 5 + octet]) * (1.0 / 32767.0))
        total = lines[0][at + octet : at + octet + 1] + lines[1][at + 2 + octet : at + 3 + octet]
        left[pixels:, pair * sources : (pair + 1) * sources] = jnp.broadcast_to(
            total * scales[pair], (left.shape[0] - pixels, sources)
        )
    for half in range(2):
        for col in range(pixels // (2 * looks)):
            words = received[pl.ds(col * 2 + half, sources, stride=MESSAGE), :]
            for octet, value in enumerate((words >> 16, (words << 16) >> 16)):
                turned = aligned(value, half)
                for at in range(8):
                    pair = octet * 8 + at
                    row = (col * 2 + half) * looks
                    left[row : row + looks, pair * sources : (pair + 1) * sources] = (
                        turned[at * looks : (at + 1) * looks] * scales[pair]
                    )
    product = jnp.dot(
        left[...], right[...], precision=lax.Precision.HIGHEST, preferred_element_type=jnp.float32
    )
    out[...] = product[:pixels] * (1.0 / CODES)
    bias[...] = product[pixels:] * (1.0 / (CODES * band_pixels))


def invert(received, inverse, pixels, band_pixels):
    total_pairs, dates = inverse.shape[0], 2 * inverse.shape[1]
    return pl.pallas_call(
        partial(invert_kernel, band_pixels),
        in_specs=[pl.BlockSpec(memory_space=pltpu.VMEM)] * 2,
        out_specs=[pl.BlockSpec(memory_space=pltpu.VMEM)] * 2,
        out_shape=[
            jax.ShapeDtypeStruct((pixels, dates), jnp.float32),
            jax.ShapeDtypeStruct((8, dates), jnp.float32),
        ],
        scratch_shapes=[
            pltpu.VMEM((pixels + 8, total_pairs), jnp.float32),
            pltpu.VMEM((total_pairs, dates), jnp.float32),
        ],
        compiler_params=pltpu.CompilerParams(vmem_limit_bytes=24 << 20),
        name="invert",
    )(received, inverse)


def body(acquisitions, date_pairs, cycle_maps, inverse):
    group, _, height, width = acquisitions.shape
    devices = lax.axis_size("date")
    total_dates = group * devices
    pair_count, look_rows, look_cols = cycle_maps.shape
    rows = height // 2
    half = look_rows // 2
    me = lax.axis_index("date")
    odd = me % 2

    gaps = (date_pairs[:, 1] - date_pairs[:, 0] + total_dates) % total_dates
    combos = (date_pairs[:, 0] - me * group) * group + gaps - 1
    named = jnp.broadcast_to(combos[None, :, None], (1, half, look_cols))
    low_data = jnp.concatenate([cycle_maps[:, half:], named]).astype(jnp.bfloat16)
    words, exponent = coded_inverse(inverse)
    line = exponent_line(exponent)
    low_data, words = lax.optimization_barrier((low_data, words))
    low_data = passed_along(low_data, "date", 1)
    share = sent_inverse(words)

    def part(images, block, start, stop):
        return lax.dynamic_slice(images, (0, 0, block * rows, start), (group, 2, rows, stop - start))

    across = [(at, (at + 1 if at % 2 else at - 1) % devices) for at in range(devices)]
    groups = [[at, at + 1] for at in range(0, devices, 2)]
    beside, across_parts, left = [], [], acquisitions
    for start, stop in INNER:
        sent, left = lax.optimization_barrier((part(left, 1 - odd, start, stop), left))
        beside.append(lax.all_gather(sent, "date", axis_index_groups=groups))
    across_parts = [part(left, odd, start, stop) for start, stop in OUTER]
    across_parts, low_data = lax.optimization_barrier((across_parts, low_data))
    crossed = [lax.ppermute(sent, "date", across) for sent in across_parts]

    low_combos = low_data[-1, :, 0].astype(jnp.int32)
    cycles = jnp.stack([cycle_maps[:, :half].astype(jnp.float32), low_data[:-1].astype(jnp.float32)])
    cycles = (TWO_PI * cycles).reshape(2 * pair_count * half, look_cols).T

    inner = jnp.stack([odd, odd, odd * group, 1 - odd])
    outer = jnp.stack([1 - odd, 1 - odd, (1 - odd) * group, odd * 0])
    inner = jnp.concatenate([inner, jnp.where(odd == 0, combos, low_combos)])
    outer = jnp.concatenate([outer, jnp.where(odd == 0, low_combos, combos)])

    inverse = lax.all_gather(share, "row", axis=0, tiled=True).reshape(-1, LANES)

    earlier = ()
    for at, slot in ORDER:
        start, stop = (INNER, OUTER)[slot][at]
        other = crossed[at][None] if slot else beside[at]
        earlier = phases(
            slot,
            start,
            stop,
            (at, slot) == ORDER[-1],
            outer if slot else inner,
            acquisitions,
            other,
            cycles,
            line,
            earlier,
        )

    payload = earlier[0]
    received = lax.all_to_all(
        payload.reshape(devices, 1, -1), "date", split_axis=0, concat_axis=0, tiled=True
    ).reshape(payload.shape)
    out_cols = look_cols // devices
    row_count = lax.axis_size("row")
    result, bias = invert(received, inverse, out_cols * look_rows, look_rows * look_cols * row_count)
    for step in range(1, row_count):
        result = result - passed_along(bias, "row", step)[:1]
    result = result - bias[:1]
    return result.reshape(out_cols, look_rows, total_dates)


def solution(mesh):
    return jax.shard_map(
        body,
        mesh=mesh,
        in_specs=(
            P("date", None, "row", None),
            P("date", None),
            P("date", "row", None),
            P(None, "date"),
        ),
        out_specs=P("date", "row", None),
        check_vma=False,
    )
```

time: 105 us -> 103 us (0.981)
  waiting for transfers between devices: 30.7 us -> 9.29 us
  blocking collectives: 0 us -> 13.3 us
  between operations: 0.21 us -> 13.5 us
  starting transfers between devices: 38.7 us -> 27.2 us
  Pallas kernels: 19.9 us -> 24.8 us
    ppermute x11 -> x4, waiting for transfers between devices: 29.7 us -> 9.24 us  [passed_along(): return lax.ppermute(value, axis, pairs)]
    ppermute x11 -> x4, starting transfers between devices: 19.4 us -> 4.36 us  [passed_along(): return lax.ppermute(value, axis, pairs)]
    all_gather x0 -> x1, blocking collectives: none -> 13.3 us  [body(): lax.all_gather(share, 'row', axis=0, tiled=True).reshape(-1, LANES)]
    dynamic_slice x1 -> x4, local copies, waits for them, and re-layouts: 0.01 us -> 6.46 us  [the longest x3 6.46 us: part(): lax.dynamic_slice(images, (0, 0, block * rows, start), (group, 2, rows, s...]
    slice x2 -> x0, local copies, waits for them, and re-layouts: 6.23 us -> none  [body(): acquisitions[:, :, rows:, start:stop]]
    pallas_call x3 -> x4, Pallas kernels: 19 us -> 23.9 us  [phases(): pl.pallas_call(partial(phase_kernel, slot, first_step, steps, final), gri...]
    ppermute x1 -> x2, starting transfers between devices: 0.2 us -> 3.86 us  [body(): crossed = [lax.ppermute(sent, 'date', across) for sent in across_parts]]
    unnamed x18 -> x11, local copies, waits for them, and re-layouts: 4.21 us -> 1.1 us
  transfers between devices with their start and end apart: 14 -> 10, of which waited for: 6 -> 4; matrix products, arithmetic and copies ran while one was open for 3% -> 10% of each run, Pallas kernels for 18% -> 23%
where the time goes in v3:
time: 103 us
  starting transfers between devices  27.2 us (26%)
  Pallas kernels  24.8 us (24%)
  between operations  13.5 us (13%)
  blocking collectives  13.3 us (13%)
  local copies, waits for them, and re-layouts  11.2 us (11%)
  waiting for transfers between devices  9.29 us (9%)
  other arithmetic  3.28 us (3%)
    pallas_call x4, Pallas kernels, phases(): pl.pallas_call(partial(phase_kernel, slot, first_step, steps, final), gri...  23.9 us
    all_gather x1, blocking collectives, body(): lax.all_gather(share, 'row', axis=0, tiled=True).reshape(-1, LANES)  13.3 us
    all_to_all x1, starting transfers between devices, body(): lax.all_to_all(payload.reshape(devices, 1, -1), 'date', split_axis=0, con...  10.3 us
    ppermute x4, waiting for transfers between devices, passed_along(): return lax.ppermute(value, axis, pairs)  9.24 us
    all_to_all x1, starting transfers between devices, sent_inverse(): got = lax.all_to_all(sent, 'date', split_axis=0, concat_axis=0, tiled=True)  8.66 us
    dynamic_slice x3, local copies, waits for them, and re-layouts, part(): lax.dynamic_slice(images, (0, 0, block * rows, start), (group, 2, rows, s...  6.46 us
    ppermute x4, starting transfers between devices, passed_along(): return lax.ppermute(value, axis, pairs)  4.36 us
    ppermute x2, starting transfers between devices, body(): crossed = [lax.ppermute(sent, 'date', across) for sent in across_parts]  3.86 us
  transfers between devices with their start and end apart: 10, of which 4 were waited for; matrix products, arithmetic and copies ran while one was open for 10% of the time, Pallas kernels for 23%

profile of v3, /device:TPU:6, one launch (start us, length us, event | category | flops | bytes accessed | tf_op | source)
XLA Modules:
  0.0 102.7 jit_solution(1944079649090916908)
XLA Ops:
  6.5 0.0 all-gather.7.cloned.1.call-start
  6.5 2.3 %constant_dynamic-slice_fusion.4 = bf16[4,2,64,1024]{3,2,1,0:T(8,128)(2,1)} fusion(bf16[4,2,128,2048]{3,2,1,0:T(8,128)(2,1)} %own.7, s32[]{:T(128)S(6)} %select_n.42), kind=kLoop, calls=%fused_computation.19 | loop fusion | bytes 2097156 | tf_op jit(solution)/shard_map/dynamic_slice | solution.py:287
  8.9 0.0 all-gather.7.cloned.1.call-update
  8.9 0.0 all-gather.5.cloned.1.call-start
  8.9 2.3 %constant_dynamic-slice_fusion.3 = bf16[4,2,64,1024]{3,2,1,0:T(8,128)(2,1)} fusion(bf16[4,2,128,2048]{3,2,1,0:T(8,128)(2,1)} %own.7, s32[]{:T(128)S(6)} %select_n.42), kind=kLoop, calls=%fused_computation.18 | loop fusion | bytes 2097156 | tf_op jit(solution)/shard_map/dynamic_slice | solution.py:287
  11.3 0.0 all-gather.5.cloned.1.call-update
  11.3 0.0 copy-done.1
  11.3 0.7 convert_bitcast_fusion
  12.0 0.1 abs_reduce_fusion
  12.1 0.1 broadcast_in_dim.12
  12.2 0.1 convert_bitcast_fusion.1
  12.3 0.0 collective-permute-start
  12.3 1.8 %constant_dynamic-slice_fusion.1 = (bf16[4,2,64,1024]{3,2,1,0:T(8,128)(2,1)S(1)}, bf16[4,2,64,1024]{3,2,1,0:T(8,128)(2,1)S(1)}) fusion(bf16[4,2,128,2048]{3,2,1,0:T(8,128)(2,1)} %own.7, s32[]{:T(128)S(6)} %select_n.43), kind=kLoop, calls=%fused_computation.16 | loop fusion | bytes 4194308 | tf_op jit(solution)/shard_map/dynamic_slice | solution.py:287
  14.2 5.7 %collective-permute-done = bf16[17,16,128]{2,1,0:T(8,128)(2,1)S(1)} collective-permute-done((bf16[17,16,128]{2,1,0:T(8,128)(2,1)S(1)}, bf16[17,16,128]{2,1,0:T(8,128)(2,1)S(1)}, u32[]{:S(2)}, u32[]{:S(2)}) %collective-permute-start) | collective-permute-done | bytes 69664 | tf_op jit(solution)/shard_map/ppermute | solution.py:26
  19.9 0.0 collective-permute-start.2
  19.9 3.9 %collective-permute-start.1 = (bf16[4,2,64,1024]{3,2,1,0:T(8,128)(2,1)S(1)}, bf16[4,2,64,1024]{3,2,1,0:T(8,128)(2,1)S(1)}, u32[]{:S(2)}, u32[]{:S(2)}) collective-permute-start(bf16[4,2,64,1024]{3,2,1,0:T(8,128)(2,1)S(1)} %get-tuple-element.27), channel_id=1, source_target_pairs={{0,252},{4,8},{8,4},{12,16},{16,12},{20,24},{24,20},{28,32},{32,28... | collective-permute-start | bytes 3145736 | tf_op jit(solution)/shard_map/ppermute | solution.py:297
  23.7 0.7 broadcast_in_dim.31
  24.4 8.7 %all-to-all-start.1 = ((s32[64,4,128]{2,1,0:T(4,128)}), s32[64,4,128]{2,1,0:T(4,128)S(1)}, u32[]{:S(2)}, u32[]{:S(2)}) async-start(s32[64,4,128]{2,1,0:T(4,128)} %broadcast_in_dim.31), calls=%async_computation.1 | async-start | bytes 262144 | tf_op jit(solution)/shard_map/all_to_all | solution.py:203
  33.1 0.1 reshape.94
  33.2 0.1 copy.13
  33.2 0.1 pad.4.clone
  33.3 0.1 broadcast_in_dim.28
  33.4 0.0 copy-done.2
  33.4 0.9 maximum_multiply_fusion
  34.4 0.8 convert_reduce_fusion
  35.2 0.8 copy.9
  36.0 0.6 concatenate.12.scalars
  36.6 0.7 concatenate.11.scalars
  37.3 0.6 broadcast_in_dim.29.rest_0_
  37.9 5.8 %phases.4 = (s32[320,128]{1,0:T(8,128)}, s32[8,128]{1,0:T(8,128)}) custom-call(s32[20]{0:T(128)} %concatenate.12.scalars, bf16[4,2,128,2048]{3,2,1,0:T(8,128)(2,1)} %own.7, bf16[2,4,2,64,1024]{4,3,2,1,0:T(8,128)(2,1)} %bitcast.43, f32[128,512]{1,0:T(8,128)} %bitcast.39, s32[8,128]{1,0:T(8,128)} %broadcast_in_dim.29.rest_0_), custom_call_target="tpu_custom_call" | custom-call | flops 8388608 | bytes 2097152 | tf_op jit(solution)/shard_map/phases/pallas_call | solution.py:154
  43.7 0.0 collective-permute-done.2
  43.7 5.9 %phases.5 = (s32[320,128]{1,0:T(8,128)}, s32[8,128]{1,0:T(8,128)}) custom-call(s32[20]{0:T(128)} %concatenate.11.scalars, bf16[4,2,128,2048]{3,2,1,0:T(8,128)(2,1)} %own.7, bf16[1,4,2,64,1024]{4,3,2,1,0:T(8,128)(2,1)} %bitcast.14.other, f32[128,512]{1,0:T(8,128)} %bitcast.40, s32[8,128]{1,0:T(8,128)} %broadcast_in_dim.29.rest_0_, ...), custom_call_target="tpu_custom_call" | custom-call | flops 8388608 | bytes 2097152 | tf_op jit(solution)/shard_map/phases/pallas_call | solution.py:154
  49.6 5.9 %phases.6 = (s32[320,128]{1,0:T(8,128)}, s32[8,128]{1,0:T(8,128)}) custom-call(s32[20]{0:T(128)} %concatenate.12.scalars, bf16[4,2,128,2048]{3,2,1,0:T(8,128)(2,1)} %own.7, bf16[2,4,2,64,1024]{4,3,2,1,0:T(8,128)(2,1)} %bitcast.44, f32[128,512]{1,0:T(8,128)} %bitcast.41, s32[8,128]{1,0:T(8,128)} %broadcast_in_dim.29.rest_0_, ...), custom_call_target="tpu_custom_call" | custom-call | flops 8388608 | bytes 2097152 | tf_op jit(solution)/shard_map/phases/pallas_call | solution.py:154
  55.5 0.0 collective-permute-done.1
  55.5 1.0 copy-done
  56.5 6.3 %phases.7 = (s32[320,128]{1,0:T(8,128)}, s32[8,128]{1,0:T(8,128)}) custom-call(s32[20]{0:T(128)} %concatenate.11.scalars, bf16[4,2,128,2048]{3,2,1,0:T(8,128)(2,1)} %own.7, bf16[1,4,2,64,1024]{4,3,2,1,0:T(8,128)(2,1)} %bitcast.46, f32[128,512]{1,0:T(8,128)} %bitcast.42, s32[8,128]{1,0:T(8,128)} %broadcast_in_dim.29.rest_0_, ...), custom_call_target="tpu_custom_call" | custom-call | flops 8388608 | bytes 2097152 | tf_op jit(solution)/shard_map/phases/pallas_call | solution.py:154
  62.7 0.0 all-to-all-done.1
  62.7 10.3 %all-to-all-start = ((s32[64,1,640]{2,1,0:T(1,128)}), s32[64,1,640]{2,1,0:T(1,128)S(1)}, u32[]{:S(2)}, u32[]{:S(2)}) async-start(s32[64,1,640]{2,1,0:T(1,128)} %bitcast.48), calls=%async_computation | async-start | bytes 327680 | tf_op jit(solution)/shard_map/all_to_all | solution.py:328
  73.1 13.3 %all_gather.19 = s32[16,64,128]{2,1,0:T(8,128)S(1)} all-gather(s32[4,64,128]{2,1,0:T(8,128)S(1)} %copy.12), channel_id=1, replica_groups=mesh['date'=64,'row'=4] {'row'}, dimensions={0}, use_global_device_ids=true | all-gather | bytes 655360 | tf_op jit(solution)/shard_map/all_gather | solution.py:308
  86.4 0.0 all-to-all-done
  86.4 1.0 invert.1
  87.4 1.6 %collective-permute-start.3 = (f32[8,256]{1,0:T(8,128)S(1)}, f32[8,256]{1,0:T(8,128)S(1)}, u32[]{:S(2)}, u32[]{:S(2)}) collective-permute-start(f32[8,256]{1,0:T(8,128)S(1)} %get-tuple-element.40), channel_id=1, source_target_pairs={{0,1},{1,2},{2,3},{3,0},{4,5},{5,6},{6,7},{7,4},{8,9},{9,10},{10,1... | collective-permute-start | bytes 24584 | tf_op jit(solution)/shard_map/ppermute | solution.py:26
  88.9 2.7 %collective-permute-start.4 = (f32[8,256]{1,0:T(8,128)S(1)}, f32[8,256]{1,0:T(8,128)S(1)}, u32[]{:S(2)}, u32[]{:S(2)}) collective-permute-start(f32[8,256]{1,0:T(8,128)S(1)} %get-tuple-element.40), channel_id=1, source_target_pairs={{0,2},{1,3},{2,0},{3,1},{4,6},{5,7},{6,4},{7,5},{8,10},{9,11},{10,... | collective-permute-start | bytes 24584 | tf_op jit(solution)/shard_map/ppermute | solution.py:26
  91.6 0.1 collective-permute-start.5
  91.7 0.6 collective-permute-done.3
  92.3 1.8 %collective-permute-done.4 = f32[8,256]{1,0:T(8,128)S(1)} collective-permute-done((f32[8,256]{1,0:T(8,128)S(1)}, f32[8,256]{1,0:T(8,128)S(1)}, u32[]{:S(2)}, u32[]{:S(2)}) %collective-permute-start.4) | collective-permute-done | bytes 8224 | tf_op jit(solution)/shard_map/ppermute | solution.py:26
  94.1 1.2 %collective-permute-done.5 = f32[8,256]{1,0:T(8,128)S(1)} collective-permute-done((f32[8,256]{1,0:T(8,128)S(1)}, f32[8,256]{1,0:T(8,128)S(1)}, u32[]{:S(2)}, u32[]{:S(2)}) %collective-permute-start.5) | collective-permute-done | bytes 8224 | tf_op jit(solution)/shard_map/ppermute | solution.py:26
  95.3 0.6 subtract_subtract_fusion
  (21 shorter events, 0.1 us)
Async XLA Ops:
  6.5 4.7 %copy-start.1 = (s32[16,32,128]{2,1,0:T(8,128)S(1)}, s32[16,32,128]{2,1,0:T(8,128)}, u32[]{:S(2)}) copy-start(s32[16,32,128]{2,1,0:T(8,128)} %param.6) | copy-start | bytes 786436
  6.5 5.4 %copy-start.4 = (s32[16,2]{0,1:T(2,128)S(1)}, s32[16,2]{0,1:T(2,128)}, u32[]{:S(2)}) copy-start(s32[16,2]{0,1:T(2,128)} %param.5) | copy-start | bytes 388
  6.5 5.4 %copy-start.3 = (f32[256,16]{0,1:T(8,128)S(1)}, f32[256,16]{0,1:T(8,128)}, u32[]{:S(2)}) copy-start(f32[256,16]{0,1:T(8,128)} %param.7) | copy-start | bytes 49156
  6.5 30.7 %all-gather.7.cloned.1.call-start = ((), (), s32[]{:S(2)}) async-start(), calls=%async_computation.3 | async-start | bytes 3145728 | tf_op jit(solution)/shard_map/all_gather | solution.py:294
  8.9 40.7 %all-gather.5.cloned.1.call-start = ((), (), s32[]{:S(2)}) async-start(), calls=%async_computation.2 | async-start | bytes 3145728 | tf_op jit(solution)/shard_map/all_gather | solution.py:294
  12.3 7.6 %collective-permute-start = (bf16[17,16,128]{2,1,0:T(8,128)(2,1)S(1)}, bf16[17,16,128]{2,1,0:T(8,128)(2,1)S(1)}, u32[]{:S(2)}, u32[]{:S(2)}) collective-permute-start(bf16[17,16,128]{2,1,0:T(8,128)(2,1)S(1)} %pad_maximum_fusion), channel_id=1, source_target_pairs={{0,4},{4,8},{8,12},{12,16},{16,20},{20,24},{24,28},{28,32},{32,36}... | collective-permute-start | bytes 208904 | tf_op jit(solution)/shard_map/ppermute | solution.py:26
  19.9 13.6 %copy-start.2 = (bf16[17,16,128]{2,1,0:T(8,128)(2,1)}, bf16[17,16,128]{2,1,0:T(8,128)(2,1)S(1)}, u32[]{:S(2)}) copy-start(bf16[17,16,128]{2,1,0:T(8,128)(2,1)S(1)} %collective-permute-done) | copy-start | bytes 208900
  19.9 23.8 %collective-permute-start.2 = (bf16[4,2,64,1024]{3,2,1,0:T(8,128)(2,1)S(1)}, bf16[4,2,64,1024]{3,2,1,0:T(8,128)(2,1)}, u32[]{:S(2)}, u32[]{:S(2)}) collective-permute-start(bf16[4,2,64,1024]{3,2,1,0:T(8,128)(2,1)S(1)} %get-tuple-element.29), channel_id=1, source_target_pairs={{0,252},{4,8},{8,4},{12,16},{16,12},{20,24},{24,20},{28,32},{32,28... | collective-permute-start | bytes 3145736 | tf_op jit(solution)/shard_map/ppermute | solution.py:297
  19.9 35.6 %collective-permute-start.1 = (bf16[4,2,64,1024]{3,2,1,0:T(8,128)(2,1)S(1)}, bf16[4,2,64,1024]{3,2,1,0:T(8,128)(2,1)S(1)}, u32[]{:S(2)}, u32[]{:S(2)}) collective-permute-start(bf16[4,2,64,1024]{3,2,1,0:T(8,128)(2,1)S(1)} %get-tuple-element.27), channel_id=1, source_target_pairs={{0,252},{4,8},{8,4},{12,16},{16,12},{20,24},{24,20},{28,32},{32,28... | collective-permute-start | bytes 3145736 | tf_op jit(solution)/shard_map/ppermute | solution.py:297
  24.4 38.3 %all-to-all-start.1 = ((s32[64,4,128]{2,1,0:T(4,128)}), s32[64,4,128]{2,1,0:T(4,128)S(1)}, u32[]{:S(2)}, u32[]{:S(2)}) async-start(s32[64,4,128]{2,1,0:T(4,128)} %broadcast_in_dim.31), calls=%async_computation.1 | async-start | bytes 262144 | tf_op jit(solution)/shard_map/all_to_all | solution.py:203
  55.5 1.0 copy-start
  62.7 23.7 %all-to-all-start = ((s32[64,1,640]{2,1,0:T(1,128)}), s32[64,1,640]{2,1,0:T(1,128)S(1)}, u32[]{:S(2)}, u32[]{:S(2)}) async-start(s32[64,1,640]{2,1,0:T(1,128)} %bitcast.48), calls=%async_computation | async-start | bytes 327680 | tf_op jit(solution)/shard_map/all_to_all | solution.py:328
  87.4 4.9 %collective-permute-start.3 = (f32[8,256]{1,0:T(8,128)S(1)}, f32[8,256]{1,0:T(8,128)S(1)}, u32[]{:S(2)}, u32[]{:S(2)}) collective-permute-start(f32[8,256]{1,0:T(8,128)S(1)} %get-tuple-element.40), channel_id=1, source_target_pairs={{0,1},{1,2},{2,3},{3,0},{4,5},{5,6},{6,7},{7,4},{8,9},{9,10},{10,1... | collective-permute-start | bytes 24584 | tf_op jit(solution)/shard_map/ppermute | solution.py:26
  88.9 5.2 %collective-permute-start.4 = (f32[8,256]{1,0:T(8,128)S(1)}, f32[8,256]{1,0:T(8,128)S(1)}, u32[]{:S(2)}, u32[]{:S(2)}) collective-permute-start(f32[8,256]{1,0:T(8,128)S(1)} %get-tuple-element.40), channel_id=1, source_target_pairs={{0,2},{1,3},{2,0},{3,1},{4,6},{5,7},{6,4},{7,5},{8,10},{9,11},{10,... | collective-permute-start | bytes 24584 | tf_op jit(solution)/shard_map/ppermute | solution.py:26
  91.6 3.7 %collective-permute-start.5 = (f32[8,256]{1,0:T(8,128)S(1)}, f32[8,256]{1,0:T(8,128)S(1)}, u32[]{:S(2)}, u32[]{:S(2)}) collective-permute-start(f32[8,256]{1,0:T(8,128)S(1)} %get-tuple-element.40), channel_id=1, source_target_pairs={{0,3},{1,0},{2,1},{3,2},{4,7},{5,4},{6,5},{7,6},{8,11},{9,8},{10,9... | collective-permute-start | bytes 24584 | tf_op jit(solution)/shard_map/ppermute | solution.py:26
Sparse Core Ops, SparseCore 0:
  9.2 18.8 all-gather.6
  29.8 17.2 all-gather.4

commit v4 on v3

--- a/solution.py
+++ b/solution.py
@@ -12,11 +12,9 @@
 LOOK_C = 16
 TWO_PI = 2.0 * math.pi
 CODES = 32767.0 / TWO_PI
-INNER = ((0, 1024), (1024, 2048))
-OUTER = ((0, 1024), (1024, 2048))
-ORDER = ((0, 0), (0, 1), (1, 0), (1, 1))
+CHUNKS = ((0, 1024), (1024, 2048))
 STEP = 512
-MESSAGE = 5
+MESSAGE = 8
 LANES = 128
 
 
@@ -143,7 +141,7 @@
 
     in_specs = [
         pl.BlockSpec((group, 2, rows, STEP), lambda i, p: (0, 0, p[1], first_step + i)),
-        pl.BlockSpec((None, group, 2, rows, STEP), lambda i, p: (p[3], 0, 0, 0, i)),
+        pl.BlockSpec((group, 2, rows, STEP), lambda i, p: (0, 0, 0, i)),
         pl.BlockSpec((out_cols, lanes), lambda i, p: (first_step + i, p[0])),
         pl.BlockSpec((8, LANES), lambda i, p: (0, 0)),
     ]
@@ -170,7 +168,7 @@
             jax.ShapeDtypeStruct(payload_shape, jnp.int32),
             jax.ShapeDtypeStruct((8, LANES), jnp.int32),
         ],
-        compiler_params=pltpu.CompilerParams(vmem_limit_bytes=60 << 20),
+        compiler_params=pltpu.CompilerParams(vmem_limit_bytes=20 << 20),
         cost_estimate=pl.CostEstimate(
             flops=8 * group * group * rows * (stop - start),
             bytes_accessed=group * 4 * rows * (stop - start) * 2,
@@ -196,12 +194,10 @@
 
 
 def sent_inverse(words):
-    devices, row_count = lax.axis_size("date"), lax.axis_size("row")
-    per = words.shape[0] // row_count
-    mine = lax.dynamic_slice_in_dim(words, lax.axis_index("row") * per, per, axis=0)
-    sent = jnp.broadcast_to(mine[None], (devices, per, LANES))
+    devices = lax.axis_size("date")
+    sent = jnp.broadcast_to(words[None], (devices, *words.shape))
     got = lax.all_to_all(sent, "date", split_axis=0, concat_axis=0, tiled=True)
-    return got.transpose(1, 0, 2)
+    return got.reshape(-1, LANES)
 
 
 def invert_kernel(band_pixels, received, inverse, out, bias, left, right):
@@ -214,8 +210,11 @@
         value = words.astype(jnp.float32)
         return (pltpu.roll(value, sources - 1, 0) if half else value).T
 
-    right[:, :LANES] = (inverse[...] >> 16).astype(jnp.float32)
-    right[:, LANES:] = ((inverse[...] << 16) >> 16).astype(jnp.float32)
+    for pair in range(pair_count):
+        words = inverse[pl.ds(pair, sources, stride=pair_count), :]
+        place = slice(pair * sources, (pair + 1) * sources)
+        right[place, :LANES] = (words >> 16).astype(jnp.float32)
+        right[place, LANES:] = ((words << 16) >> 16).astype(jnp.float32)
     line = received[pl.ds(4, sources, stride=MESSAGE), :]
     lines = aligned(line, 0), aligned(line, 1)
     scales = []
@@ -271,7 +270,6 @@
     rows = height // 2
     half = look_rows // 2
     me = lax.axis_index("date")
-    odd = me % 2
 
     gaps = (date_pairs[:, 1] - date_pairs[:, 0] + total_dates) % total_dates
     combos = (date_pairs[:, 0] - me * group) * group + gaps - 1
@@ -281,52 +279,41 @@
     line = exponent_line(exponent)
     low_data, words = lax.optimization_barrier((low_data, words))
     low_data = passed_along(low_data, "date", 1)
-    share = sent_inverse(words)
-
-    def part(images, block, start, stop):
-        return lax.dynamic_slice(images, (0, 0, block * rows, start), (group, 2, rows, stop - start))
-
-    across = [(at, (at + 1 if at % 2 else at - 1) % devices) for at in range(devices)]
-    groups = [[at, at + 1] for at in range(0, devices, 2)]
-    beside, across_parts, left = [], [], acquisitions
-    for start, stop in INNER:
-        sent, left = lax.optimization_barrier((part(left, 1 - odd, start, stop), left))
-        beside.append(lax.all_gather(sent, "date", axis_index_groups=groups))
-    across_parts = [part(left, odd, start, stop) for start, stop in OUTER]
-    across_parts, low_data = lax.optimization_barrier((across_parts, low_data))
-    crossed = [lax.ppermute(sent, "date", across) for sent in across_parts]
+    inverse = sent_inverse(words)
+
+    others, left = [], acquisitions
+    for start, stop in CHUNKS:
+        parts = left[:, :, :rows, start:stop], left[:, :, rows:, start:stop]
+        parts, left, low_data = lax.optimization_barrier((parts, left, low_data))
+        others.append((passed_along(parts[0], "date", -1), passed_along(parts[1], "date", 1)))
 
     low_combos = low_data[-1, :, 0].astype(jnp.int32)
     cycles = jnp.stack([cycle_maps[:, :half].astype(jnp.float32), low_data[:-1].astype(jnp.float32)])
     cycles = (TWO_PI * cycles).reshape(2 * pair_count * half, look_cols).T
 
-    inner = jnp.stack([odd, odd, odd * group, 1 - odd])
-    outer = jnp.stack([1 - odd, 1 - odd, (1 - odd) * group, odd * 0])
-    inner = jnp.concatenate([inner, jnp.where(odd == 0, combos, low_combos)])
-    outer = jnp.concatenate([outer, jnp.where(odd == 0, low_combos, combos)])
-
-    inverse = lax.all_gather(share, "row", axis=0, tiled=True).reshape(-1, LANES)
-
+    scalars = [
+        jnp.concatenate([jnp.array([side, side, side * group, 0], jnp.int32), named])
+        for side, named in enumerate((combos, low_combos))
+    ]
     earlier = ()
-    for at, slot in ORDER:
-        start, stop = (INNER, OUTER)[slot][at]
-        other = crossed[at][None] if slot else beside[at]
-        earlier = phases(
-            slot,
-            start,
-            stop,
-            (at, slot) == ORDER[-1],
-            outer if slot else inner,
-            acquisitions,
-            other,
-            cycles,
-            line,
-            earlier,
-        )
+    for chunk, (start, stop) in enumerate(CHUNKS):
+        for side in range(2):
+            earlier = phases(
+                side,
+                start,
+                stop,
+                stop == width and side == 1,
+                scalars[side],
+                acquisitions,
+                others[chunk][side],
+                cycles,
+                line,
+                earlier,
+            )
 
     payload = earlier[0]
     received = lax.all_to_all(
-        payload.reshape(devices, 1, -1), "date", split_axis=0, concat_axis=0, tiled=True
+        payload.reshape(devices, MESSAGE, LANES), "date", split_axis=0, concat_axis=0, tiled=True
     ).reshape(payload.shape)
     out_cols = look_cols // devices
     row_count = lax.axis_size("row")

time: 103 us -> 91.3 us (0.89)
  between operations: 13.5 us -> 0.12 us
  blocking collectives: 13.3 us -> 22.6 us
  starting transfers between devices: 27.2 us -> 19.4 us
  waiting for transfers between devices: 9.29 us -> 16.1 us
  Pallas kernels: 24.8 us -> 19.8 us
  local copies, waits for them, and re-layouts: 11.2 us -> 8.51 us
  other arithmetic: 3.28 us -> 4.39 us
    all_to_all x0 -> x1, blocking collectives: none -> 22.6 us  [body(): lax.all_to_all(payload.reshape(devices, MESSAGE, LANES), 'date', split_ax...]
    all_gather x1 -> x0, blocking collectives: 13.3 us -> none  [body(): lax.all_gather(share, 'row', axis=0, tiled=True).reshape(-1, LANES)]
    all_to_all x1 -> x0, starting transfers between devices: 10.3 us -> none  [body(): lax.all_to_all(payload.reshape(devices, 1, -1), 'date', split_axis=0, con...]
    ppermute x4 -> x8, waiting for transfers between devices: 9.24 us -> 16.1 us  [passed_along(): return lax.ppermute(value, axis, pairs)]
    dynamic_slice x4 -> x0, local copies, waits for them, and re-layouts: 6.46 us -> none  [the longest x3 6.46 us: part(): lax.dynamic_slice(images, (0, 0, block * rows, start), (group, 2, rows, s...]
    pallas_call x4, Pallas kernels: 23.9 us -> 18.8 us  [phases(): pl.pallas_call(partial(phase_kernel, slot, first_step, steps, final), gri...]
    slice x0 -> x2, local copies, waits for them, and re-layouts: none -> 4.86 us  [body(): parts = (left[:, :, :rows, start:stop], left[:, :, rows:, start:stop])]
    ppermute x4 -> x8, starting transfers between devices: 4.36 us -> 9.14 us  [passed_along(): return lax.ppermute(value, axis, pairs)]
  transfers between devices with their start and end apart: 10 -> 9, of which waited for: 4 -> 4; matrix products, arithmetic and copies ran while one was open for 10% -> 7% of each run, Pallas kernels for 23% -> 21%
where the time goes in v4:
time: 91.3 us; the launch traced here: 90.8 us
  blocking collectives  22.6 us (25%)
  Pallas kernels  19.8 us (22%)
  starting transfers between devices  19.4 us (21%)
  waiting for transfers between devices  16.1 us (18%)
  local copies, waits for them, and re-layouts  8.51 us (9%)
  other arithmetic  4.39 us (5%)
    all_to_all x1, blocking collectives, body(): lax.all_to_all(payload.reshape(devices, MESSAGE, LANES), 'date', split_ax...  22.6 us
    pallas_call x4, Pallas kernels, phases(): pl.pallas_call(partial(phase_kernel, slot, first_step, steps, final), gri...  18.8 us
    ppermute x8, waiting for transfers between devices, passed_along(): return lax.ppermute(value, axis, pairs)  16.1 us
    all_to_all x1, starting transfers between devices, sent_inverse(): got = lax.all_to_all(sent, 'date', split_axis=0, concat_axis=0, tiled=True)  10.2 us
    ppermute x8, starting transfers between devices, passed_along(): return lax.ppermute(value, axis, pairs)  9.14 us
    slice x2, local copies, waits for them, and re-layouts, body(): parts = (left[:, :, :rows, start:stop], left[:, :, rows:, start:stop])  4.86 us
    unnamed x7, local copies, waits for them, and re-layouts  2.28 us
  transfers between devices with their start and end apart: 9, of which 4 were waited for; matrix products, arithmetic and copies ran while one was open for 7% of the time, Pallas kernels for 21%

profile of v4, /device:TPU:6, one launch (start us, length us, event | category | flops | bytes accessed | tf_op | source)
XLA Modules:
  0.0 90.8 jit_solution(7632644488874848615)
XLA Ops:
  0.0 0.8 abs_reduce_fusion
  0.8 0.8 convert_bitcast_fusion.1
  1.7 1.0 %convert_bitcast_fusion = (f32[1,16,16,128]{3,2,1,0:T(8,128)S(1)}, bf16[16,16,128]{2,1,0:T(8,128)(2,1)S(1)}) fusion(s32[16,32,128]{2,1,0:T(8,128)} %param.8), kind=kLoop, calls=%fused_computation.2 | loop fusion | flops 65536 | bytes 458752 | tf_op jit(solution)/shard_map/stack | solution.py:291
  2.7 0.0 copy-start
  2.7 0.9 fusion.5
  3.5 0.1 broadcast_in_dim.8
  3.6 0.1 collective-permute-start
  3.7 3.4 %fusion.8 = (bf16[4,2,64,1024]{3,2,1,0:T(8,128)(2,1)}, bf16[4,2,64,1024]{3,2,1,0:T(8,128)(2,1)}) fusion(bf16[4,2,128,2048]{3,2,1,0:T(8,128)(2,1)} %own.7), kind=kLoop, calls=%fused_computation.24 | loop fusion | bytes 4194304 | tf_op jit(solution)/shard_map/slice | solution.py:286
  7.1 0.0 copy-start.2
  7.1 4.2 %collective-permute-done = bf16[17,16,128]{2,1,0:T(8,128)(2,1)S(1)} collective-permute-done((bf16[17,16,128]{2,1,0:T(8,128)(2,1)S(1)}, bf16[17,16,128]{2,1,0:T(8,128)(2,1)S(1)}, u32[]{:S(2)}, u32[]{:S(2)}) %collective-permute-start) | collective-permute-done | bytes 69664 | tf_op jit(solution)/shard_map/ppermute | solution.py:24
  11.3 0.0 collective-permute-start.3
  11.3 3.9 %collective-permute-start.4 = (bf16[4,2,64,1024]{3,2,1,0:T(8,128)(2,1)}, bf16[4,2,64,1024]{3,2,1,0:T(8,128)(2,1)S(1)}, u32[]{:S(2)}, u32[]{:S(2)}) collective-permute-start(bf16[4,2,64,1024]{3,2,1,0:T(8,128)(2,1)} %get-tuple-element.30), channel_id=1, source_target_pairs={{0,252},{4,0},{8,4},{12,8},{16,12},{20,16},{24,20},{28,24},{32,28}... | collective-permute-start | bytes 3145736 | tf_op jit(solution)/shard_map/ppermute | solution.py:24
  15.1 0.0 copy-done
  15.1 1.5 %fusion.7 = (bf16[4,2,64,1024]{3,2,1,0:T(8,128)(2,1)}, bf16[4,2,64,1024]{3,2,1,0:T(8,128)(2,1)}) fusion(bf16[4,2,128,2048]{3,2,1,0:T(8,128)(2,1)S(1)} %copy-done), kind=kLoop, calls=%fused_computation.23 | loop fusion | bytes 4194304 | tf_op jit(solution)/shard_map/slice | solution.py:286
  16.6 0.0 collective-permute-start.2
  16.6 0.5 collective-permute-start.1
  17.1 0.8 broadcast_in_dim.11
  18.0 10.2 %all-to-all-start.1 = ((s32[64,16,128]{2,1,0:T(8,128)}), s32[64,16,128]{2,1,0:T(8,128)S(1)}, u32[]{:S(2)}, u32[]{:S(2)}) async-start(s32[64,16,128]{2,1,0:T(8,128)} %broadcast_in_dim.11), calls=%async_computation.1 | async-start | bytes 1048576 | tf_op jit(solution)/shard_map/all_to_all | solution.py:199
  28.2 0.1 reshape.94
  28.3 0.1 copy.11
  28.4 0.1 pad.5.scalars
  28.4 0.1 pad.4.clone
  28.5 0.1 broadcast_in_dim.9
  28.6 0.1 copy.9
  28.8 0.1 convert_reduce_fusion
  28.9 0.0 copy-done.2
  28.9 0.1 pad_add_fusion.scalars
  29.0 0.0 collective-permute-done.4.other
  29.0 0.0 copy-start.1
  29.0 2.2 %copy-done.1 = bf16[4,2,128,2048]{3,2,1,0:T(8,128)(2,1)S(1)} copy-done((bf16[4,2,128,2048]{3,2,1,0:T(8,128)(2,1)S(1)}, bf16[4,2,128,2048]{3,2,1,0:T(8,128)(2,1)}, u32[]{:S(2)}) %copy-start.1) | copy-done | bytes 4194328
  31.2 4.0 %phases.4 = (s32[512,128]{1,0:T(8,128)S(1)}, s32[8,128]{1,0:T(8,128)S(1)}) custom-call(s32[20]{0:T(128)S(1)} %pad.5.scalars, bf16[4,2,128,2048]{3,2,1,0:T(8,128)(2,1)S(1)} %copy-done.1, bf16[4,2,64,1024]{3,2,1,0:T(8,128)(2,1)S(1)} %collective-permute-done.4.other, f32[128,512]{1,0:T(8,128)S(1)} %bitcast.28, s32[8,128]{1,0:T(8,128)S(1)} %broadcast_in_dim.10.rest_0_), custom_call_target="tpu_custom_call" | custom-call | flops 8388608 | bytes 2097152 | tf_op jit(solution)/shard_map/phases/pallas_call | solution.py:152
  35.2 0.0 collective-permute-done.3.other
  35.2 4.9 %phases.5 = (s32[512,128]{1,0:T(8,128)S(1)}, s32[8,128]{1,0:T(8,128)S(1)}) custom-call(s32[20]{0:T(128)S(1)} %pad_add_fusion.scalars, bf16[4,2,128,2048]{3,2,1,0:T(8,128)(2,1)S(1)} %copy-done.1, bf16[4,2,64,1024]{3,2,1,0:T(8,128)(2,1)} %collective-permute-done.3.other, f32[128,512]{1,0:T(8,128)S(1)} %bitcast.29, s32[8,128]{1,0:T(8,128)S(1)} %broadcast_in_dim.10.rest_0_, ...), custom_call_target="tpu_custom_call" | custom-call | flops 8388608 | bytes 2097152 | tf_op jit(solution)/shard_map/phases/pallas_call | solution.py:152
  40.1 8.0 %collective-permute-done.2.other = bf16[4,2,64,1024]{3,2,1,0:T(8,128)(2,1)} collective-permute-done((bf16[4,2,64,1024]{3,2,1,0:T(8,128)(2,1)}, bf16[4,2,64,1024]{3,2,1,0:T(8,128)(2,1)}, u32[]{:S(2)}, u32[]{:S(2)}) %collective-permute-start.2) | collective-permute-done | bytes 1048608 | tf_op jit(solution)/shard_map/ppermute | solution.py:24
  48.1 4.9 %phases.6 = (s32[512,128]{1,0:T(8,128)S(1)}, s32[8,128]{1,0:T(8,128)S(1)}) custom-call(s32[20]{0:T(128)S(1)} %pad.5.scalars, bf16[4,2,128,2048]{3,2,1,0:T(8,128)(2,1)S(1)} %copy-done.1, bf16[4,2,64,1024]{3,2,1,0:T(8,128)(2,1)} %collective-permute-done.2.other, f32[128,512]{1,0:T(8,128)S(1)} %bitcast.30, s32[8,128]{1,0:T(8,128)S(1)} %broadcast_in_dim.10.rest_0_, ...), custom_call_target="tpu_custom_call" | custom-call | flops 8388608 | bytes 2097152 | tf_op jit(solution)/shard_map/phases/pallas_call | solution.py:152
  53.0 0.0 collective-permute-done.1.other
  53.1 5.0 %phases.7 = (s32[512,128]{1,0:T(8,128)S(1)}, s32[8,128]{1,0:T(8,128)}) custom-call(s32[20]{0:T(128)S(1)} %pad_add_fusion.scalars, bf16[4,2,128,2048]{3,2,1,0:T(8,128)(2,1)S(1)} %copy-done.1, bf16[4,2,64,1024]{3,2,1,0:T(8,128)(2,1)S(1)} %collective-permute-done.1.other, f32[128,512]{1,0:T(8,128)S(1)} %bitcast.31, s32[8,128]{1,0:T(8,128)S(1)} %broadcast_in_dim.10.rest_0_, ...), custom_call_target="tpu_custom_call" | custom-call | flops 8388608 | bytes 2097152 | tf_op jit(solution)/shard_map/phases/pallas_call | solution.py:152
  58.0 0.0 all-to-all-done.1
  58.0 22.6 %all_to_all.10 = s32[64,8,128]{2,1,0:T(8,128)S(1)} all-to-all(s32[64,8,128]{2,1,0:T(8,128)S(1)} %bitcast.34), channel_id=1, replica_groups=mesh['date'=64,'row'=4] {'date'}, dimensions={0} | all-to-all | bytes 524288 | tf_op jit(solution)/shard_map/all_to_all | solution.py:315
  80.6 1.0 %invert.1 = (f32[64,256]{1,0:T(8,128)S(1)}, f32[8,256]{1,0:T(8,128)S(1)}) custom-call(s32[512,128]{1,0:T(8,128)S(1)} %bitcast.33, s32[1024,128]{1,0:T(8,128)S(1)} %bitcast.32), custom_call_target="tpu_custom_call" | custom-call | tf_op jit(solution)/shard_map/invert/pallas_call | solution.py:248
  81.6 3.1 %collective-permute-start.7 = (f32[8,256]{1,0:T(8,128)S(1)}, f32[8,256]{1,0:T(8,128)S(1)}, u32[]{:S(2)}, u32[]{:S(2)}) collective-permute-start(f32[8,256]{1,0:T(8,128)S(1)} %get-tuple-element.40), channel_id=1, source_target_pairs={{0,3},{1,0},{2,1},{3,2},{4,7},{5,4},{6,5},{7,6},{8,11},{9,8},{10,9... | collective-permute-start | bytes 24584 | tf_op jit(solution)/shard_map/ppermute | solution.py:24
  84.7 0.6 collective-permute-start.6
  85.3 1.0 %collective-permute-start.5 = (f32[8,256]{1,0:T(8,128)S(1)}, f32[8,256]{1,0:T(8,128)S(1)}, u32[]{:S(2)}, u32[]{:S(2)}) collective-permute-start(f32[8,256]{1,0:T(8,128)S(1)} %get-tuple-element.40), channel_id=1, source_target_pairs={{0,1},{1,2},{2,3},{3,0},{4,5},{5,6},{6,7},{7,4},{8,9},{9,10},{10,1... | collective-permute-start | bytes 24584 | tf_op jit(solution)/shard_map/ppermute | solution.py:24
  86.3 0.0 collective-permute-done.7
  86.3 3.5 %collective-permute-done.6 = f32[8,256]{1,0:T(8,128)S(1)} collective-permute-done((f32[8,256]{1,0:T(8,128)S(1)}, f32[8,256]{1,0:T(8,128)S(1)}, u32[]{:S(2)}, u32[]{:S(2)}) %collective-permute-start.6) | collective-permute-done | bytes 8224 | tf_op jit(solution)/shard_map/ppermute | solution.py:24
  89.9 0.3 collective-permute-done.5
  90.2 0.6 subtract_subtract_fusion
  (10 shorter events, 0.1 us)
Async XLA Ops:
  2.7 12.5 %copy-start = (bf16[4,2,128,2048]{3,2,1,0:T(8,128)(2,1)S(1)}, bf16[4,2,128,2048]{3,2,1,0:T(8,128)(2,1)}, u32[]{:S(2)}) copy-start(bf16[4,2,128,2048]{3,2,1,0:T(8,128)(2,1)} %own.7) | copy-start | bytes 12582916
  3.6 7.6 %collective-permute-start = (bf16[17,16,128]{2,1,0:T(8,128)(2,1)S(1)}, bf16[17,16,128]{2,1,0:T(8,128)(2,1)S(1)}, u32[]{:S(2)}, u32[]{:S(2)}) collective-permute-start(bf16[17,16,128]{2,1,0:T(8,128)(2,1)S(1)} %pad_maximum_fusion), channel_id=1, source_target_pairs={{0,4},{4,8},{8,12},{12,16},{16,20},{20,24},{24,28},{28,32},{32,36}... | collective-permute-start | bytes 208904 | tf_op jit(solution)/shard_map/ppermute | solution.py:24
  7.1 21.8 %copy-start.2 = (s32[4]{0:T(128)S(1)}, s32[4]{0:T(128)}, u32[]{:S(2)}) copy-start(s32[4]{0:T(128)} %constant.56.clone) | copy-start | bytes 52
  11.3 23.9 %collective-permute-start.3 = (bf16[4,2,64,1024]{3,2,1,0:T(8,128)(2,1)}, bf16[4,2,64,1024]{3,2,1,0:T(8,128)(2,1)}, u32[]{:S(2)}, u32[]{:S(2)}) collective-permute-start(bf16[4,2,64,1024]{3,2,1,0:T(8,128)(2,1)} %get-tuple-element.29), channel_id=1, source_target_pairs={{0,4},{4,8},{8,12},{12,16},{16,20},{20,24},{24,28},{28,32},{32,36}... | collective-permute-start | bytes 3145736 | tf_op jit(solution)/shard_map/ppermute | solution.py:24
  11.3 17.7 %collective-permute-start.4 = (bf16[4,2,64,1024]{3,2,1,0:T(8,128)(2,1)}, bf16[4,2,64,1024]{3,2,1,0:T(8,128)(2,1)S(1)}, u32[]{:S(2)}, u32[]{:S(2)}) collective-permute-start(bf16[4,2,64,1024]{3,2,1,0:T(8,128)(2,1)} %get-tuple-element.30), channel_id=1, source_target_pairs={{0,252},{4,0},{8,4},{12,8},{16,12},{20,16},{24,20},{28,24},{32,28}... | collective-permute-start | bytes 3145736 | tf_op jit(solution)/shard_map/ppermute | solution.py:24
  16.6 31.5 %collective-permute-start.2 = (bf16[4,2,64,1024]{3,2,1,0:T(8,128)(2,1)}, bf16[4,2,64,1024]{3,2,1,0:T(8,128)(2,1)}, u32[]{:S(2)}, u32[]{:S(2)}) collective-permute-start(bf16[4,2,64,1024]{3,2,1,0:T(8,128)(2,1)} %get-tuple-element.28), channel_id=1, source_target_pairs={{0,252},{4,0},{8,4},{12,8},{16,12},{20,16},{24,20},{28,24},{32,28}... | collective-permute-start | bytes 3145736 | tf_op jit(solution)/shard_map/ppermute | solution.py:24
  16.6 36.4 %collective-permute-start.1 = (bf16[4,2,64,1024]{3,2,1,0:T(8,128)(2,1)}, bf16[4,2,64,1024]{3,2,1,0:T(8,128)(2,1)S(1)}, u32[]{:S(2)}, u32[]{:S(2)}) collective-permute-start(bf16[4,2,64,1024]{3,2,1,0:T(8,128)(2,1)} %get-tuple-element.27), channel_id=1, source_target_pairs={{0,4},{4,8},{8,12},{12,16},{16,20},{20,24},{24,28},{28,32},{32,36}... | collective-permute-start | bytes 3145736 | tf_op jit(solution)/shard_map/ppermute | solution.py:24
  18.0 40.0 %all-to-all-start.1 = ((s32[64,16,128]{2,1,0:T(8,128)}), s32[64,16,128]{2,1,0:T(8,128)S(1)}, u32[]{:S(2)}, u32[]{:S(2)}) async-start(s32[64,16,128]{2,1,0:T(8,128)} %broadcast_in_dim.11), calls=%async_computation.1 | async-start | bytes 1048576 | tf_op jit(solution)/shard_map/all_to_all | solution.py:199
  29.0 2.2 %copy-start.1 = (bf16[4,2,128,2048]{3,2,1,0:T(8,128)(2,1)S(1)}, bf16[4,2,128,2048]{3,2,1,0:T(8,128)(2,1)}, u32[]{:S(2)}) copy-start(bf16[4,2,128,2048]{3,2,1,0:T(8,128)(2,1)} %own.7) | copy-start | bytes 12582916
  81.6 4.7 %collective-permute-start.7 = (f32[8,256]{1,0:T(8,128)S(1)}, f32[8,256]{1,0:T(8,128)S(1)}, u32[]{:S(2)}, u32[]{:S(2)}) collective-permute-start(f32[8,256]{1,0:T(8,128)S(1)} %get-tuple-element.40), channel_id=1, source_target_pairs={{0,3},{1,0},{2,1},{3,2},{4,7},{5,4},{6,5},{7,6},{8,11},{9,8},{10,9... | collective-permute-start | bytes 24584 | tf_op jit(solution)/shard_map/ppermute | solution.py:24
  84.7 5.2 %collective-permute-start.6 = (f32[8,256]{1,0:T(8,128)S(1)}, f32[8,256]{1,0:T(8,128)S(1)}, u32[]{:S(2)}, u32[]{:S(2)}) collective-permute-start(f32[8,256]{1,0:T(8,128)S(1)} %get-tuple-element.40), channel_id=1, source_target_pairs={{0,2},{1,3},{2,0},{3,1},{4,6},{5,7},{6,4},{7,5},{8,10},{9,11},{10,... | collective-permute-start | bytes 24584 | tf_op jit(solution)/shard_map/ppermute | solution.py:24
  85.3 4.9 %collective-permute-start.5 = (f32[8,256]{1,0:T(8,128)S(1)}, f32[8,256]{1,0:T(8,128)S(1)}, u32[]{:S(2)}, u32[]{:S(2)}) collective-permute-start(f32[8,256]{1,0:T(8,128)S(1)} %get-tuple-element.40), channel_id=1, source_target_pairs={{0,1},{1,2},{2,3},{3,0},{4,5},{5,6},{6,7},{7,4},{8,9},{9,10},{10,1... | collective-permute-start | bytes 24584 | tf_op jit(solution)/shard_map/ppermute | solution.py:24

commit v5 on v0

v5 whole, which is shorter than its diff:
```python
from functools import partial
import math

import jax
import jax.numpy as jnp
from jax import lax
from jax.experimental import pallas as pl
from jax.experimental.pallas import tpu as pltpu
from jax.sharding import PartitionSpec as P

LOOK_R = 4
LOOK_C = 16
TWO_PI = 2.0 * math.pi
CODES = 32767.0 / TWO_PI
CHUNKS = ((0, 1536), (1536, 2048))
STEP = 512
MESSAGE = 8
LANES = 128


def passed_along(value, axis, steps):
    count = lax.axis_size(axis)
    pairs = [(source, (source + steps) % count) for source in range(count)]
    return lax.ppermute(value, axis, pairs)


def phase_kernel(first_col, last, combos, own, following, previous, high_cycles, low_cycles, line, *rest):
    payload, sums, images, high, low, looked, picked, cycles, words = rest[-9:]
    group, _, rows, _ = following.shape
    _, width, _ = picked.shape
    looks = rows // LOOK_R
    pair_count = group * group
    step_cols = width // LOOK_C
    tiles = width // LANES
    cols = last - first_col
    steps = cols // step_cols
    if len(rest) == 9:
        sums[...] = jnp.zeros_like(sums)
    else:
        payload[...] = rest[0][...]
        sums[...] = rest[1][...]
    cycles[0] = TWO_PI * high_cycles[:, :looks, :].astype(jnp.float32).reshape(cycles.shape[1:])
    cycles[1] = TWO_PI * low_cycles[...].astype(jnp.float32).reshape(cycles.shape[1:])
    for step in range(steps):
        shape = picked.shape[1:]
        of = lax.broadcasted_iota(jnp.int32, shape, 0) // LOOK_C + first_col + step * step_cols
        chosen = of == lax.broadcasted_iota(jnp.int32, shape, 1)
        picked[step] = jnp.where(chosen, 1.0, 0.0).astype(jnp.bfloat16)

    def widen(source, start, row, col):
        @pl.loop(0, 2 * group)
        def _(index):
            date, part = index // 2, index % 2
            for tile in range(tiles):
                lanes = pl.ds(pl.multiple_of(col + tile * LANES, LANES), LANES)
                images[start + date, part, tile] = source[date, part, pl.ds(row, rows), lanes].astype(jnp.float32)

    @pl.loop(0, 2 * steps)
    def _(index):
        half, step_at = index // steps, index % steps
        widen(own, half * group, pl.multiple_of(half * rows, rows), step_at * width)

        @pl.when(half == 0)
        def _():
            widen(following, group, 0, step_at * width)

        @pl.when(half == 1)
        def _():
            widen(previous, 0, 0, step_at * width)

        @pl.loop(0, tiles)
        def _(tile):
            lanes = pl.ds(pl.multiple_of(tile * LANES, LANES), LANES)
            for date in range(0, group, 2):
                totals = {}
                for block in range(looks // 8):
                    for step in range(LOOK_R):
                        at = pl.ds(block * 8 * LOOK_R + step, 8, stride=LOOK_R)
                        seen = {
                            image: [images[image, part, tile, at, :] for part in range(2)]
                            for image in range(date, date + group + 2)
                        }
                        for first in range(date, date + 2):
                            a0, a1 = seen[first]
                            for gap in range(group):
                                b0, b1 = seen[first + gap + 1]
                                re, im = a0 * b0 + a1 * b1, a1 * b0 - a0 * b1
                                for part, value in enumerate((re, im)):
                                    key = first, gap, part, block
                                    totals[key] = totals[key] + value if key in totals else value
                for first in range(date, date + 2):
                    for gap in range(group):
                        for part in range(2):
                            value = jnp.concatenate(
                                [totals[first, gap, part, block] for block in range(looks // 8)], axis=0
                            )
                            head = value.astype(jnp.bfloat16)
                            tail = (value - head.astype(jnp.float32)).astype(jnp.bfloat16)
                            start = (part * pair_count + first * group + gap) * looks
                            high[start : start + looks, lanes] = head
                            low[start : start + looks, lanes] = tail

        summed = jnp.dot(high[...], picked[step_at], preferred_element_type=jnp.float32)
        summed += jnp.dot(low[...], picked[step_at], preferred_element_type=jnp.float32)

        @pl.when(step_at == 0)
        def _():
            looked[half] = summed

        @pl.when(step_at > 0)
        def _():
            looked[half] += summed

    @pl.loop(0, 2)
    def _(half):
        taken = []
        for part in range(2):
            for pair in range(pair_count):
                start = (part * pair_count + combos[half * pair_count + pair]) * looks
                taken.append(looked[half, pl.ds(pl.multiple_of(start, 8), looks), :])
        real = jnp.concatenate(taken[:pair_count], axis=0)
        imag = jnp.concatenate(taken[pair_count:], axis=0)
        imag = jnp.where(imag == 0.0, 0.0, imag)
        phase = jnp.arctan2(imag, real) - cycles[half]
        codes = jnp.round((phase + math.pi) * CODES).T[first_col:last]
        total = jnp.sum(codes, axis=0, keepdims=True).astype(jnp.int32)
        codes = codes.astype(jnp.int32)
        for octet in range(2):
            sums[pl.ds(2 * half + octet, 1), :] += total[:, octet * LANES : (octet + 1) * LANES]
        words[...] = (codes[:, :LANES] << 16) | (codes[:, LANES:] & 0xFFFF)
        for col in range(2):
            place = pl.ds(first_col // 2 * MESSAGE + 2 * col + half, cols // 2, stride=MESSAGE)
            payload[place, :] = words[pl.ds(col, cols // 2, stride=2), :]

    if last * MESSAGE // 2 == payload.shape[0]:

        total = sums[...]
        for step in (8, 4, 2, 1):
            total += pltpu.roll(total, LANES - step, 1)
        lane = lax.broadcasted_iota(jnp.int32, (1, LANES), 1) % looks
        full = line[0:1, :]
        for row in range(4):
            moved = pltpu.roll(total, row, 1)[row : row + 1]
            full = jnp.where(lane == row, moved, full)
        count = payload.shape[0] // MESSAGE
        payload[pl.ds(4, count, stride=MESSAGE), :] = jnp.broadcast_to(full, (count, LANES))


def phases(start, stop, combos, own, following, previous, high_cycles, low_cycles, line, earlier):
    group, _, height, _ = own.shape
    rows = height // 2
    looked_cols = low_cycles.shape[2]
    payload_shape = (looked_cols // 2 * MESSAGE, LANES)
    looks = rows // LOOK_R
    tiles = STEP // LANES
    pair_count = group * group
    steps = (stop - start) // STEP
    vmem = pl.BlockSpec(memory_space=pltpu.VMEM)
    return pl.pallas_call(
        partial(phase_kernel, start // LOOK_C, stop // LOOK_C),
        in_specs=[pl.BlockSpec(memory_space=pltpu.SMEM)] + [vmem] * (6 + len(earlier)),
        out_specs=[vmem] * 2,
        out_shape=[
            jax.ShapeDtypeStruct(payload_shape, jnp.int32),
            jax.ShapeDtypeStruct((8, LANES), jnp.int32),
        ],
        scratch_shapes=[
            pltpu.VMEM((2 * group, 2, tiles, rows, LANES), jnp.float32),
            pltpu.VMEM((2 * pair_count * looks, STEP), jnp.bfloat16),
            pltpu.VMEM((2 * pair_count * looks, STEP), jnp.bfloat16),
            pltpu.VMEM((2, 2 * pair_count * looks, looked_cols), jnp.float32),
            pltpu.VMEM((steps, STEP, looked_cols), jnp.bfloat16),
            pltpu.VMEM((2, pair_count * looks, looked_cols), jnp.float32),
            pltpu.VMEM(((stop - start) // LOOK_C, LANES), jnp.int32),
        ],
        compiler_params=pltpu.CompilerParams(vmem_limit_bytes=16 << 20),
        cost_estimate=pl.CostEstimate(
            flops=8 * pair_count * height * (stop - start),
            bytes_accessed=group * 4 * height * (stop - start) * 2,
            transcendentals=0,
        ),
        name="phases",
    )(combos, own, following, previous, high_cycles, low_cycles, line, *earlier)


def coded_inverse(inverse):
    turned = inverse.T
    peak = jnp.max(jnp.abs(turned), axis=1, keepdims=True)
    exponent = jnp.clip(jnp.floor(jnp.log2(peak)) + 1.0, -100.0, 100.0)
    codes = jnp.round(turned * jnp.exp2(-exponent) * 32767.0).astype(jnp.int32)
    words = (codes[:, :LANES] << 16) | (codes[:, LANES:] & 0xFFFF)
    return words, exponent[:, 0].astype(jnp.int32)


def exponent_line(exponent):
    spread = exponent.reshape(2, -1).T
    spread = jnp.pad(spread, ((0, 0), (4, LANES // spread.shape[0] - 6)))
    return jnp.broadcast_to(spread.reshape(1, LANES), (8, LANES))


def sent_inverse(words):
    devices = lax.axis_size("date")
    per = words.shape[0] // 2
    sent = jnp.broadcast_to(words.reshape(1, 2, per, LANES), (devices // 2, 2, per, LANES))
    got = lax.all_to_all(
        sent.reshape(devices, per, LANES), "date", split_axis=0, concat_axis=0, tiled=True
    ).reshape(-1, LANES)
    return got


def unpack_kernel(side, kept, swapped, right):
    pair_count = 16
    per = pair_count // 2
    sources = kept.shape[0] // per
    for at in range(per):
        for owner, source in ((side[0], kept), (1 - side[0], swapped)):
            words = source[pl.ds(at, sources, stride=per), :]
            place = pl.ds(pl.multiple_of((owner * per + at) * sources, 8), sources)
            right[place, :LANES] = (words >> 16).astype(jnp.float32)
            right[place, LANES:] = ((words << 16) >> 16).astype(jnp.float32)


def unpacked(kept, swapped):
    vmem = pl.BlockSpec(memory_space=pltpu.VMEM)
    return pl.pallas_call(
        unpack_kernel,
        in_specs=[pl.BlockSpec(memory_space=pltpu.SMEM), vmem, vmem],
        out_specs=vmem,
        out_shape=jax.ShapeDtypeStruct((2 * kept.shape[0], 2 * LANES), jnp.float32),
        name="unpack",
    )((lax.axis_index("date") % 2).reshape(1), kept, swapped)


def invert_kernel(band_pixels, received, right, out, bias, left):
    pair_count = 16
    sources = right.shape[0] // pair_count
    looks = LANES * 2 // pair_count
    pixels = out.shape[0]

    def aligned(words, half):
        value = words.astype(jnp.float32)
        return (pltpu.roll(value, sources - 1, 0) if half else value).T

    line = received[pl.ds(4, sources, stride=MESSAGE), :]
    lines = aligned(line, 0), aligned(line, 1)
    scales = []
    for pair in range(pair_count):
        octet, at = pair // 8, pair % 8 * looks
        scales.append(jnp.exp2(lines[0][at + 4 + octet : at + 5 + octet]) * (1.0 / 32767.0))
        total = lines[0][at + octet : at + octet + 1] + lines[1][at + 2 + octet : at + 3 + octet]
        left[pixels:, pair * sources : (pair + 1) * sources] = jnp.broadcast_to(
            total * scales[pair], (left.shape[0] - pixels, sources)
        )
    for half in range(2):
        for col in range(pixels // (2 * looks)):
            words = received[pl.ds(col * 2 + half, sources, stride=MESSAGE), :]
            for octet, value in enumerate((words >> 16, (words << 16) >> 16)):
                turned = aligned(value, half)
                for at in range(8):
                    pair = octet * 8 + at
                    row = (col * 2 + half) * looks
                    left[row : row + looks, pair * sources : (pair + 1) * sources] = (
                        turned[at * looks : (at + 1) * looks] * scales[pair]
                    )
    product = jnp.dot(
        left[...], right[...], precision=lax.Precision.HIGHEST, preferred_element_type=jnp.float32
    )
    out[...] = product[:pixels] * (1.0 / CODES)
    bias[...] = product[pixels:] * (1.0 / (CODES * band_pixels))


def invert(received, codes, pixels, band_pixels):
    total_pairs, dates = codes.shape
    vmem = pl.BlockSpec(memory_space=pltpu.VMEM)
    return pl.pallas_call(
        partial(invert_kernel, band_pixels),
        in_specs=[vmem] * 2,
        out_specs=[vmem] * 2,
        out_shape=[
            jax.ShapeDtypeStruct((pixels, dates), jnp.float32),
            jax.ShapeDtypeStruct((8, dates), jnp.float32),
        ],
        scratch_shapes=[pltpu.VMEM((pixels + 8, total_pairs), jnp.float32)],
        compiler_params=pltpu.CompilerParams(vmem_limit_bytes=24 << 20),
        name="invert",
    )(received, codes)


def body(acquisitions, date_pairs, cycle_maps, inverse):
    group, _, height, width = acquisitions.shape
    devices = lax.axis_size("date")
    total_dates = group * devices
    pair_count, look_rows, look_cols = cycle_maps.shape
    rows = height // 2
    half = look_rows // 2
    me = lax.axis_index("date")

    def parts(images, start, stop):
        return images[:, :, :rows, start:stop], images[:, :, rows:, start:stop]

    def exchanged(pair):
        return passed_along(pair[0], "date", -1), passed_along(pair[1], "date", 1)

    gaps = (date_pairs[:, 1] - date_pairs[:, 0] + total_dates) % total_dates
    combos = (date_pairs[:, 0] - me * group) * group + gaps - 1
    low_combos = passed_along(combos, "date", 1)
    low_cycles = passed_along(cycle_maps[:, half:].astype(jnp.bfloat16), "date", 1)
    left, others = acquisitions, []
    for start, stop in CHUNKS:
        sent, left, low_combos, low_cycles, inverse = lax.optimization_barrier(
            (parts(left, start, stop), left, low_combos, low_cycles, inverse)
        )
        others.append(exchanged(sent))

    words, exponent = coded_inverse(inverse)
    line = exponent_line(exponent)
    kept = sent_inverse(words)

    combos = jnp.concatenate([combos, low_combos])
    owned = [acquisitions[:, :, :, start:stop] for start, stop in CHUNKS]
    owned, combos = lax.optimization_barrier((owned, combos))
    earlier = ()
    for (start, stop), own, (following, previous) in zip(CHUNKS, owned, others):
        blank = jnp.zeros_like(line) if stop < width else line
        earlier = phases(
            start, stop, combos, own, following, previous, cycle_maps, low_cycles, blank, earlier
        )

    payload, kept = lax.optimization_barrier((earlier[0], kept))
    swapped = lax.ppermute(kept, "date", [(at, at ^ 1) for at in range(devices)])
    codes = unpacked(kept, swapped)
    received = lax.all_to_all(
        payload.reshape(devices, MESSAGE, LANES), "date", split_axis=0, concat_axis=0, tiled=True
    ).reshape(payload.shape)
    out_cols = look_cols // devices
    row_count = lax.axis_size("row")
    result, bias = invert(received, codes, out_cols * look_rows, look_rows * look_cols * row_count)
    for step in range(1, row_count):
        result = result - passed_along(bias, "row", step)[:1]
    result = result - bias[:1]
    return result.reshape(out_cols, look_rows, total_dates)


def solution(mesh):
    return jax.shard_map(
        body,
        mesh=mesh,
        in_specs=(
            P("date", None, "row", None),
            P("date", None),
            P("date", "row", None),
            P(None, "date"),
        ),
        out_specs=P("date", "row", None),
        check_vma=False,
    )
```

time: 394 us -> 85.7 us (0.22)
  waiting for transfers between devices: 185 us -> 14 us
  other arithmetic: 69.1 us -> 2.62 us
  loops' own time: 58.2 us -> 0 us
  starting transfers between devices: 5.56 us -> 34.2 us
  Pallas kernels: 0 us -> 20.7 us
  matrix products: 19.4 us -> 0 us
  local copies, waits for them, and re-layouts: 30.6 us -> 13.6 us
  between operations: 13.4 us -> 0.13 us
  blocking collectives: 10.7 us -> 0 us
    reduce_scatter x1 -> x0, waiting for transfers between devices: 139 us -> none  [body(): result = lax.psum_scatter(product, 'date', scatter_dimension=0, tiled=True)]
    another operation x1 -> x0, loops' own time: 58.2 us -> none  [body(): wrapped = lax.map(partial(form_pair, extended, column_sums), local_pairs)]
    ppermute x1 -> x9, waiting for transfers between devices: 45.5 us -> 5.57 us  [passed_along(): return lax.ppermute(value, axis, pairs)]
    convert_element_type x16 -> x1, other arithmetic: 33 us -> 0.08 us  [coded_inverse(): codes = jnp.round(turned * jnp.exp2(-exponent) * 32767.0).astype(jnp.int32)]
    reduce_sum x33 -> x0, other arithmetic: 21.4 us -> none  [the longest x16 10.1 us: form_pair(): real_rows = real_part.reshape(height // LOOK_R, LOOK_R, width).sum(axis=1)]
    all_to_all x0 -> x2, starting transfers between devices: none -> 21.2 us  [the longest x1 10.9 us: sent_inverse(): lax.all_to_all(sent.reshape(devices, per, LANES), 'date', split_axis=0, c...]
    pallas_call x0 -> x4, Pallas kernels: none -> 20.7 us  [the longest x2 17.6 us: phases(): pl.pallas_call(partial(phase_kernel, start // LOOK_C, stop // LOOK_C), in...]
    dot_general x17 -> x0, matrix products: 19.4 us -> none  [the longest x16 14.4 us: form_pair(): jnp.dot(stacked, column_sums, precision=lax.Precision.HIGHEST, preferred_...]
  transfers between devices with their start and end apart: 2 -> 12, of which waited for: 2 -> 5; matrix products, arithmetic and copies ran while one was open for 0% -> 15% of each run, Pallas kernels for 0% -> 23%
where the time goes in v5:
time: 85.7 us; the launch traced here: 85.3 us
  starting transfers between devices  34.2 us (40%)
  Pallas kernels  20.7 us (24%)
  waiting for transfers between devices  14 us (16%)
  local copies, waits for them, and re-layouts  13.6 us (16%)
  other arithmetic  2.62 us (3%)
    pallas_call x2, Pallas kernels, phases(): pl.pallas_call(partial(phase_kernel, start // LOOK_C, stop // LOOK_C), in...  17.6 us
    ppermute x9, starting transfers between devices, passed_along(): return lax.ppermute(value, axis, pairs)  12.7 us
    all_to_all x1, starting transfers between devices, sent_inverse(): lax.all_to_all(sent.reshape(devices, per, LANES), 'date', split_axis=0, c...  10.9 us
    all_to_all x1, starting transfers between devices, body(): lax.all_to_all(payload.reshape(devices, MESSAGE, LANES), 'date', split_ax...  10.3 us
    all_to_all x1, waiting for transfers between devices, body(): lax.all_to_all(payload.reshape(devices, MESSAGE, LANES), 'date', split_ax...  6.83 us
    slice x2, local copies, waits for them, and re-layouts, parts(): return (images[:, :, :rows, start:stop], images[:, :, rows:, start:stop])  6.18 us
    ppermute x9, waiting for transfers between devices, passed_along(): return lax.ppermute(value, axis, pairs)  5.57 us
    slice x2, local copies, waits for them, and re-layouts, body(): owned = [acquisitions[:, :, :, start:stop] for start, stop in CHUNKS]  4.41 us
  transfers between devices with their start and end apart: 12, of which 5 were waited for; matrix products, arithmetic and copies ran while one was open for 15% of the time, Pallas kernels for 23%

profile of v5, /device:TPU:6, one launch (start us, length us, event | category | flops | bytes accessed | tf_op | source)
XLA Modules:
  0.0 85.3 jit_solution(5473652691807565382)
XLA Ops:
  0.0 0.8 fusion.4
  0.8 0.1 collective-permute-start
  0.9 0.9 %slice_convert_fusion = bf16[16,16,128]{2,1,0:T(8,128)(2,1)S(1)} fusion(s32[16,32,128]{2,1,0:T(8,128)} %high_cycles.3), kind=kLoop, calls=%fused_computation | loop fusion | flops 32768 | bytes 196608 | tf_op jit(solution)/shard_map/convert
  1.8 2.1 %collective-permute-start.1 = (bf16[16,16,128]{2,1,0:T(8,128)(2,1)S(1)}, bf16[16,16,128]{2,1,0:T(8,128)(2,1)S(1)}, u32[]{:S(2)}, u32[]{:S(2)}) collective-permute-start(bf16[16,16,128]{2,1,0:T(8,128)(2,1)S(1)} %slice_convert_fusion), channel_id=1, source_target_pairs={{0,4},{4,8},{8,12},{12,16},{16,20},{20,24},{24,28},{28,32},{32,36}... | collective-permute-start | bytes 196616 | tf_op jit(solution)/shard_map/ppermute | solution.py:24
  3.9 3.8 %fusion.7 = (bf16[4,2,64,1536]{3,2,1,0:T(8,128)(2,1)}, bf16[4,2,64,1536]{3,2,1,0:T(8,128)(2,1)}) fusion(bf16[4,2,128,2048]{3,2,1,0:T(8,128)(2,1)} %param.4), kind=kLoop, calls=%fused_computation.19 | loop fusion | bytes 6291456 | tf_op jit(solution)/shard_map/slice | solution.py:299
  7.7 0.0 collective-permute-done
  7.7 1.7 %collective-permute-done.1.low_cycles = bf16[16,16,128]{2,1,0:T(8,128)(2,1)S(1)} collective-permute-done((bf16[16,16,128]{2,1,0:T(8,128)(2,1)S(1)}, bf16[16,16,128]{2,1,0:T(8,128)(2,1)S(1)}, u32[]{:S(2)}, u32[]{:S(2)}) %collective-permute-start.1) | collective-permute-done | bytes 65568 | tf_op jit(solution)/shard_map/ppermute | solution.py:24
  9.4 2.0 %collective-permute-start.4 = (bf16[4,2,64,1536]{3,2,1,0:T(8,128)(2,1)}, bf16[4,2,64,1536]{3,2,1,0:T(8,128)(2,1)}, u32[]{:S(2)}, u32[]{:S(2)}) collective-permute-start(bf16[4,2,64,1536]{3,2,1,0:T(8,128)(2,1)} %get-tuple-element.38), channel_id=1, source_target_pairs={{0,252},{4,0},{8,4},{12,8},{16,12},{20,16},{24,20},{28,24},{32,28}... | collective-permute-start | bytes 4718600 | tf_op jit(solution)/shard_map/ppermute | solution.py:24
  11.3 0.0 collective-permute-start.5
  11.4 2.4 %fusion.6 = (bf16[4,2,64,512]{3,2,1,0:T(8,128)(2,1)}, bf16[4,2,64,512]{3,2,1,0:T(8,128)(2,1)}) fusion(bf16[4,2,128,2048]{3,2,1,0:T(8,128)(2,1)} %param.4), kind=kLoop, calls=%fused_computation.18 | loop fusion | bytes 2097152 | tf_op jit(solution)/shard_map/slice | solution.py:299
  13.7 3.9 %collective-permute-start.2 = (bf16[4,2,64,512]{3,2,1,0:T(8,128)(2,1)}, bf16[4,2,64,512]{3,2,1,0:T(8,128)(2,1)}, u32[]{:S(2)}, u32[]{:S(2)}) collective-permute-start(bf16[4,2,64,512]{3,2,1,0:T(8,128)(2,1)} %get-tuple-element.33), channel_id=1, source_target_pairs={{0,252},{4,0},{8,4},{12,8},{16,12},{20,16},{24,20},{28,24},{32,28}... | collective-permute-start | bytes 1572872 | tf_op jit(solution)/shard_map/ppermute | solution.py:24
  17.6 0.0 collective-permute-start.3
  17.6 0.0 copy-done.4
  17.6 0.1 abs_reduce_fusion
  17.7 0.1 convert_bitcast_fusion
  17.8 0.7 broadcast_in_dim.22
  18.5 10.9 %all-to-all-start = ((s32[64,8,128]{2,1,0:T(8,128)}), s32[64,8,128]{2,1,0:T(8,128)}, u32[]{:S(2)}, u32[]{:S(2)}) async-start(s32[64,8,128]{2,1,0:T(8,128)} %bitcast.5), calls=%async_computation | async-start | bytes 524288 | tf_op jit(solution)/shard_map/all_to_all | solution.py:205
  29.4 2.1 %slice.47.own = bf16[4,2,128,1536]{3,2,1,0:T(8,128)(2,1)S(1)} slice(bf16[4,2,128,2048]{3,2,1,0:T(8,128)(2,1)} %param.4), slice={[0:4], [0:2], [0:128], [0:1536]} | slice | bytes 6291456 | tf_op jit(solution)/shard_map/slice | solution.py:320
  31.5 0.0 copy-start.2
  31.5 2.3 %slice.48.own = bf16[4,2,128,512]{3,2,1,0:T(8,128)(2,1)} slice(bf16[4,2,128,2048]{3,2,1,0:T(8,128)(2,1)} %param.4), slice={[0:4], [0:2], [0:128], [1536:2048]} | slice | bytes 2097152 | tf_op jit(solution)/shard_map/slice | solution.py:320
  33.9 0.1 pad_add_fusion.combos
  33.9 0.1 reshape.65
  34.0 0.1 copy.6
  34.1 0.1 pad.4.clone
  34.2 0.1 broadcast_in_dim.18
  34.3 0.0 collective-permute-done.4.following
  34.3 0.0 collective-permute-done.5.previous
  34.3 0.0 copy-done.2
  34.3 11.7 %phases.2 = (s32[512,128]{1,0:T(8,128)S(1)}, s32[8,128]{1,0:T(8,128)S(1)}) custom-call(s32[32]{0:T(128)S(1)} %pad_add_fusion.combos, bf16[4,2,128,1536]{3,2,1,0:T(8,128)(2,1)S(1)} %slice.47.own, bf16[4,2,64,1536]{3,2,1,0:T(8,128)(2,1)} %collective-permute-done.4.following, bf16[4,2,64,1536]{3,2,1,0:T(8,128)(2,1)} %collective-permute-done.5.previous, ...), custom_call_target="tpu_custom_call" | custom-call | flops 25165824 | bytes 6291456 | tf_op jit(solution)/shard_map/phases/pallas_call | solution.py:159
  46.0 0.0 collective-permute-done.2.following
  46.0 0.0 collective-permute-done.3.previous
  46.0 5.9 %phases.3 = (s32[512,128]{1,0:T(8,128)}, s32[8,128]{1,0:T(8,128)}) custom-call(s32[32]{0:T(128)S(1)} %pad_add_fusion.combos, bf16[4,2,128,512]{3,2,1,0:T(8,128)(2,1)S(1)} %copy-done.1, bf16[4,2,64,512]{3,2,1,0:T(8,128)(2,1)} %collective-permute-done.2.following, bf16[4,2,64,512]{3,2,1,0:T(8,128)(2,1)} %collective-permute-done.3.previous, ...), custom_call_target="tpu_custom_call" | custom-call | flops 8388608 | bytes 2097152 | tf_op jit(solution)/shard_map/phases/pallas_call | solution.py:159
  52.0 0.0 all-to-all-done
  52.0 10.3 %all-to-all-start.1 = ((s32[64,8,128]{2,1,0:T(8,128)}), s32[64,8,128]{2,1,0:T(8,128)S(1)}, u32[]{:S(2)}, u32[]{:S(2)}) async-start(s32[64,8,128]{2,1,0:T(8,128)} %bitcast.7), calls=%async_computation.1 | async-start | bytes 524288 | tf_op jit(solution)/shard_map/all_to_all | solution.py:332
  62.3 0.2 collective-permute-start.6
  62.5 1.6 %collective-permute-done.6.swapped = s32[512,128]{1,0:T(8,128)S(1)} collective-permute-done((s32[512,128]{1,0:T(8,128)}, s32[512,128]{1,0:T(8,128)S(1)}, u32[]{:S(2)}, u32[]{:S(2)}) %collective-permute-start.6) | collective-permute-done | bytes 262176 | tf_op jit(solution)/shard_map/ppermute | solution.py:330
  64.1 0.7 copy-done.3
  64.8 2.2 %unpack.1.right = f32[1024,256]{1,0:T(8,128)} custom-call(s32[1]{0:T(128)} %bitcast.9.side, s32[512,128]{1,0:T(8,128)} %bitcast.6.kept, s32[512,128]{1,0:T(8,128)} %copy-done.3), custom_call_target="tpu_custom_call" | custom-call | tf_op jit(solution)/shard_map/unpack/pallas_call | solution.py:225
  67.0 6.8 %all-to-all-done.1 = s32[64,8,128]{2,1,0:T(8,128)S(1)} async-done(((s32[64,8,128]{2,1,0:T(8,128)}), s32[64,8,128]{2,1,0:T(8,128)S(1)}, u32[]{:S(2)}, u32[]{:S(2)}) %all-to-all-start.1) | async-done | bytes 262176 | tf_op jit(solution)/shard_map/all_to_all | solution.py:332
  73.8 1.2 %copy-done = f32[1024,256]{1,0:T(8,128)S(1)} copy-done((f32[1024,256]{1,0:T(8,128)S(1)}, f32[1024,256]{1,0:T(8,128)}, u32[]{:S(2)}) %copy-start) | copy-done | bytes 1048600
  75.1 1.0 %invert.1 = (f32[64,256]{1,0:T(8,128)S(1)}, f32[8,256]{1,0:T(8,128)S(1)}) custom-call(s32[512,128]{1,0:T(8,128)S(1)} %bitcast.23, f32[1024,256]{1,0:T(8,128)S(1)} %copy-done), custom_call_target="tpu_custom_call" | custom-call | tf_op jit(solution)/shard_map/invert/pallas_call | solution.py:275
  76.0 3.1 %collective-permute-start.9 = (f32[8,256]{1,0:T(8,128)S(1)}, f32[8,256]{1,0:T(8,128)S(1)}, u32[]{:S(2)}, u32[]{:S(2)}) collective-permute-start(f32[8,256]{1,0:T(8,128)S(1)} %get-tuple-element.46), channel_id=1, source_target_pairs={{0,3},{1,0},{2,1},{3,2},{4,7},{5,4},{6,5},{7,6},{8,11},{9,8},{10,9... | collective-permute-start | bytes 24584 | tf_op jit(solution)/shard_map/ppermute | solution.py:24
  79.1 0.6 collective-permute-start.8
  79.7 1.0 %collective-permute-start.7 = (f32[8,256]{1,0:T(8,128)S(1)}, f32[8,256]{1,0:T(8,128)S(1)}, u32[]{:S(2)}, u32[]{:S(2)}) collective-permute-start(f32[8,256]{1,0:T(8,128)S(1)} %get-tuple-element.46), channel_id=1, source_target_pairs={{0,1},{1,2},{2,3},{3,0},{4,5},{5,6},{6,7},{7,4},{8,9},{9,10},{10,1... | collective-permute-start | bytes 24584 | tf_op jit(solution)/shard_map/ppermute | solution.py:24
  80.7 0.0 collective-permute-done.9
  80.7 3.5 %collective-permute-done.8 = f32[8,256]{1,0:T(8,128)S(1)} collective-permute-done((f32[8,256]{1,0:T(8,128)S(1)}, f32[8,256]{1,0:T(8,128)S(1)}, u32[]{:S(2)}, u32[]{:S(2)}) %collective-permute-start.8) | collective-permute-done | bytes 8224 | tf_op jit(solution)/shard_map/ppermute | solution.py:24
  84.3 0.3 collective-permute-done.7
  84.6 0.6 subtract_subtract_fusion
  (13 shorter events, 0.0 us)
Async XLA Ops:
  0.8 6.9 %collective-permute-start = (s32[16]{0:T(128)S(1)}, s32[16]{0:T(128)S(1)}, u32[]{:S(2)}, u32[]{:S(2)}) collective-permute-start(s32[16]{0:T(128)S(1)} %fusion.4), channel_id=1, source_target_pairs={{0,4},{4,8},{8,12},{12,16},{16,20},{20,24},{24,28},{28,32},{32,36}... | collective-permute-start | bytes 200 | tf_op jit(solution)/shard_map/ppermute | solution.py:24
  1.8 7.6 %collective-permute-start.1 = (bf16[16,16,128]{2,1,0:T(8,128)(2,1)S(1)}, bf16[16,16,128]{2,1,0:T(8,128)(2,1)S(1)}, u32[]{:S(2)}, u32[]{:S(2)}) collective-permute-start(bf16[16,16,128]{2,1,0:T(8,128)(2,1)S(1)} %slice_convert_fusion), channel_id=1, source_target_pairs={{0,4},{4,8},{8,12},{12,16},{16,20},{20,24},{24,28},{28,32},{32,36}... | collective-permute-start | bytes 196616 | tf_op jit(solution)/shard_map/ppermute | solution.py:24
  7.7 9.9 %copy-start.4 = (f32[256,16]{0,1:T(8,128)S(1)}, f32[256,16]{0,1:T(8,128)}, u32[]{:S(2)}) copy-start(f32[256,16]{0,1:T(8,128)} %param.7) | copy-start | bytes 49156
  9.4 24.9 %collective-permute-start.4 = (bf16[4,2,64,1536]{3,2,1,0:T(8,128)(2,1)}, bf16[4,2,64,1536]{3,2,1,0:T(8,128)(2,1)}, u32[]{:S(2)}, u32[]{:S(2)}) collective-permute-start(bf16[4,2,64,1536]{3,2,1,0:T(8,128)(2,1)} %get-tuple-element.38), channel_id=1, source_target_pairs={{0,252},{4,0},{8,4},{12,8},{16,12},{20,16},{24,20},{28,24},{32,28}... | collective-permute-start | bytes 4718600 | tf_op jit(solution)/shard_map/ppermute | solution.py:24
  11.3 22.9 %collective-permute-start.5 = (bf16[4,2,64,1536]{3,2,1,0:T(8,128)(2,1)}, bf16[4,2,64,1536]{3,2,1,0:T(8,128)(2,1)}, u32[]{:S(2)}, u32[]{:S(2)}) collective-permute-start(bf16[4,2,64,1536]{3,2,1,0:T(8,128)(2,1)} %get-tuple-element.39), channel_id=1, source_target_pairs={{0,4},{4,8},{8,12},{12,16},{16,20},{20,24},{24,28},{28,32},{32,36}... | collective-permute-start | bytes 4718600 | tf_op jit(solution)/shard_map/ppermute | solution.py:24
  13.7 32.3 %collective-permute-start.2 = (bf16[4,2,64,512]{3,2,1,0:T(8,128)(2,1)}, bf16[4,2,64,512]{3,2,1,0:T(8,128)(2,1)}, u32[]{:S(2)}, u32[]{:S(2)}) collective-permute-start(bf16[4,2,64,512]{3,2,1,0:T(8,128)(2,1)} %get-tuple-element.33), channel_id=1, source_target_pairs={{0,252},{4,0},{8,4},{12,8},{16,12},{20,16},{24,20},{28,24},{32,28}... | collective-permute-start | bytes 1572872 | tf_op jit(solution)/shard_map/ppermute | solution.py:24
  17.6 28.4 %collective-permute-start.3 = (bf16[4,2,64,512]{3,2,1,0:T(8,128)(2,1)}, bf16[4,2,64,512]{3,2,1,0:T(8,128)(2,1)}, u32[]{:S(2)}, u32[]{:S(2)}) collective-permute-start(bf16[4,2,64,512]{3,2,1,0:T(8,128)(2,1)} %get-tuple-element.34), channel_id=1, source_target_pairs={{0,4},{4,8},{8,12},{12,16},{16,20},{20,24},{24,28},{28,32},{32,36}... | collective-permute-start | bytes 1572872 | tf_op jit(solution)/shard_map/ppermute | solution.py:24
  18.5 33.4 %all-to-all-start = ((s32[64,8,128]{2,1,0:T(8,128)}), s32[64,8,128]{2,1,0:T(8,128)}, u32[]{:S(2)}, u32[]{:S(2)}) async-start(s32[64,8,128]{2,1,0:T(8,128)} %bitcast.5), calls=%async_computation | async-start | bytes 524288 | tf_op jit(solution)/shard_map/all_to_all | solution.py:205
  31.5 2.7 %copy-start.2 = (s32[16,32,128]{2,1,0:T(8,128)S(1)}, s32[16,32,128]{2,1,0:T(8,128)}, u32[]{:S(2)}) copy-start(s32[16,32,128]{2,1,0:T(8,128)} %high_cycles.3) | copy-start | bytes 786436
  34.3 11.7 %copy-start.1 = (bf16[4,2,128,512]{3,2,1,0:T(8,128)(2,1)S(1)}, bf16[4,2,128,512]{3,2,1,0:T(8,128)(2,1)}, u32[]{:S(2)}) copy-start(bf16[4,2,128,512]{3,2,1,0:T(8,128)(2,1)} %slice.48.own) | copy-start | bytes 3145732
  52.0 21.9 %all-to-all-start.1 = ((s32[64,8,128]{2,1,0:T(8,128)}), s32[64,8,128]{2,1,0:T(8,128)S(1)}, u32[]{:S(2)}, u32[]{:S(2)}) async-start(s32[64,8,128]{2,1,0:T(8,128)} %bitcast.7), calls=%async_computation.1 | async-start | bytes 524288 | tf_op jit(solution)/shard_map/all_to_all | solution.py:332
  62.3 1.8 %collective-permute-start.6 = (s32[512,128]{1,0:T(8,128)}, s32[512,128]{1,0:T(8,128)S(1)}, u32[]{:S(2)}, u32[]{:S(2)}) collective-permute-start(s32[512,128]{1,0:T(8,128)} %bitcast.6.kept), channel_id=1, source_target_pairs={{0,4},{4,0},{8,12},{12,8},{16,20},{20,16},{24,28},{28,24},{32,36},... | collective-permute-start | bytes 786440 | tf_op jit(solution)/shard_map/ppermute | solution.py:330
  64.1 0.7 copy-start.3
  73.8 1.2 %copy-start = (f32[1024,256]{1,0:T(8,128)S(1)}, f32[1024,256]{1,0:T(8,128)}, u32[]{:S(2)}) copy-start(f32[1024,256]{1,0:T(8,128)} %unpack.1.right) | copy-start | bytes 3145732
  76.0 4.7 %collective-permute-start.9 = (f32[8,256]{1,0:T(8,128)S(1)}, f32[8,256]{1,0:T(8,128)S(1)}, u32[]{:S(2)}, u32[]{:S(2)}) collective-permute-start(f32[8,256]{1,0:T(8,128)S(1)} %get-tuple-element.46), channel_id=1, source_target_pairs={{0,3},{1,0},{2,1},{3,2},{4,7},{5,4},{6,5},{7,6},{8,11},{9,8},{10,9... | collective-permute-start | bytes 24584 | tf_op jit(solution)/shard_map/ppermute | solution.py:24
  79.1 5.2 %collective-permute-start.8 = (f32[8,256]{1,0:T(8,128)S(1)}, f32[8,256]{1,0:T(8,128)S(1)}, u32[]{:S(2)}, u32[]{:S(2)}) collective-permute-start(f32[8,256]{1,0:T(8,128)S(1)} %get-tuple-element.46), channel_id=1, source_target_pairs={{0,2},{1,3},{2,0},{3,1},{4,6},{5,7},{6,4},{7,5},{8,10},{9,11},{10,... | collective-permute-start | bytes 24584 | tf_op jit(solution)/shard_map/ppermute | solution.py:24
  79.7 4.9 %collective-permute-start.7 = (f32[8,256]{1,0:T(8,128)S(1)}, f32[8,256]{1,0:T(8,128)S(1)}, u32[]{:S(2)}, u32[]{:S(2)}) collective-permute-start(f32[8,256]{1,0:T(8,128)S(1)} %get-tuple-element.46), channel_id=1, source_target_pairs={{0,1},{1,2},{2,3},{3,0},{4,5},{5,6},{6,7},{7,4},{8,9},{9,10},{10,1... | collective-permute-start | bytes 24584 | tf_op jit(solution)/shard_map/ppermute | solution.py:24

commit v6 on v5

--- a/solution.py
+++ b/solution.py
@@ -14,8 +14,18 @@
 CODES = 32767.0 / TWO_PI
 CHUNKS = ((0, 1536), (1536, 2048))
 STEP = 512
-MESSAGE = 8
+MESSAGE = 5
 LANES = 128
+ATAN = (
+    0.9999993329,
+    -0.3332985605,
+    0.1994653599,
+    -0.1390853351,
+    0.0964200441,
+    -0.0559098861,
+    0.0218612288,
+    -0.0040540580,
+)
 
 
 def passed_along(value, axis, steps):
@@ -24,23 +34,33 @@
     return lax.ppermute(value, axis, pairs)
 
 
-def phase_kernel(first_col, last, combos, own, following, previous, high_cycles, low_cycles, line, *rest):
-    payload, sums, images, high, low, looked, picked, cycles, words = rest[-9:]
+def arctan2(y, x):
+    wide, tall = jnp.abs(x), jnp.abs(y)
+    larger = jnp.maximum(wide, tall)
+    ratio = jnp.minimum(wide, tall) / jnp.where(larger == 0.0, 1.0, larger)
+    square = ratio * ratio
+    value = jnp.full_like(square, ATAN[-1])
+    for factor in ATAN[-2::-1]:
+        value = value * square + factor
+    value = value * ratio
+    value = jnp.where(tall > wide, 0.5 * math.pi - value, value)
+    value = jnp.where(x < 0.0, math.pi - value, value)
+    return jnp.where(y < 0.0, -value, value)
+
+
+def phase_kernel(first_col, last, final, own, following, previous, *refs):
+    refs = list(refs)
+    earlier = refs.pop(0) if first_col else None
+    if final:
+        combos, high_cycles, low_cycles, line, payload, images, high, low, picked, looked, cycles, sums, words = refs
+    else:
+        looked, images, high, low, picked = refs
     group, _, rows, _ = following.shape
-    _, width, _ = picked.shape
+    steps, width, _ = picked.shape
     looks = rows // LOOK_R
     pair_count = group * group
     step_cols = width // LOOK_C
     tiles = width // LANES
-    cols = last - first_col
-    steps = cols // step_cols
-    if len(rest) == 9:
-        sums[...] = jnp.zeros_like(sums)
-    else:
-        payload[...] = rest[0][...]
-        sums[...] = rest[1][...]
-    cycles[0] = TWO_PI * high_cycles[:, :looks, :].astype(jnp.float32).reshape(cycles.shape[1:])
-    cycles[1] = TWO_PI * low_cycles[...].astype(jnp.float32).reshape(cycles.shape[1:])
     for step in range(steps):
         shape = picked.shape[1:]
         of = lax.broadcasted_iota(jnp.int32, shape, 0) // LOOK_C + first_col + step * step_cols
@@ -58,7 +78,7 @@
     @pl.loop(0, 2 * steps)
     def _(index):
         half, step_at = index // steps, index % steps
-        widen(own, half * group, pl.multiple_of(half * rows, rows), step_at * width)
+        widen(own, half * group, pl.multiple_of(half * rows, rows), first_col * LOOK_C + step_at * width)
 
         @pl.when(half == 0)
         def _():
@@ -105,11 +125,16 @@
 
         @pl.when(step_at == 0)
         def _():
-            looked[half] = summed
+            looked[half] = summed if earlier is None else earlier[half] + summed
 
         @pl.when(step_at > 0)
         def _():
             looked[half] += summed
+
+    if not final:
+        return
+    cycles[0] = TWO_PI * high_cycles[:, :looks, :].astype(jnp.float32).reshape(cycles.shape[1:])
+    cycles[1] = TWO_PI * low_cycles[...].astype(jnp.float32).reshape(cycles.shape[1:])
 
     @pl.loop(0, 2)
     def _(half):
@@ -120,59 +145,60 @@
                 taken.append(looked[half, pl.ds(pl.multiple_of(start, 8), looks), :])
         real = jnp.concatenate(taken[:pair_count], axis=0)
         imag = jnp.concatenate(taken[pair_count:], axis=0)
-        imag = jnp.where(imag == 0.0, 0.0, imag)
-        phase = jnp.arctan2(imag, real) - cycles[half]
-        codes = jnp.round((phase + math.pi) * CODES).T[first_col:last]
+        codes = jnp.round((arctan2(imag, real) - cycles[half] + math.pi) * CODES).T
         total = jnp.sum(codes, axis=0, keepdims=True).astype(jnp.int32)
         codes = codes.astype(jnp.int32)
         for octet in range(2):
-            sums[pl.ds(2 * half + octet, 1), :] += total[:, octet * LANES : (octet + 1) * LANES]
+            sums[pl.ds(2 * half + octet, 1), :] = total[:, octet * LANES : (octet + 1) * LANES]
         words[...] = (codes[:, :LANES] << 16) | (codes[:, LANES:] & 0xFFFF)
+        count = last // 2
         for col in range(2):
-            place = pl.ds(first_col // 2 * MESSAGE + 2 * col + half, cols // 2, stride=MESSAGE)
-            payload[place, :] = words[pl.ds(col, cols // 2, stride=2), :]
-
-    if last * MESSAGE // 2 == payload.shape[0]:
-
-        total = sums[...]
-        for step in (8, 4, 2, 1):
-            total += pltpu.roll(total, LANES - step, 1)
-        lane = lax.broadcasted_iota(jnp.int32, (1, LANES), 1) % looks
-        full = line[0:1, :]
-        for row in range(4):
-            moved = pltpu.roll(total, row, 1)[row : row + 1]
-            full = jnp.where(lane == row, moved, full)
-        count = payload.shape[0] // MESSAGE
-        payload[pl.ds(4, count, stride=MESSAGE), :] = jnp.broadcast_to(full, (count, LANES))
-
-
-def phases(start, stop, combos, own, following, previous, high_cycles, low_cycles, line, earlier):
+            payload[pl.ds(2 * col + half, count, stride=MESSAGE), :] = words[pl.ds(col, count, stride=2), :]
+
+    total = sums[...]
+    for step in (8, 4, 2, 1):
+        total += pltpu.roll(total, LANES - step, 1)
+    lane = lax.broadcasted_iota(jnp.int32, (1, LANES), 1) % looks
+    full = line[0:1, :]
+    for row in range(4):
+        moved = pltpu.roll(total, row, 1)[row : row + 1]
+        full = jnp.where(lane == row, moved, full)
+    payload[pl.ds(4, last // 2, stride=MESSAGE), :] = jnp.broadcast_to(full, (last // 2, LANES))
+
+
+def phases(start, stop, final, own, following, previous, earlier, *rest):
     group, _, height, _ = own.shape
     rows = height // 2
-    looked_cols = low_cycles.shape[2]
-    payload_shape = (looked_cols // 2 * MESSAGE, LANES)
+    looked_cols = own.shape[3] // LOOK_C
     looks = rows // LOOK_R
     tiles = STEP // LANES
     pair_count = group * group
     steps = (stop - start) // STEP
     vmem = pl.BlockSpec(memory_space=pltpu.VMEM)
+    in_specs = [vmem] * (3 + len(earlier))
+    looked_shape = (2, 2 * pair_count * looks, looked_cols)
+    out_shape = jax.ShapeDtypeStruct(looked_shape, jnp.float32)
+    scratch = [
+        pltpu.VMEM((2 * group, 2, tiles, rows, LANES), jnp.float32),
+        pltpu.VMEM((2 * pair_count * looks, STEP), jnp.bfloat16),
+        pltpu.VMEM((2 * pair_count * looks, STEP), jnp.bfloat16),
+        pltpu.VMEM((steps, STEP, looked_cols), jnp.bfloat16),
+    ]
+    if final:
+        in_specs += [pl.BlockSpec(memory_space=pltpu.SMEM)] + [vmem] * 3
+        out_shape = jax.ShapeDtypeStruct((looked_cols // 2 * MESSAGE, LANES), jnp.int32)
+        scratch += [
+            pltpu.VMEM(looked_shape, jnp.float32),
+            pltpu.VMEM((2, pair_count * looks, looked_cols), jnp.float32),
+            pltpu.VMEM((8, LANES), jnp.int32),
+            pltpu.VMEM((looked_cols, LANES), jnp.int32),
+        ]
     return pl.pallas_call(
-        partial(phase_kernel, start // LOOK_C, stop // LOOK_C),
-        in_specs=[pl.BlockSpec(memory_space=pltpu.SMEM)] + [vmem] * (6 + len(earlier)),
-        out_specs=[vmem] * 2,
-        out_shape=[
-            jax.ShapeDtypeStruct(payload_shape, jnp.int32),
-            jax.ShapeDtypeStruct((8, LANES), jnp.int32),
-        ],
-        scratch_shapes=[
-            pltpu.VMEM((2 * group, 2, tiles, rows, LANES), jnp.float32),
-            pltpu.VMEM((2 * pair_count * looks, STEP), jnp.bfloat16),
-            pltpu.VMEM((2 * pair_count * looks, STEP), jnp.bfloat16),
-            pltpu.VMEM((2, 2 * pair_count * looks, looked_cols), jnp.float32),
-            pltpu.VMEM((steps, STEP, looked_cols), jnp.bfloat16),
-            pltpu.VMEM((2, pair_count * looks, looked_cols), jnp.float32),
-            pltpu.VMEM(((stop - start) // LOOK_C, LANES), jnp.int32),
-        ],
+        partial(phase_kernel, start // LOOK_C, stop // LOOK_C, final),
+        in_specs=in_specs,
+        out_specs=vmem,
+        out_shape=out_shape,
+        scratch_shapes=scratch,
         compiler_params=pltpu.CompilerParams(vmem_limit_bytes=16 << 20),
         cost_estimate=pl.CostEstimate(
             flops=8 * pair_count * height * (stop - start),
@@ -180,7 +206,7 @@
             transcendentals=0,
         ),
         name="phases",
-    )(combos, own, following, previous, high_cycles, low_cycles, line, *earlier)
+    )(own, following, previous, *earlier, *rest)
 
 
 def coded_inverse(inverse):
@@ -208,39 +234,23 @@
     return got
 
 
-def unpack_kernel(side, kept, swapped, right):
+def invert_kernel(band_pixels, side, received, kept, swapped, out, bias, left, right):
     pair_count = 16
     per = pair_count // 2
     sources = kept.shape[0] // per
+    looks = LANES * 2 // pair_count
+    pixels = out.shape[0]
+
+    def aligned(words, half):
+        value = words.astype(jnp.float32)
+        return (pltpu.roll(value, sources - 1, 0) if half else value).T
+
     for at in range(per):
         for owner, source in ((side[0], kept), (1 - side[0], swapped)):
             words = source[pl.ds(at, sources, stride=per), :]
             place = pl.ds(pl.multiple_of((owner * per + at) * sources, 8), sources)
             right[place, :LANES] = (words >> 16).astype(jnp.float32)
             right[place, LANES:] = ((words << 16) >> 16).astype(jnp.float32)
-
-
-def unpacked(kept, swapped):
-    vmem = pl.BlockSpec(memory_space=pltpu.VMEM)
-    return pl.pallas_call(
-        unpack_kernel,
-        in_specs=[pl.BlockSpec(memory_space=pltpu.SMEM), vmem, vmem],
-        out_specs=vmem,
-        out_shape=jax.ShapeDtypeStruct((2 * kept.shape[0], 2 * LANES), jnp.float32),
-        name="unpack",
-    )((lax.axis_index("date") % 2).reshape(1), kept, swapped)
-
-
-def invert_kernel(band_pixels, received, right, out, bias, left):
-    pair_count = 16
-    sources = right.shape[0] // pair_count
-    looks = LANES * 2 // pair_count
-    pixels = out.shape[0]
-
-    def aligned(words, half):
-        value = words.astype(jnp.float32)
-        return (pltpu.roll(value, sources - 1, 0) if half else value).T
-
     line = received[pl.ds(4, sources, stride=MESSAGE), :]
     lines = aligned(line, 0), aligned(line, 1)
     scales = []
@@ -269,21 +279,24 @@
     bias[...] = product[pixels:] * (1.0 / (CODES * band_pixels))
 
 
-def invert(received, codes, pixels, band_pixels):
-    total_pairs, dates = codes.shape
+def invert(received, kept, swapped, pixels, band_pixels):
+    total_pairs, dates = 2 * kept.shape[0], 2 * LANES
     vmem = pl.BlockSpec(memory_space=pltpu.VMEM)
     return pl.pallas_call(
         partial(invert_kernel, band_pixels),
-        in_specs=[vmem] * 2,
+        in_specs=[pl.BlockSpec(memory_space=pltpu.SMEM)] + [vmem] * 3,
         out_specs=[vmem] * 2,
         out_shape=[
             jax.ShapeDtypeStruct((pixels, dates), jnp.float32),
             jax.ShapeDtypeStruct((8, dates), jnp.float32),
         ],
-        scratch_shapes=[pltpu.VMEM((pixels + 8, total_pairs), jnp.float32)],
-        compiler_params=pltpu.CompilerParams(vmem_limit_bytes=24 << 20),
+        scratch_shapes=[
+            pltpu.VMEM((pixels + 8, total_pairs), jnp.float32),
+            pltpu.VMEM((total_pairs, dates), jnp.float32),
+        ],
+        compiler_params=pltpu.CompilerParams(vmem_limit_bytes=16 << 20),
         name="invert",
-    )(received, codes)
+    )((lax.axis_index("date") % 2).reshape(1), received, kept, swapped)
 
 
 def body(acquisitions, date_pairs, cycle_maps, inverse):
@@ -317,24 +330,20 @@
     kept = sent_inverse(words)
 
     combos = jnp.concatenate([combos, low_combos])
-    owned = [acquisitions[:, :, :, start:stop] for start, stop in CHUNKS]
-    owned, combos = lax.optimization_barrier((owned, combos))
-    earlier = ()
-    for (start, stop), own, (following, previous) in zip(CHUNKS, owned, others):
-        blank = jnp.zeros_like(line) if stop < width else line
-        earlier = phases(
-            start, stop, combos, own, following, previous, cycle_maps, low_cycles, blank, earlier
-        )
-
-    payload, kept = lax.optimization_barrier((earlier[0], kept))
+    looked = ()
+    for (start, stop), (following, previous) in zip(CHUNKS, others):
+        final = stop == width
+        rest = (combos, cycle_maps, low_cycles, line) if final else ()
+        looked = (phases(start, stop, final, acquisitions, following, previous, looked, *rest),)
+
+    payload, kept = lax.optimization_barrier((looked[0], kept))
     swapped = lax.ppermute(kept, "date", [(at, at ^ 1) for at in range(devices)])
-    codes = unpacked(kept, swapped)
     received = lax.all_to_all(
-        payload.reshape(devices, MESSAGE, LANES), "date", split_axis=0, concat_axis=0, tiled=True
+        payload.reshape(devices, 1, -1), "date", split_axis=0, concat_axis=0, tiled=True
     ).reshape(payload.shape)
     out_cols = look_cols // devices
     row_count = lax.axis_size("row")
-    result, bias = invert(received, codes, out_cols * look_rows, look_rows * look_cols * row_count)
+    result, bias = invert(received, kept, swapped, out_cols * look_rows, look_rows * look_cols * row_count)
     for step in range(1, row_count):
         result = result - passed_along(bias, "row", step)[:1]
     result = result - bias[:1]

time: 85.7 us -> 81.5 us (0.951)
  waiting for transfers between devices: 14 us -> 18.9 us
  Pallas kernels: 20.7 us -> 16.2 us
  local copies, waits for them, and re-layouts: 13.6 us -> 9.4 us
    pallas_call x4 -> x3, Pallas kernels: 20.7 us -> 16.2 us  [the longest x2 15.1 us: phases(): pl.pallas_call(partial(phase_kernel, start // LOOK_C, stop // LOOK_C, fin...]
    slice x2 -> x0, local copies, waits for them, and re-layouts: 4.41 us -> none  [body(): owned = [acquisitions[:, :, :, start:stop] for start, stop in CHUNKS]]
    ppermute x9, waiting for transfers between devices: 5.57 us -> 9.65 us  [passed_along(): return lax.ppermute(value, axis, pairs)]
    all_to_all x1, waiting for transfers between devices: 6.83 us -> 7.91 us  [body(): lax.all_to_all(payload.reshape(devices, 1, -1), 'date', split_axis=0, con...]
    unnamed x11 -> x7, local copies, waits for them, and re-layouts: 2.05 us -> 2.28 us
  transfers between devices with their start and end apart: 12 -> 12, of which waited for: 5 -> 6; matrix products, arithmetic and copies ran while one was open for 15% -> 10% of each run, Pallas kernels for 23% -> 19%
where the time goes in v6:
time: 81.5 us; the launch traced here: 80.9 us
  starting transfers between devices  33.7 us (41%)
  waiting for transfers between devices  18.9 us (23%)
  Pallas kernels  16.2 us (20%)
  local copies, waits for them, and re-layouts  9.4 us (12%)
  other arithmetic  2.62 us (3%)
    pallas_call x2, Pallas kernels, phases(): pl.pallas_call(partial(phase_kernel, start // LOOK_C, stop // LOOK_C, fin...  15.1 us
    ppermute x9, starting transfers between devices, passed_along(): return lax.ppermute(value, axis, pairs)  12.7 us
    all_to_all x1, starting transfers between devices, sent_inverse(): lax.all_to_all(sent.reshape(devices, per, LANES), 'date', split_axis=0, c...  10.7 us
    all_to_all x1, starting transfers between devices, body(): lax.all_to_all(payload.reshape(devices, 1, -1), 'date', split_axis=0, con...  10.1 us
    ppermute x9, waiting for transfers between devices, passed_along(): return lax.ppermute(value, axis, pairs)  9.65 us
    all_to_all x1, waiting for transfers between devices, body(): lax.all_to_all(payload.reshape(devices, 1, -1), 'date', split_axis=0, con...  7.91 us
    slice x2, local copies, waits for them, and re-layouts, parts(): return (images[:, :, :rows, start:stop], images[:, :, rows:, start:stop])  6.1 us
    unnamed x7, local copies, waits for them, and re-layouts  2.28 us
  transfers between devices with their start and end apart: 12, of which 6 were waited for; matrix products, arithmetic and copies ran while one was open for 10% of the time, Pallas kernels for 19%

profile of v6, /device:TPU:6, one launch (start us, length us, event | category | flops | bytes accessed | tf_op | source)
XLA Modules:
  0.0 80.9 jit_solution(1575460122636115802)
XLA Ops:
  0.0 0.8 fusion.4
  0.8 0.1 collective-permute-start
  0.9 0.9 %slice_convert_fusion = bf16[16,16,128]{2,1,0:T(8,128)(2,1)S(1)} fusion(s32[16,32,128]{2,1,0:T(8,128)} %refs_2_.1), kind=kLoop, calls=%fused_computation | loop fusion | flops 32768 | bytes 196608 | tf_op jit(solution)/shard_map/convert
  1.8 2.1 %collective-permute-start.1 = (bf16[16,16,128]{2,1,0:T(8,128)(2,1)S(1)}, bf16[16,16,128]{2,1,0:T(8,128)(2,1)S(1)}, u32[]{:S(2)}, u32[]{:S(2)}) collective-permute-start(bf16[16,16,128]{2,1,0:T(8,128)(2,1)S(1)} %slice_convert_fusion), channel_id=1, source_target_pairs={{0,4},{4,8},{8,12},{12,16},{16,20},{20,24},{24,28},{28,32},{32,36}... | collective-permute-start | bytes 196616 | tf_op jit(solution)/shard_map/ppermute | solution.py:34
  3.9 3.8 %fusion.7 = (bf16[4,2,64,1536]{3,2,1,0:T(8,128)(2,1)}, bf16[4,2,64,1536]{3,2,1,0:T(8,128)(2,1)}) fusion(bf16[4,2,128,2048]{3,2,1,0:T(8,128)(2,1)} %own.3), kind=kLoop, calls=%fused_computation.19 | loop fusion | bytes 6291456 | tf_op jit(solution)/shard_map/slice | solution.py:312
  7.7 0.0 copy-start.2
  7.7 0.0 collective-permute-done
  7.7 1.7 %collective-permute-done.1.refs_3_ = bf16[16,16,128]{2,1,0:T(8,128)(2,1)S(1)} collective-permute-done((bf16[16,16,128]{2,1,0:T(8,128)(2,1)S(1)}, bf16[16,16,128]{2,1,0:T(8,128)(2,1)S(1)}, u32[]{:S(2)}, u32[]{:S(2)}) %collective-permute-start.1) | collective-permute-done | bytes 65568 | tf_op jit(solution)/shard_map/ppermute | solution.py:34
  9.4 2.0 %collective-permute-start.4 = (bf16[4,2,64,1536]{3,2,1,0:T(8,128)(2,1)}, bf16[4,2,64,1536]{3,2,1,0:T(8,128)(2,1)S(1)}, u32[]{:S(2)}, u32[]{:S(2)}) collective-permute-start(bf16[4,2,64,1536]{3,2,1,0:T(8,128)(2,1)} %get-tuple-element.26), channel_id=1, source_target_pairs={{0,252},{4,0},{8,4},{12,8},{16,12},{20,16},{24,20},{28,24},{32,28}... | collective-permute-start | bytes 4718600 | tf_op jit(solution)/shard_map/ppermute | solution.py:34
  11.4 0.0 collective-permute-start.5
  11.4 2.3 %fusion.6 = (bf16[4,2,64,512]{3,2,1,0:T(8,128)(2,1)}, bf16[4,2,64,512]{3,2,1,0:T(8,128)(2,1)}) fusion(bf16[4,2,128,2048]{3,2,1,0:T(8,128)(2,1)} %own.3), kind=kLoop, calls=%fused_computation.18 | loop fusion | bytes 2097152 | tf_op jit(solution)/shard_map/slice | solution.py:312
  13.6 3.9 %collective-permute-start.2 = (bf16[4,2,64,512]{3,2,1,0:T(8,128)(2,1)}, bf16[4,2,64,512]{3,2,1,0:T(8,128)(2,1)}, u32[]{:S(2)}, u32[]{:S(2)}) collective-permute-start(bf16[4,2,64,512]{3,2,1,0:T(8,128)(2,1)} %get-tuple-element.24), channel_id=1, source_target_pairs={{0,252},{4,0},{8,4},{12,8},{16,12},{20,16},{24,20},{28,24},{32,28}... | collective-permute-start | bytes 1572872 | tf_op jit(solution)/shard_map/ppermute | solution.py:34
  17.5 0.0 collective-permute-start.3
  17.5 0.0 copy-done.2
  17.5 0.1 abs_reduce_fusion
  17.6 0.1 convert_bitcast_fusion
  17.7 0.8 broadcast_in_dim.18
  18.5 10.7 %all-to-all-start = ((s32[64,8,128]{2,1,0:T(8,128)}), s32[64,8,128]{2,1,0:T(8,128)S(1)}, u32[]{:S(2)}, u32[]{:S(2)}) async-start(s32[64,8,128]{2,1,0:T(8,128)} %bitcast.26), calls=%async_computation | async-start | bytes 524288 | tf_op jit(solution)/shard_map/all_to_all | solution.py:231
  29.2 0.1 reshape.65
  29.3 0.1 copy.8
  29.4 0.1 pad.4.clone
  29.5 0.1 broadcast_in_dim.15
  29.5 0.1 pad_add_fusion.refs_1_
  29.6 0.0 collective-permute-done.4.following
  29.6 4.1 %collective-permute-done.5.previous = bf16[4,2,64,1536]{3,2,1,0:T(8,128)(2,1)S(1)} collective-permute-done((bf16[4,2,64,1536]{3,2,1,0:T(8,128)(2,1)}, bf16[4,2,64,1536]{3,2,1,0:T(8,128)(2,1)S(1)}, u32[]{:S(2)}, u32[]{:S(2)}) %collective-permute-start.5) | collective-permute-done | bytes 1572896 | tf_op jit(solution)/shard_map/ppermute | solution.py:34
  33.7 0.0 copy-start
  33.7 2.2 %copy-done = bf16[4,2,128,2048]{3,2,1,0:T(8,128)(2,1)S(1)} copy-done((bf16[4,2,128,2048]{3,2,1,0:T(8,128)(2,1)S(1)}, bf16[4,2,128,2048]{3,2,1,0:T(8,128)(2,1)}, u32[]{:S(2)}) %copy-start) | copy-done | bytes 4194328
  35.9 0.0 copy-start.1
  35.9 9.4 %phases.2.refs_0_ = f32[2,512,128]{2,1,0:T(8,128)S(1)} custom-call(bf16[4,2,128,2048]{3,2,1,0:T(8,128)(2,1)S(1)} %copy-done, bf16[4,2,64,1536]{3,2,1,0:T(8,128)(2,1)S(1)} %collective-permute-done.4.following, bf16[4,2,64,1536]{3,2,1,0:T(8,128)(2,1)S(1)} %collective-permute-done.5.previous), custom_call_target="tpu_custom_call" | custom-call | flops 25165824 | bytes 6291456 | tf_op jit(solution)/shard_map/phases/pallas_call | solution.py:196
  45.3 0.0 collective-permute-done.2.following
  45.3 0.0 collective-permute-done.3.previous
  45.3 0.0 copy-done.1
  45.3 5.7 %phases.3 = s32[320,128]{1,0:T(8,128)} custom-call(bf16[4,2,128,2048]{3,2,1,0:T(8,128)(2,1)S(1)} %copy-done, bf16[4,2,64,512]{3,2,1,0:T(8,128)(2,1)} %collective-permute-done.2.following, bf16[4,2,64,512]{3,2,1,0:T(8,128)(2,1)} %collective-permute-done.3.previous, f32[2,512,128]{2,1,0:T(8,128)S(1)} %phases.2.refs_0_, s32[32]{0:T(128)S(1)} %pad_add_fusion.refs_1_, ...), custom_call_target="tpu_custom_call" | custom-call | flops 8388608 | bytes 2097152 | tf_op jit(solution)/shard_map/phases/pallas_call | solution.py:196
  51.1 0.0 all-to-all-done
  51.1 10.1 %all-to-all-start.1 = ((s32[64,1,640]{2,1,0:T(1,128)}), s32[64,1,640]{2,1,0:T(1,128)S(1)}, u32[]{:S(2)}, u32[]{:S(2)}) async-start(s32[64,1,640]{2,1,0:T(1,128)} %bitcast.8), calls=%async_computation.1 | async-start | bytes 327680 | tf_op jit(solution)/shard_map/all_to_all | solution.py:341
  61.1 0.2 collective-permute-start.6
  61.4 1.4 %collective-permute-done.6.swapped = s32[512,128]{1,0:T(8,128)S(1)} collective-permute-done((s32[512,128]{1,0:T(8,128)S(1)}, s32[512,128]{1,0:T(8,128)S(1)}, u32[]{:S(2)}, u32[]{:S(2)}) %collective-permute-start.6) | collective-permute-done | bytes 262176 | tf_op jit(solution)/shard_map/ppermute | solution.py:340
  62.7 7.9 %all-to-all-done.1 = s32[64,1,640]{2,1,0:T(1,128)S(1)} async-done(((s32[64,1,640]{2,1,0:T(1,128)}), s32[64,1,640]{2,1,0:T(1,128)S(1)}, u32[]{:S(2)}, u32[]{:S(2)}) %all-to-all-start.1) | async-done | bytes 163872 | tf_op jit(solution)/shard_map/all_to_all | solution.py:341
  70.7 1.1 %invert.1 = (f32[64,256]{1,0:T(8,128)S(1)}, f32[8,256]{1,0:T(8,128)S(1)}) custom-call(s32[1]{0:T(128)} %bitcast.side, s32[320,128]{1,0:T(8,128)S(1)} %bitcast.25, s32[512,128]{1,0:T(8,128)S(1)} %bitcast.24, s32[512,128]{1,0:T(8,128)S(1)} %collective-permute-done.6.swapped), custom_call_target="tpu_custom_call" | custom-call | tf_op jit(solution)/shard_map/invert/pallas_call | solution.py:285
  71.7 3.1 %collective-permute-start.9 = (f32[8,256]{1,0:T(8,128)S(1)}, f32[8,256]{1,0:T(8,128)S(1)}, u32[]{:S(2)}, u32[]{:S(2)}) collective-permute-start(f32[8,256]{1,0:T(8,128)S(1)} %get-tuple-element.34), channel_id=1, source_target_pairs={{0,3},{1,0},{2,1},{3,2},{4,7},{5,4},{6,5},{7,6},{8,11},{9,8},{10,9... | collective-permute-start | bytes 24584 | tf_op jit(solution)/shard_map/ppermute | solution.py:34
  74.8 0.6 collective-permute-start.8
  75.4 1.0 %collective-permute-start.7 = (f32[8,256]{1,0:T(8,128)S(1)}, f32[8,256]{1,0:T(8,128)S(1)}, u32[]{:S(2)}, u32[]{:S(2)}) collective-permute-start(f32[8,256]{1,0:T(8,128)S(1)} %get-tuple-element.34), channel_id=1, source_target_pairs={{0,1},{1,2},{2,3},{3,0},{4,5},{5,6},{6,7},{7,4},{8,9},{9,10},{10,1... | collective-permute-start | bytes 24584 | tf_op jit(solution)/shard_map/ppermute | solution.py:34
  76.4 0.0 collective-permute-done.9
  76.4 3.5 %collective-permute-done.8 = f32[8,256]{1,0:T(8,128)S(1)} collective-permute-done((f32[8,256]{1,0:T(8,128)S(1)}, f32[8,256]{1,0:T(8,128)S(1)}, u32[]{:S(2)}, u32[]{:S(2)}) %collective-permute-start.8) | collective-permute-done | bytes 8224 | tf_op jit(solution)/shard_map/ppermute | solution.py:34
  80.0 0.3 collective-permute-done.7
  80.3 0.6 subtract_subtract_fusion
  (7 shorter events, 0.0 us)
Async XLA Ops:
  0.8 6.9 %collective-permute-start = (s32[16]{0:T(128)S(1)}, s32[16]{0:T(128)S(1)}, u32[]{:S(2)}, u32[]{:S(2)}) collective-permute-start(s32[16]{0:T(128)S(1)} %fusion.4), channel_id=1, source_target_pairs={{0,4},{4,8},{8,12},{12,16},{16,20},{20,24},{24,28},{28,32},{32,36}... | collective-permute-start | bytes 200 | tf_op jit(solution)/shard_map/ppermute | solution.py:34
  1.8 7.6 %collective-permute-start.1 = (bf16[16,16,128]{2,1,0:T(8,128)(2,1)S(1)}, bf16[16,16,128]{2,1,0:T(8,128)(2,1)S(1)}, u32[]{:S(2)}, u32[]{:S(2)}) collective-permute-start(bf16[16,16,128]{2,1,0:T(8,128)(2,1)S(1)} %slice_convert_fusion), channel_id=1, source_target_pairs={{0,4},{4,8},{8,12},{12,16},{16,20},{20,24},{24,28},{28,32},{32,36}... | collective-permute-start | bytes 196616 | tf_op jit(solution)/shard_map/ppermute | solution.py:34
  7.7 9.8 %copy-start.2 = (f32[256,16]{0,1:T(8,128)S(1)}, f32[256,16]{0,1:T(8,128)}, u32[]{:S(2)}) copy-start(f32[256,16]{0,1:T(8,128)} %param.7) | copy-start | bytes 49156
  9.4 20.2 %collective-permute-start.4 = (bf16[4,2,64,1536]{3,2,1,0:T(8,128)(2,1)}, bf16[4,2,64,1536]{3,2,1,0:T(8,128)(2,1)S(1)}, u32[]{:S(2)}, u32[]{:S(2)}) collective-permute-start(bf16[4,2,64,1536]{3,2,1,0:T(8,128)(2,1)} %get-tuple-element.26), channel_id=1, source_target_pairs={{0,252},{4,0},{8,4},{12,8},{16,12},{20,16},{24,20},{28,24},{32,28}... | collective-permute-start | bytes 4718600 | tf_op jit(solution)/shard_map/ppermute | solution.py:34
  11.4 22.3 %collective-permute-start.5 = (bf16[4,2,64,1536]{3,2,1,0:T(8,128)(2,1)}, bf16[4,2,64,1536]{3,2,1,0:T(8,128)(2,1)S(1)}, u32[]{:S(2)}, u32[]{:S(2)}) collective-permute-start(bf16[4,2,64,1536]{3,2,1,0:T(8,128)(2,1)} %get-tuple-element.27), channel_id=1, source_target_pairs={{0,4},{4,8},{8,12},{12,16},{16,20},{20,24},{24,28},{28,32},{32,36}... | collective-permute-start | bytes 4718600 | tf_op jit(solution)/shard_map/ppermute | solution.py:34
  13.6 31.7 %collective-permute-start.2 = (bf16[4,2,64,512]{3,2,1,0:T(8,128)(2,1)}, bf16[4,2,64,512]{3,2,1,0:T(8,128)(2,1)}, u32[]{:S(2)}, u32[]{:S(2)}) collective-permute-start(bf16[4,2,64,512]{3,2,1,0:T(8,128)(2,1)} %get-tuple-element.24), channel_id=1, source_target_pairs={{0,252},{4,0},{8,4},{12,8},{16,12},{20,16},{24,20},{28,24},{32,28}... | collective-permute-start | bytes 1572872 | tf_op jit(solution)/shard_map/ppermute | solution.py:34
  17.5 27.8 %collective-permute-start.3 = (bf16[4,2,64,512]{3,2,1,0:T(8,128)(2,1)}, bf16[4,2,64,512]{3,2,1,0:T(8,128)(2,1)}, u32[]{:S(2)}, u32[]{:S(2)}) collective-permute-start(bf16[4,2,64,512]{3,2,1,0:T(8,128)(2,1)} %get-tuple-element.25), channel_id=1, source_target_pairs={{0,4},{4,8},{8,12},{12,16},{16,20},{20,24},{24,28},{28,32},{32,36}... | collective-permute-start | bytes 1572872 | tf_op jit(solution)/shard_map/ppermute | solution.py:34
  18.5 32.6 %all-to-all-start = ((s32[64,8,128]{2,1,0:T(8,128)}), s32[64,8,128]{2,1,0:T(8,128)S(1)}, u32[]{:S(2)}, u32[]{:S(2)}) async-start(s32[64,8,128]{2,1,0:T(8,128)} %bitcast.26), calls=%async_computation | async-start | bytes 524288 | tf_op jit(solution)/shard_map/all_to_all | solution.py:231
  33.7 2.2 %copy-start = (bf16[4,2,128,2048]{3,2,1,0:T(8,128)(2,1)S(1)}, bf16[4,2,128,2048]{3,2,1,0:T(8,128)(2,1)}, u32[]{:S(2)}) copy-start(bf16[4,2,128,2048]{3,2,1,0:T(8,128)(2,1)} %own.3) | copy-start | bytes 12582916
  35.9 9.4 %copy-start.1 = (s32[16,32,128]{2,1,0:T(8,128)S(1)}, s32[16,32,128]{2,1,0:T(8,128)}, u32[]{:S(2)}) copy-start(s32[16,32,128]{2,1,0:T(8,128)} %refs_2_.1) | copy-start | bytes 786436
  51.1 19.6 %all-to-all-start.1 = ((s32[64,1,640]{2,1,0:T(1,128)}), s32[64,1,640]{2,1,0:T(1,128)S(1)}, u32[]{:S(2)}, u32[]{:S(2)}) async-start(s32[64,1,640]{2,1,0:T(1,128)} %bitcast.8), calls=%async_computation.1 | async-start | bytes 327680 | tf_op jit(solution)/shard_map/all_to_all | solution.py:341
  61.1 1.6 %collective-permute-start.6 = (s32[512,128]{1,0:T(8,128)S(1)}, s32[512,128]{1,0:T(8,128)S(1)}, u32[]{:S(2)}, u32[]{:S(2)}) collective-permute-start(s32[512,128]{1,0:T(8,128)S(1)} %bitcast.23), channel_id=1, source_target_pairs={{0,4},{4,0},{8,12},{12,8},{16,20},{20,16},{24,28},{28,24},{32,36},... | collective-permute-start | bytes 786440 | tf_op jit(solution)/shard_map/ppermute | solution.py:340
  71.7 4.7 %collective-permute-start.9 = (f32[8,256]{1,0:T(8,128)S(1)}, f32[8,256]{1,0:T(8,128)S(1)}, u32[]{:S(2)}, u32[]{:S(2)}) collective-permute-start(f32[8,256]{1,0:T(8,128)S(1)} %get-tuple-element.34), channel_id=1, source_target_pairs={{0,3},{1,0},{2,1},{3,2},{4,7},{5,4},{6,5},{7,6},{8,11},{9,8},{10,9... | collective-permute-start | bytes 24584 | tf_op jit(solution)/shard_map/ppermute | solution.py:34
  74.8 5.2 %collective-permute-start.8 = (f32[8,256]{1,0:T(8,128)S(1)}, f32[8,256]{1,0:T(8,128)S(1)}, u32[]{:S(2)}, u32[]{:S(2)}) collective-permute-start(f32[8,256]{1,0:T(8,128)S(1)} %get-tuple-element.34), channel_id=1, source_target_pairs={{0,2},{1,3},{2,0},{3,1},{4,6},{5,7},{6,4},{7,5},{8,10},{9,11},{10,... | collective-permute-start | bytes 24584 | tf_op jit(solution)/shard_map/ppermute | solution.py:34
  75.4 4.9 %collective-permute-start.7 = (f32[8,256]{1,0:T(8,128)S(1)}, f32[8,256]{1,0:T(8,128)S(1)}, u32[]{:S(2)}, u32[]{:S(2)}) collective-permute-start(f32[8,256]{1,0:T(8,128)S(1)} %get-tuple-element.34), channel_id=1, source_target_pairs={{0,1},{1,2},{2,3},{3,0},{4,5},{5,6},{6,7},{7,4},{8,9},{9,10},{10,1... | collective-permute-start | bytes 24584 | tf_op jit(solution)/shard_map/ppermute | solution.py:34

commit v7 on v6

--- a/solution.py
+++ b/solution.py
@@ -75,10 +75,22 @@
                 lanes = pl.ds(pl.multiple_of(col + tile * LANES, LANES), LANES)
                 images[start + date, part, tile] = source[date, part, pl.ds(row, rows), lanes].astype(jnp.float32)
 
+    looked[...] = jnp.zeros_like(looked) if earlier is None else earlier[...]
+    quarter = high.shape[1] // tiles
+
+    def multiplied(index, piece):
+        place = pl.ds(pl.multiple_of(piece * quarter, quarter), quarter)
+        chosen = picked[lax.rem(index + steps, steps)]
+        held = lax.rem(index + 2, 2)
+        summed = jnp.dot(high[held, place, :], chosen, preferred_element_type=jnp.float32)
+        summed += jnp.dot(low[held, place, :], chosen, preferred_element_type=jnp.float32)
+        target = jnp.where(index < 0, 2, index // steps)
+        looked[target, place, :] += summed
+
     @pl.loop(0, 2 * steps)
     def _(index):
         half, step_at = index // steps, index % steps
-        widen(own, half * group, pl.multiple_of(half * rows, rows), first_col * LOOK_C + step_at * width)
+        widen(own, half * group, pl.multiple_of(half * rows, rows), step_at * width)
 
         @pl.when(half == 0)
         def _():
@@ -90,6 +102,7 @@
 
         @pl.loop(0, tiles)
         def _(tile):
+            multiplied(index - 1, tile)
             lanes = pl.ds(pl.multiple_of(tile * LANES, LANES), LANES)
             for date in range(0, group, 2):
                 totals = {}
@@ -117,24 +130,17 @@
                             head = value.astype(jnp.bfloat16)
                             tail = (value - head.astype(jnp.float32)).astype(jnp.bfloat16)
                             start = (part * pair_count + first * group + gap) * looks
-                            high[start : start + looks, lanes] = head
-                            low[start : start + looks, lanes] = tail
-
-        summed = jnp.dot(high[...], picked[step_at], preferred_element_type=jnp.float32)
-        summed += jnp.dot(low[...], picked[step_at], preferred_element_type=jnp.float32)
-
-        @pl.when(step_at == 0)
-        def _():
-            looked[half] = summed if earlier is None else earlier[half] + summed
-
-        @pl.when(step_at > 0)
-        def _():
-            looked[half] += summed
+                            high[lax.rem(index, 2), start : start + looks, lanes] = head
+                            low[lax.rem(index, 2), start : start + looks, lanes] = tail
+
+    @pl.loop(0, tiles)
+    def _(piece):
+        multiplied(2 * steps - 1, piece)
 
     if not final:
         return
     cycles[0] = TWO_PI * high_cycles[:, :looks, :].astype(jnp.float32).reshape(cycles.shape[1:])
-    cycles[1] = TWO_PI * low_cycles[...].astype(jnp.float32).reshape(cycles.shape[1:])
+    cycles[1] = TWO_PI * low_cycles[:, looks:, :].astype(jnp.float32).reshape(cycles.shape[1:])
 
     @pl.loop(0, 2)
     def _(half):
@@ -169,19 +175,19 @@
 def phases(start, stop, final, own, following, previous, earlier, *rest):
     group, _, height, _ = own.shape
     rows = height // 2
-    looked_cols = own.shape[3] // LOOK_C
+    looked_cols = LANES
     looks = rows // LOOK_R
     tiles = STEP // LANES
     pair_count = group * group
     steps = (stop - start) // STEP
     vmem = pl.BlockSpec(memory_space=pltpu.VMEM)
     in_specs = [vmem] * (3 + len(earlier))
-    looked_shape = (2, 2 * pair_count * looks, looked_cols)
+    looked_shape = (3, 2 * pair_count * looks, looked_cols)
     out_shape = jax.ShapeDtypeStruct(looked_shape, jnp.float32)
     scratch = [
         pltpu.VMEM((2 * group, 2, tiles, rows, LANES), jnp.float32),
-        pltpu.VMEM((2 * pair_count * looks, STEP), jnp.bfloat16),
-        pltpu.VMEM((2 * pair_count * looks, STEP), jnp.bfloat16),
+        pltpu.VMEM((2, 2 * pair_count * looks, STEP), jnp.bfloat16),
+        pltpu.VMEM((2, 2 * pair_count * looks, STEP), jnp.bfloat16),
         pltpu.VMEM((steps, STEP, looked_cols), jnp.bfloat16),
     ]
     if final:
@@ -306,7 +312,6 @@
     pair_count, look_rows, look_cols = cycle_maps.shape
     rows = height // 2
     half = look_rows // 2
-    me = lax.axis_index("date")
 
     def parts(images, start, stop):
         return images[:, :, :rows, start:stop], images[:, :, rows:, start:stop]
@@ -314,27 +319,31 @@
     def exchanged(pair):
         return passed_along(pair[0], "date", -1), passed_along(pair[1], "date", 1)
 
-    gaps = (date_pairs[:, 1] - date_pairs[:, 0] + total_dates) % total_dates
-    combos = (date_pairs[:, 0] - me * group) * group + gaps - 1
-    low_combos = passed_along(combos, "date", 1)
-    low_cycles = passed_along(cycle_maps[:, half:].astype(jnp.bfloat16), "date", 1)
-    left, others = acquisitions, []
-    for start, stop in CHUNKS:
-        sent, left, low_combos, low_cycles, inverse = lax.optimization_barrier(
-            (parts(left, start, stop), left, low_combos, low_cycles, inverse)
-        )
-        others.append(exchanged(sent))
-
+    low_pairs = passed_along(date_pairs, "date", 1)
+    low_cycles = passed_along(cycle_maps, "date", 1)
+    sent, left, low_pairs, low_cycles, date_pairs, inverse = lax.optimization_barrier(
+        (parts(acquisitions, *CHUNKS[0]), acquisitions, low_pairs, low_cycles, date_pairs, inverse)
+    )
+    others = [exchanged(sent)]
     words, exponent = coded_inverse(inverse)
     line = exponent_line(exponent)
+    for start, stop in CHUNKS[1:]:
+        sent, left, words = lax.optimization_barrier((parts(left, start, stop), left, words))
+        others.append(exchanged(sent))
+
     kept = sent_inverse(words)
 
-    combos = jnp.concatenate([combos, low_combos])
+    pairs = jnp.concatenate([date_pairs, low_pairs])
+    gaps = (pairs[:, 1] - pairs[:, 0] + total_dates) % total_dates
+    combos = pairs[:, 0] % group * group + gaps - 1
+    late, words = lax.optimization_barrier((left, words))
+    owned = [late[:, :, :, start:stop] for start, stop in CHUNKS]
+    owned, combos = lax.optimization_barrier((owned, combos))
     looked = ()
-    for (start, stop), (following, previous) in zip(CHUNKS, others):
+    for (start, stop), own, (following, previous) in zip(CHUNKS, owned, others):
         final = stop == width
         rest = (combos, cycle_maps, low_cycles, line) if final else ()
-        looked = (phases(start, stop, final, acquisitions, following, previous, looked, *rest),)
+        looked = (phases(start, stop, final, own, following, previous, looked, *rest),)
 
     payload, kept = lax.optimization_barrier((looked[0], kept))
     swapped = lax.ppermute(kept, "date", [(at, at ^ 1) for at in range(devices)])

time: 81.5 us -> 81.5 us (level)
  local copies, waits for them, and re-layouts: 9.4 us -> 12.5 us
  Pallas kernels: 16.2 us -> 18.3 us
  starting transfers between devices: 33.7 us -> 31.9 us
  waiting for transfers between devices: 18.9 us -> 17.2 us
  other arithmetic: 2.62 us -> 0.95 us
    slice x0 -> x2, local copies, waits for them, and re-layouts: none -> 4.5 us  [body(): owned = [late[:, :, :, start:stop] for start, stop in CHUNKS]]
    ppermute x9, starting transfers between devices: 12.7 us -> 10.6 us  [passed_along(): return lax.ppermute(value, axis, pairs)]
    pallas_call x2, Pallas kernels: 15.1 us -> 17.2 us  [phases(): pl.pallas_call(partial(phase_kernel, start // LOOK_C, stop // LOOK_C, fin...]
    ppermute x9, waiting for transfers between devices: 9.65 us -> 7.95 us  [passed_along(): return lax.ppermute(value, axis, pairs)]
    unnamed x7 -> x13, local copies, waits for them, and re-layouts: 2.28 us -> 0.8 us
    another operation x1 -> x0, other arithmetic: 0.92 us -> none
  transfers between devices with their start and end apart: 12 -> 12, of which waited for: 6 -> 6; matrix products, arithmetic and copies ran while one was open for 10% -> 15% of each run, Pallas kernels for 19% -> 21%
where the time goes in v7:
time: 81.5 us; the launch traced here: 80.9 us
  starting transfers between devices  31.9 us (39%)
  Pallas kernels  18.3 us (22%)
  waiting for transfers between devices  17.2 us (21%)
  local copies, waits for them, and re-layouts  12.5 us (15%)
  other arithmetic  0.95 us (1%)
    pallas_call x2, Pallas kernels, phases(): pl.pallas_call(partial(phase_kernel, start // LOOK_C, stop // LOOK_C, fin...  17.2 us
    all_to_all x1, starting transfers between devices, sent_inverse(): lax.all_to_all(sent.reshape(devices, per, LANES), 'date', split_axis=0, c...  10.7 us
    ppermute x9, starting transfers between devices, passed_along(): return lax.ppermute(value, axis, pairs)  10.6 us
    all_to_all x1, starting transfers between devices, body(): lax.all_to_all(payload.reshape(devices, 1, -1), 'date', split_axis=0, con...  10.3 us
    ppermute x9, waiting for transfers between devices, passed_along(): return lax.ppermute(value, axis, pairs)  7.95 us
    all_to_all x1, waiting for transfers between devices, body(): lax.all_to_all(payload.reshape(devices, 1, -1), 'date', split_axis=0, con...  7.91 us
    slice x2, local copies, waits for them, and re-layouts, parts(): return (images[:, :, :rows, start:stop], images[:, :, rows:, start:stop])  6.21 us
    slice x2, local copies, waits for them, and re-layouts, body(): owned = [late[:, :, :, start:stop] for start, stop in CHUNKS]  4.5 us
  transfers between devices with their start and end apart: 12, of which 6 were waited for; matrix products, arithmetic and copies ran while one was open for 15% of the time, Pallas kernels for 21%

profile of v7, /device:TPU:6, one launch (start us, length us, event | category | flops | bytes accessed | tf_op | source)
XLA Modules:
  0.0 80.9 jit_solution(16658296817058499677)
XLA Ops:
  0.0 0.0 collective-permute-start
  0.0 2.0 %collective-permute-start.1 = (s32[16,32,128]{2,1,0:T(8,128)}, s32[16,32,128]{2,1,0:T(8,128)S(1)}, u32[]{:S(2)}, u32[]{:S(2)}) collective-permute-start(s32[16,32,128]{2,1,0:T(8,128)} %refs_2_.1), channel_id=1, source_target_pairs={{0,4},{4,8},{8,12},{12,16},{16,20},{20,24},{24,28},{28,32},{32,36}... | collective-permute-start | bytes 786440 | tf_op jit(solution)/shard_map/ppermute | solution.py:34
  2.0 3.8 %fusion.9 = (bf16[4,2,64,1536]{3,2,1,0:T(8,128)(2,1)}, bf16[4,2,64,1536]{3,2,1,0:T(8,128)(2,1)}) fusion(bf16[4,2,128,2048]{3,2,1,0:T(8,128)(2,1)} %param.4), kind=kLoop, calls=%fused_computation.24 | loop fusion | bytes 6291456 | tf_op jit(solution)/shard_map/slice | solution.py:317
  5.9 1.2 %collective-permute-done = s32[16,2]{0,1:T(2,128)S(1)} collective-permute-done((s32[16,2]{0,1:T(2,128)}, s32[16,2]{0,1:T(2,128)S(1)}, u32[]{:S(2)}, u32[]{:S(2)}) %collective-permute-start) | collective-permute-done | bytes 160 | tf_op jit(solution)/shard_map/ppermute | solution.py:34
  7.0 2.9 %collective-permute-done.1.refs_3_ = s32[16,32,128]{2,1,0:T(8,128)S(1)} collective-permute-done((s32[16,32,128]{2,1,0:T(8,128)}, s32[16,32,128]{2,1,0:T(8,128)S(1)}, u32[]{:S(2)}, u32[]{:S(2)}) %collective-permute-start.1) | collective-permute-done | bytes 262176 | tf_op jit(solution)/shard_map/ppermute | solution.py:34
  9.9 0.7 copy-done.2
  10.6 0.0 collective-permute-start.4
  10.6 0.5 collective-permute-start.5
  11.1 0.0 copy-done.4
  11.1 0.1 abs_reduce_fusion
  11.2 0.1 convert_bitcast_fusion
  11.3 2.4 %fusion.8 = (bf16[4,2,64,512]{3,2,1,0:T(8,128)(2,1)}, bf16[4,2,64,512]{3,2,1,0:T(8,128)(2,1)}) fusion(bf16[4,2,128,2048]{3,2,1,0:T(8,128)(2,1)} %param.4), kind=kLoop, calls=%fused_computation.23 | loop fusion | bytes 2097152 | tf_op jit(solution)/shard_map/slice | solution.py:317
  13.7 3.3 %collective-permute-start.2 = (bf16[4,2,64,512]{3,2,1,0:T(8,128)(2,1)}, bf16[4,2,64,512]{3,2,1,0:T(8,128)(2,1)}, u32[]{:S(2)}, u32[]{:S(2)}) collective-permute-start(bf16[4,2,64,512]{3,2,1,0:T(8,128)(2,1)} %get-tuple-element.32), channel_id=1, source_target_pairs={{0,252},{4,0},{8,4},{12,8},{16,12},{20,16},{24,20},{28,24},{32,28}... | collective-permute-start | bytes 1572872 | tf_op jit(solution)/shard_map/ppermute | solution.py:34
  17.1 0.0 collective-permute-start.3
  17.1 0.7 broadcast_in_dim.18
  17.8 10.7 %all-to-all-start = ((s32[64,8,128]{2,1,0:T(8,128)}), s32[64,8,128]{2,1,0:T(8,128)S(1)}, u32[]{:S(2)}, u32[]{:S(2)}) async-start(s32[64,8,128]{2,1,0:T(8,128)} %bitcast.6), calls=%async_computation | async-start | bytes 524288 | tf_op jit(solution)/shard_map/all_to_all | solution.py:237
  28.5 2.3 %slice.50.own = bf16[4,2,128,512]{3,2,1,0:T(8,128)(2,1)} slice(bf16[4,2,128,2048]{3,2,1,0:T(8,128)(2,1)} %param.4), slice={[0:4], [0:2], [0:128], [1536:2048]} | slice | bytes 2097152 | tf_op jit(solution)/shard_map/slice | solution.py:340
  30.8 2.2 %slice.49.own = bf16[4,2,128,1536]{3,2,1,0:T(8,128)(2,1)S(1)} slice(bf16[4,2,128,2048]{3,2,1,0:T(8,128)(2,1)} %param.4), slice={[0:4], [0:2], [0:128], [0:1536]} | slice | bytes 6291456 | tf_op jit(solution)/shard_map/slice | solution.py:340
  33.0 0.1 reshape.58
  33.1 0.1 copy.8
  33.2 0.1 pad.4.clone
  33.3 0.1 broadcast_in_dim.15
  33.3 0.0 copy-done.5
  33.3 0.1 pad_add_fusion
  33.4 0.0 copy-start
  33.5 0.0 copy-start.1
  33.5 0.0 copy-start.3
  33.5 0.0 collective-permute-done.4.following
  33.5 0.0 collective-permute-done.5.previous
  33.5 11.0 %phases.2.refs_0_ = f32[3,512,128]{2,1,0:T(8,128)S(1)} custom-call(bf16[4,2,128,1536]{3,2,1,0:T(8,128)(2,1)S(1)} %slice.49.own, bf16[4,2,64,1536]{3,2,1,0:T(8,128)(2,1)} %collective-permute-done.4.following, bf16[4,2,64,1536]{3,2,1,0:T(8,128)(2,1)} %collective-permute-done.5.previous), custom_call_target="tpu_custom_call" | custom-call | flops 25165824 | bytes 6291456 | tf_op jit(solution)/shard_map/phases/pallas_call | solution.py:202
  44.5 0.0 collective-permute-done.2.following
  44.5 0.0 collective-permute-done.3.previous
  44.5 0.0 copy-done
  44.5 0.0 copy-done.1
  44.5 6.2 %phases.3 = s32[320,128]{1,0:T(8,128)} custom-call(bf16[4,2,128,512]{3,2,1,0:T(8,128)(2,1)S(1)} %copy-done, bf16[4,2,64,512]{3,2,1,0:T(8,128)(2,1)} %collective-permute-done.2.following, bf16[4,2,64,512]{3,2,1,0:T(8,128)(2,1)} %collective-permute-done.3.previous, f32[3,512,128]{2,1,0:T(8,128)S(1)} %phases.2.refs_0_, s32[32]{0:T(128)S(1)} %fusion.6.refs_1_, ...), custom_call_target="tpu_custom_call" | custom-call | flops 8388608 | bytes 2097152 | tf_op jit(solution)/shard_map/phases/pallas_call | solution.py:202
  50.8 0.0 all-to-all-done
  50.8 10.3 %all-to-all-start.1 = ((s32[64,1,640]{2,1,0:T(1,128)}), s32[64,1,640]{2,1,0:T(1,128)S(1)}, u32[]{:S(2)}, u32[]{:S(2)}) async-start(s32[64,1,640]{2,1,0:T(1,128)} %bitcast.8), calls=%async_computation.1 | async-start | bytes 327680 | tf_op jit(solution)/shard_map/all_to_all | solution.py:350
  61.1 0.2 collective-permute-start.6
  61.4 1.4 %collective-permute-done.6.swapped = s32[512,128]{1,0:T(8,128)S(1)} collective-permute-done((s32[512,128]{1,0:T(8,128)S(1)}, s32[512,128]{1,0:T(8,128)S(1)}, u32[]{:S(2)}, u32[]{:S(2)}) %collective-permute-start.6) | collective-permute-done | bytes 262176 | tf_op jit(solution)/shard_map/ppermute | solution.py:349
  62.8 7.9 %all-to-all-done.1 = s32[64,1,640]{2,1,0:T(1,128)S(1)} async-done(((s32[64,1,640]{2,1,0:T(1,128)}), s32[64,1,640]{2,1,0:T(1,128)S(1)}, u32[]{:S(2)}, u32[]{:S(2)}) %all-to-all-start.1) | async-done | bytes 163872 | tf_op jit(solution)/shard_map/all_to_all | solution.py:350
  70.7 1.1 %invert.1 = (f32[64,256]{1,0:T(8,128)S(1)}, f32[8,256]{1,0:T(8,128)S(1)}) custom-call(s32[1]{0:T(128)} %bitcast.side, s32[320,128]{1,0:T(8,128)S(1)} %bitcast.28, s32[512,128]{1,0:T(8,128)S(1)} %bitcast.27, s32[512,128]{1,0:T(8,128)S(1)} %collective-permute-done.6.swapped), custom_call_target="tpu_custom_call" | custom-call | tf_op jit(solution)/shard_map/invert/pallas_call | solution.py:291
  71.7 3.1 %collective-permute-start.9 = (f32[8,256]{1,0:T(8,128)S(1)}, f32[8,256]{1,0:T(8,128)S(1)}, u32[]{:S(2)}, u32[]{:S(2)}) collective-permute-start(f32[8,256]{1,0:T(8,128)S(1)} %get-tuple-element.42), channel_id=1, source_target_pairs={{0,3},{1,0},{2,1},{3,2},{4,7},{5,4},{6,5},{7,6},{8,11},{9,8},{10,9... | collective-permute-start | bytes 24584 | tf_op jit(solution)/shard_map/ppermute | solution.py:34
  74.8 0.6 collective-permute-start.8
  75.4 1.0 %collective-permute-start.7 = (f32[8,256]{1,0:T(8,128)S(1)}, f32[8,256]{1,0:T(8,128)S(1)}, u32[]{:S(2)}, u32[]{:S(2)}) collective-permute-start(f32[8,256]{1,0:T(8,128)S(1)} %get-tuple-element.42), channel_id=1, source_target_pairs={{0,1},{1,2},{2,3},{3,0},{4,5},{5,6},{6,7},{7,4},{8,9},{9,10},{10,1... | collective-permute-start | bytes 24584 | tf_op jit(solution)/shard_map/ppermute | solution.py:34
  76.4 0.0 collective-permute-done.9
  76.4 3.5 %collective-permute-done.8 = f32[8,256]{1,0:T(8,128)S(1)} collective-permute-done((f32[8,256]{1,0:T(8,128)S(1)}, f32[8,256]{1,0:T(8,128)S(1)}, u32[]{:S(2)}, u32[]{:S(2)}) %collective-permute-start.8) | collective-permute-done | bytes 8224 | tf_op jit(solution)/shard_map/ppermute | solution.py:34
  80.0 0.3 collective-permute-done.7
  80.3 0.6 subtract_subtract_fusion
  (12 shorter events, 0.1 us)
Async XLA Ops:
  0.0 11.1 %copy-start.4 = (f32[256,16]{0,1:T(8,128)S(1)}, f32[256,16]{0,1:T(8,128)}, u32[]{:S(2)}) copy-start(f32[256,16]{0,1:T(8,128)} %param.7) | copy-start | bytes 49156
  0.0 7.0 %collective-permute-start = (s32[16,2]{0,1:T(2,128)}, s32[16,2]{0,1:T(2,128)S(1)}, u32[]{:S(2)}, u32[]{:S(2)}) collective-permute-start(s32[16,2]{0,1:T(2,128)} %param.5), channel_id=1, source_target_pairs={{0,4},{4,8},{8,12},{12,16},{16,20},{20,24},{24,28},{28,32},{32,36}... | collective-permute-start | bytes 392 | tf_op jit(solution)/shard_map/ppermute | solution.py:34
  0.0 9.9 %collective-permute-start.1 = (s32[16,32,128]{2,1,0:T(8,128)}, s32[16,32,128]{2,1,0:T(8,128)S(1)}, u32[]{:S(2)}, u32[]{:S(2)}) collective-permute-start(s32[16,32,128]{2,1,0:T(8,128)} %refs_2_.1), channel_id=1, source_target_pairs={{0,4},{4,8},{8,12},{12,16},{16,20},{20,24},{24,28},{28,32},{32,36}... | collective-permute-start | bytes 786440 | tf_op jit(solution)/shard_map/ppermute | solution.py:34
  9.9 0.7 copy-start.2
  10.6 22.9 %collective-permute-start.4 = (bf16[4,2,64,1536]{3,2,1,0:T(8,128)(2,1)}, bf16[4,2,64,1536]{3,2,1,0:T(8,128)(2,1)}, u32[]{:S(2)}, u32[]{:S(2)}) collective-permute-start(bf16[4,2,64,1536]{3,2,1,0:T(8,128)(2,1)} %get-tuple-element.35), channel_id=1, source_target_pairs={{0,252},{4,0},{8,4},{12,8},{16,12},{20,16},{24,20},{28,24},{32,28}... | collective-permute-start | bytes 4718600 | tf_op jit(solution)/shard_map/ppermute | solution.py:34
  10.6 22.9 %collective-permute-start.5 = (bf16[4,2,64,1536]{3,2,1,0:T(8,128)(2,1)}, bf16[4,2,64,1536]{3,2,1,0:T(8,128)(2,1)}, u32[]{:S(2)}, u32[]{:S(2)}) collective-permute-start(bf16[4,2,64,1536]{3,2,1,0:T(8,128)(2,1)} %get-tuple-element.36), channel_id=1, source_target_pairs={{0,4},{4,8},{8,12},{12,16},{16,20},{20,24},{24,28},{28,32},{32,36}... | collective-permute-start | bytes 4718600 | tf_op jit(solution)/shard_map/ppermute | solution.py:34
  13.7 30.8 %collective-permute-start.2 = (bf16[4,2,64,512]{3,2,1,0:T(8,128)(2,1)}, bf16[4,2,64,512]{3,2,1,0:T(8,128)(2,1)}, u32[]{:S(2)}, u32[]{:S(2)}) collective-permute-start(bf16[4,2,64,512]{3,2,1,0:T(8,128)(2,1)} %get-tuple-element.32), channel_id=1, source_target_pairs={{0,252},{4,0},{8,4},{12,8},{16,12},{20,16},{24,20},{28,24},{32,28}... | collective-permute-start | bytes 1572872 | tf_op jit(solution)/shard_map/ppermute | solution.py:34
  17.1 27.4 %collective-permute-start.3 = (bf16[4,2,64,512]{3,2,1,0:T(8,128)(2,1)}, bf16[4,2,64,512]{3,2,1,0:T(8,128)(2,1)}, u32[]{:S(2)}, u32[]{:S(2)}) collective-permute-start(bf16[4,2,64,512]{3,2,1,0:T(8,128)(2,1)} %get-tuple-element.33), channel_id=1, source_target_pairs={{0,4},{4,8},{8,12},{12,16},{16,20},{20,24},{24,28},{28,32},{32,36}... | collective-permute-start | bytes 1572872 | tf_op jit(solution)/shard_map/ppermute | solution.py:34
  17.8 33.0 %all-to-all-start = ((s32[64,8,128]{2,1,0:T(8,128)}), s32[64,8,128]{2,1,0:T(8,128)S(1)}, u32[]{:S(2)}, u32[]{:S(2)}) async-start(s32[64,8,128]{2,1,0:T(8,128)} %bitcast.6), calls=%async_computation | async-start | bytes 524288 | tf_op jit(solution)/shard_map/all_to_all | solution.py:237
  30.8 2.6 %copy-start.5 = (s32[16,2]{0,1:T(2,128)S(1)}, s32[16,2]{0,1:T(2,128)}, u32[]{:S(2)}) copy-start(s32[16,2]{0,1:T(2,128)} %param.5) | copy-start | bytes 388
  33.4 11.1 %copy-start = (bf16[4,2,128,512]{3,2,1,0:T(8,128)(2,1)S(1)}, bf16[4,2,128,512]{3,2,1,0:T(8,128)(2,1)}, u32[]{:S(2)}) copy-start(bf16[4,2,128,512]{3,2,1,0:T(8,128)(2,1)} %slice.50.own) | copy-start | bytes 3145732
  33.5 11.1 %copy-start.1 = (s32[16,32,128]{2,1,0:T(8,128)S(1)}, s32[16,32,128]{2,1,0:T(8,128)}, u32[]{:S(2)}) copy-start(s32[16,32,128]{2,1,0:T(8,128)} %refs_2_.1) | copy-start | bytes 786436
  33.5 11.1 %copy-start.3 = (s32[16,32,128]{2,1,0:T(8,128)S(1)}, s32[16,32,128]{2,1,0:T(8,128)}, u32[]{:S(2)}) copy-start(s32[16,32,128]{2,1,0:T(8,128)} %copy-done.2) | copy-start | bytes 786436
  50.8 19.9 %all-to-all-start.1 = ((s32[64,1,640]{2,1,0:T(1,128)}), s32[64,1,640]{2,1,0:T(1,128)S(1)}, u32[]{:S(2)}, u32[]{:S(2)}) async-start(s32[64,1,640]{2,1,0:T(1,128)} %bitcast.8), calls=%async_computation.1 | async-start | bytes 327680 | tf_op jit(solution)/shard_map/all_to_all | solution.py:350
  61.1 1.6 %collective-permute-start.6 = (s32[512,128]{1,0:T(8,128)S(1)}, s32[512,128]{1,0:T(8,128)S(1)}, u32[]{:S(2)}, u32[]{:S(2)}) collective-permute-start(s32[512,128]{1,0:T(8,128)S(1)} %bitcast.26), channel_id=1, source_target_pairs={{0,4},{4,0},{8,12},{12,8},{16,20},{20,16},{24,28},{28,24},{32,36},... | collective-permute-start | bytes 786440 | tf_op jit(solution)/shard_map/ppermute | solution.py:349
  71.7 4.7 %collective-permute-start.9 = (f32[8,256]{1,0:T(8,128)S(1)}, f32[8,256]{1,0:T(8,128)S(1)}, u32[]{:S(2)}, u32[]{:S(2)}) collective-permute-start(f32[8,256]{1,0:T(8,128)S(1)} %get-tuple-element.42), channel_id=1, source_target_pairs={{0,3},{1,0},{2,1},{3,2},{4,7},{5,4},{6,5},{7,6},{8,11},{9,8},{10,9... | collective-permute-start | bytes 24584 | tf_op jit(solution)/shard_map/ppermute | solution.py:34
  74.8 5.2 %collective-permute-start.8 = (f32[8,256]{1,0:T(8,128)S(1)}, f32[8,256]{1,0:T(8,128)S(1)}, u32[]{:S(2)}, u32[]{:S(2)}) collective-permute-start(f32[8,256]{1,0:T(8,128)S(1)} %get-tuple-element.42), channel_id=1, source_target_pairs={{0,2},{1,3},{2,0},{3,1},{4,6},{5,7},{6,4},{7,5},{8,10},{9,11},{10,... | collective-permute-start | bytes 24584 | tf_op jit(solution)/shard_map/ppermute | solution.py:34
  75.4 4.9 %collective-permute-start.7 = (f32[8,256]{1,0:T(8,128)S(1)}, f32[8,256]{1,0:T(8,128)S(1)}, u32[]{:S(2)}, u32[]{:S(2)}) collective-permute-start(f32[8,256]{1,0:T(8,128)S(1)} %get-tuple-element.42), channel_id=1, source_target_pairs={{0,1},{1,2},{2,3},{3,0},{4,5},{5,6},{6,7},{7,4},{8,9},{9,10},{10,1... | collective-permute-start | bytes 24584 | tf_op jit(solution)/shard_map/ppermute | solution.py:34

commit v8 on v7

--- a/solution.py
+++ b/solution.py
@@ -75,18 +75,6 @@
                 lanes = pl.ds(pl.multiple_of(col + tile * LANES, LANES), LANES)
                 images[start + date, part, tile] = source[date, part, pl.ds(row, rows), lanes].astype(jnp.float32)
 
-    looked[...] = jnp.zeros_like(looked) if earlier is None else earlier[...]
-    quarter = high.shape[1] // tiles
-
-    def multiplied(index, piece):
-        place = pl.ds(pl.multiple_of(piece * quarter, quarter), quarter)
-        chosen = picked[lax.rem(index + steps, steps)]
-        held = lax.rem(index + 2, 2)
-        summed = jnp.dot(high[held, place, :], chosen, preferred_element_type=jnp.float32)
-        summed += jnp.dot(low[held, place, :], chosen, preferred_element_type=jnp.float32)
-        target = jnp.where(index < 0, 2, index // steps)
-        looked[target, place, :] += summed
-
     @pl.loop(0, 2 * steps)
     def _(index):
         half, step_at = index // steps, index % steps
@@ -102,7 +90,6 @@
 
         @pl.loop(0, tiles)
         def _(tile):
-            multiplied(index - 1, tile)
             lanes = pl.ds(pl.multiple_of(tile * LANES, LANES), LANES)
             for date in range(0, group, 2):
                 totals = {}
@@ -130,12 +117,19 @@
                             head = value.astype(jnp.bfloat16)
                             tail = (value - head.astype(jnp.float32)).astype(jnp.bfloat16)
                             start = (part * pair_count + first * group + gap) * looks
-                            high[lax.rem(index, 2), start : start + looks, lanes] = head
-                            low[lax.rem(index, 2), start : start + looks, lanes] = tail
-
-    @pl.loop(0, tiles)
-    def _(piece):
-        multiplied(2 * steps - 1, piece)
+                            high[start : start + looks, lanes] = head
+                            low[start : start + looks, lanes] = tail
+
+        summed = jnp.dot(high[...], picked[step_at], preferred_element_type=jnp.float32)
+        summed += jnp.dot(low[...], picked[step_at], preferred_element_type=jnp.float32)
+
+        @pl.when(step_at == 0)
+        def _():
+            looked[half] = summed if earlier is None else earlier[half] + summed
+
+        @pl.when(step_at > 0)
+        def _():
+            looked[half] += summed
 
     if not final:
         return
@@ -182,12 +176,12 @@
     steps = (stop - start) // STEP
     vmem = pl.BlockSpec(memory_space=pltpu.VMEM)
     in_specs = [vmem] * (3 + len(earlier))
-    looked_shape = (3, 2 * pair_count * looks, looked_cols)
+    looked_shape = (2, 2 * pair_count * looks, looked_cols)
     out_shape = jax.ShapeDtypeStruct(looked_shape, jnp.float32)
     scratch = [
         pltpu.VMEM((2 * group, 2, tiles, rows, LANES), jnp.float32),
-        pltpu.VMEM((2, 2 * pair_count * looks, STEP), jnp.bfloat16),
-        pltpu.VMEM((2, 2 * pair_count * looks, STEP), jnp.bfloat16),
+        pltpu.VMEM((2 * pair_count * looks, STEP), jnp.bfloat16),
+        pltpu.VMEM((2 * pair_count * looks, STEP), jnp.bfloat16),
         pltpu.VMEM((steps, STEP, looked_cols), jnp.bfloat16),
     ]
     if final:

time: 81.5 us -> 81 us (level)
  no operation moved by 1% of the time
where the time goes in v8:
time: 81 us; the launch traced here: 80.5 us
  starting transfers between devices  31.9 us (39%)
  Pallas kernels  17.8 us (22%)
  waiting for transfers between devices  17.2 us (21%)
  local copies, waits for them, and re-layouts  12.5 us (15%)
  other arithmetic  0.95 us (1%)
    pallas_call x2, Pallas kernels, phases(): pl.pallas_call(partial(phase_kernel, start // LOOK_C, stop // LOOK_C, fin...  16.7 us
    all_to_all x1, starting transfers between devices, sent_inverse(): lax.all_to_all(sent.reshape(devices, per, LANES), 'date', split_axis=0, c...  10.7 us
    ppermute x9, starting transfers between devices, passed_along(): return lax.ppermute(value, axis, pairs)  10.6 us
    all_to_all x1, starting transfers between devices, body(): lax.all_to_all(payload.reshape(devices, 1, -1), 'date', split_axis=0, con...  10.3 us
    ppermute x9, waiting for transfers between devices, passed_along(): return lax.ppermute(value, axis, pairs)  7.94 us
    all_to_all x1, waiting for transfers between devices, body(): lax.all_to_all(payload.reshape(devices, 1, -1), 'date', split_axis=0, con...  7.91 us
    slice x2, local copies, waits for them, and re-layouts, parts(): return (images[:, :, :rows, start:stop], images[:, :, rows:, start:stop])  6.21 us
    slice x2, local copies, waits for them, and re-layouts, body(): owned = [late[:, :, :, start:stop] for start, stop in CHUNKS]  4.5 us
  transfers between devices with their start and end apart: 12, of which 6 were waited for; matrix products, arithmetic and copies ran while one was open for 15% of the time, Pallas kernels for 21%

profile of v8, /device:TPU:6, one launch (start us, length us, event | category | flops | bytes accessed | tf_op | source)
XLA Modules:
  0.0 80.5 jit_solution(3792840127943117336)
XLA Ops:
  0.0 0.0 collective-permute-start
  0.0 2.0 %collective-permute-start.1 = (s32[16,32,128]{2,1,0:T(8,128)}, s32[16,32,128]{2,1,0:T(8,128)S(1)}, u32[]{:S(2)}, u32[]{:S(2)}) collective-permute-start(s32[16,32,128]{2,1,0:T(8,128)} %refs_2_.1), channel_id=1, source_target_pairs={{0,4},{4,8},{8,12},{12,16},{16,20},{20,24},{24,28},{28,32},{32,36}... | collective-permute-start | bytes 786440 | tf_op jit(solution)/shard_map/ppermute | solution.py:34
  2.0 3.8 %fusion.9 = (bf16[4,2,64,1536]{3,2,1,0:T(8,128)(2,1)}, bf16[4,2,64,1536]{3,2,1,0:T(8,128)(2,1)}) fusion(bf16[4,2,128,2048]{3,2,1,0:T(8,128)(2,1)} %param.4), kind=kLoop, calls=%fused_computation.24 | loop fusion | bytes 6291456 | tf_op jit(solution)/shard_map/slice | solution.py:311
  5.9 1.2 %collective-permute-done = s32[16,2]{0,1:T(2,128)S(1)} collective-permute-done((s32[16,2]{0,1:T(2,128)}, s32[16,2]{0,1:T(2,128)S(1)}, u32[]{:S(2)}, u32[]{:S(2)}) %collective-permute-start) | collective-permute-done | bytes 160 | tf_op jit(solution)/shard_map/ppermute | solution.py:34
  7.0 2.9 %collective-permute-done.1.refs_3_ = s32[16,32,128]{2,1,0:T(8,128)S(1)} collective-permute-done((s32[16,32,128]{2,1,0:T(8,128)}, s32[16,32,128]{2,1,0:T(8,128)S(1)}, u32[]{:S(2)}, u32[]{:S(2)}) %collective-permute-start.1) | collective-permute-done | bytes 262176 | tf_op jit(solution)/shard_map/ppermute | solution.py:34
  9.9 0.7 copy-done.2
  10.6 0.0 collective-permute-start.4
  10.6 0.5 collective-permute-start.5
  11.1 0.0 copy-done.4
  11.1 0.1 abs_reduce_fusion
  11.2 0.1 convert_bitcast_fusion
  11.3 2.4 %fusion.8 = (bf16[4,2,64,512]{3,2,1,0:T(8,128)(2,1)}, bf16[4,2,64,512]{3,2,1,0:T(8,128)(2,1)}) fusion(bf16[4,2,128,2048]{3,2,1,0:T(8,128)(2,1)} %param.4), kind=kLoop, calls=%fused_computation.23 | loop fusion | bytes 2097152 | tf_op jit(solution)/shard_map/slice | solution.py:311
  13.7 3.3 %collective-permute-start.2 = (bf16[4,2,64,512]{3,2,1,0:T(8,128)(2,1)}, bf16[4,2,64,512]{3,2,1,0:T(8,128)(2,1)}, u32[]{:S(2)}, u32[]{:S(2)}) collective-permute-start(bf16[4,2,64,512]{3,2,1,0:T(8,128)(2,1)} %get-tuple-element.32), channel_id=1, source_target_pairs={{0,252},{4,0},{8,4},{12,8},{16,12},{20,16},{24,20},{28,24},{32,28}... | collective-permute-start | bytes 1572872 | tf_op jit(solution)/shard_map/ppermute | solution.py:34
  17.1 0.0 collective-permute-start.3
  17.1 0.7 broadcast_in_dim.18
  17.8 10.7 %all-to-all-start = ((s32[64,8,128]{2,1,0:T(8,128)}), s32[64,8,128]{2,1,0:T(8,128)S(1)}, u32[]{:S(2)}, u32[]{:S(2)}) async-start(s32[64,8,128]{2,1,0:T(8,128)} %bitcast.6), calls=%async_computation | async-start | bytes 524288 | tf_op jit(solution)/shard_map/all_to_all | solution.py:231
  28.5 2.3 %slice.50.own = bf16[4,2,128,512]{3,2,1,0:T(8,128)(2,1)} slice(bf16[4,2,128,2048]{3,2,1,0:T(8,128)(2,1)} %param.4), slice={[0:4], [0:2], [0:128], [1536:2048]} | slice | bytes 2097152 | tf_op jit(solution)/shard_map/slice | solution.py:334
  30.8 2.2 %slice.49.own = bf16[4,2,128,1536]{3,2,1,0:T(8,128)(2,1)S(1)} slice(bf16[4,2,128,2048]{3,2,1,0:T(8,128)(2,1)} %param.4), slice={[0:4], [0:2], [0:128], [0:1536]} | slice | bytes 6291456 | tf_op jit(solution)/shard_map/slice | solution.py:334
  33.0 0.1 reshape.58
  33.1 0.1 copy.8
  33.2 0.1 pad.4.clone
  33.3 0.1 broadcast_in_dim.15
  33.3 0.0 copy-done.5
  33.3 0.1 pad_add_fusion
  33.4 0.0 copy-start
  33.5 0.0 copy-start.1
  33.5 0.0 collective-permute-done.4.following
  33.5 0.0 collective-permute-done.5.previous
  33.5 11.0 %phases.2.refs_0_ = f32[2,512,128]{2,1,0:T(8,128)S(1)} custom-call(bf16[4,2,128,1536]{3,2,1,0:T(8,128)(2,1)S(1)} %slice.49.own, bf16[4,2,64,1536]{3,2,1,0:T(8,128)(2,1)} %collective-permute-done.4.following, bf16[4,2,64,1536]{3,2,1,0:T(8,128)(2,1)} %collective-permute-done.5.previous), custom_call_target="tpu_custom_call" | custom-call | flops 25165824 | bytes 6291456 | tf_op jit(solution)/shard_map/phases/pallas_call | solution.py:196
  44.5 0.0 collective-permute-done.2.following
  44.6 0.0 collective-permute-done.3.previous
  44.6 0.0 copy-done
  44.6 0.0 copy-done.1
  44.6 0.0 copy-done.3
  44.6 5.7 %phases.3 = s32[320,128]{1,0:T(8,128)} custom-call(bf16[4,2,128,512]{3,2,1,0:T(8,128)(2,1)S(1)} %copy-done, bf16[4,2,64,512]{3,2,1,0:T(8,128)(2,1)} %collective-permute-done.2.following, bf16[4,2,64,512]{3,2,1,0:T(8,128)(2,1)} %collective-permute-done.3.previous, f32[2,512,128]{2,1,0:T(8,128)S(1)} %phases.2.refs_0_, s32[32]{0:T(128)S(1)} %fusion.6.refs_1_, ...), custom_call_target="tpu_custom_call" | custom-call | flops 8388608 | bytes 2097152 | tf_op jit(solution)/shard_map/phases/pallas_call | solution.py:196
  50.3 0.0 all-to-all-done
  50.3 10.3 %all-to-all-start.1 = ((s32[64,1,640]{2,1,0:T(1,128)}), s32[64,1,640]{2,1,0:T(1,128)S(1)}, u32[]{:S(2)}, u32[]{:S(2)}) async-start(s32[64,1,640]{2,1,0:T(1,128)} %bitcast.8), calls=%async_computation.1 | async-start | bytes 327680 | tf_op jit(solution)/shard_map/all_to_all | solution.py:344
  60.7 0.2 collective-permute-start.6
  60.9 1.4 %collective-permute-done.6.swapped = s32[512,128]{1,0:T(8,128)S(1)} collective-permute-done((s32[512,128]{1,0:T(8,128)S(1)}, s32[512,128]{1,0:T(8,128)S(1)}, u32[]{:S(2)}, u32[]{:S(2)}) %collective-permute-start.6) | collective-permute-done | bytes 262176 | tf_op jit(solution)/shard_map/ppermute | solution.py:343
  62.3 7.9 %all-to-all-done.1 = s32[64,1,640]{2,1,0:T(1,128)S(1)} async-done(((s32[64,1,640]{2,1,0:T(1,128)}), s32[64,1,640]{2,1,0:T(1,128)S(1)}, u32[]{:S(2)}, u32[]{:S(2)}) %all-to-all-start.1) | async-done | bytes 163872 | tf_op jit(solution)/shard_map/all_to_all | solution.py:344
  70.2 1.1 %invert.1 = (f32[64,256]{1,0:T(8,128)S(1)}, f32[8,256]{1,0:T(8,128)S(1)}) custom-call(s32[1]{0:T(128)} %bitcast.side, s32[320,128]{1,0:T(8,128)S(1)} %bitcast.28, s32[512,128]{1,0:T(8,128)S(1)} %bitcast.27, s32[512,128]{1,0:T(8,128)S(1)} %collective-permute-done.6.swapped), custom_call_target="tpu_custom_call" | custom-call | tf_op jit(solution)/shard_map/invert/pallas_call | solution.py:285
  71.2 3.1 %collective-permute-start.9 = (f32[8,256]{1,0:T(8,128)S(1)}, f32[8,256]{1,0:T(8,128)S(1)}, u32[]{:S(2)}, u32[]{:S(2)}) collective-permute-start(f32[8,256]{1,0:T(8,128)S(1)} %get-tuple-element.42), channel_id=1, source_target_pairs={{0,3},{1,0},{2,1},{3,2},{4,7},{5,4},{6,5},{7,6},{8,11},{9,8},{10,9... | collective-permute-start | bytes 24584 | tf_op jit(solution)/shard_map/ppermute | solution.py:34
  74.3 0.6 collective-permute-start.8
  75.0 1.0 %collective-permute-start.7 = (f32[8,256]{1,0:T(8,128)S(1)}, f32[8,256]{1,0:T(8,128)S(1)}, u32[]{:S(2)}, u32[]{:S(2)}) collective-permute-start(f32[8,256]{1,0:T(8,128)S(1)} %get-tuple-element.42), channel_id=1, source_target_pairs={{0,1},{1,2},{2,3},{3,0},{4,5},{5,6},{6,7},{7,4},{8,9},{9,10},{10,1... | collective-permute-start | bytes 24584 | tf_op jit(solution)/shard_map/ppermute | solution.py:34
  75.9 0.0 collective-permute-done.9
  75.9 3.5 %collective-permute-done.8 = f32[8,256]{1,0:T(8,128)S(1)} collective-permute-done((f32[8,256]{1,0:T(8,128)S(1)}, f32[8,256]{1,0:T(8,128)S(1)}, u32[]{:S(2)}, u32[]{:S(2)}) %collective-permute-start.8) | collective-permute-done | bytes 8224 | tf_op jit(solution)/shard_map/ppermute | solution.py:34
  79.5 0.3 collective-permute-done.7
  79.8 0.6 subtract_subtract_fusion
  (12 shorter events, 0.1 us)
Async XLA Ops:
  0.0 11.1 %copy-start.4 = (f32[256,16]{0,1:T(8,128)S(1)}, f32[256,16]{0,1:T(8,128)}, u32[]{:S(2)}) copy-start(f32[256,16]{0,1:T(8,128)} %param.7) | copy-start | bytes 49156
  0.0 7.0 %collective-permute-start = (s32[16,2]{0,1:T(2,128)}, s32[16,2]{0,1:T(2,128)S(1)}, u32[]{:S(2)}, u32[]{:S(2)}) collective-permute-start(s32[16,2]{0,1:T(2,128)} %param.5), channel_id=1, source_target_pairs={{0,4},{4,8},{8,12},{12,16},{16,20},{20,24},{24,28},{28,32},{32,36}... | collective-permute-start | bytes 392 | tf_op jit(solution)/shard_map/ppermute | solution.py:34
  0.0 9.9 %collective-permute-start.1 = (s32[16,32,128]{2,1,0:T(8,128)}, s32[16,32,128]{2,1,0:T(8,128)S(1)}, u32[]{:S(2)}, u32[]{:S(2)}) collective-permute-start(s32[16,32,128]{2,1,0:T(8,128)} %refs_2_.1), channel_id=1, source_target_pairs={{0,4},{4,8},{8,12},{12,16},{16,20},{20,24},{24,28},{28,32},{32,36}... | collective-permute-start | bytes 786440 | tf_op jit(solution)/shard_map/ppermute | solution.py:34
  9.9 0.7 copy-start.2
  10.6 22.9 %collective-permute-start.4 = (bf16[4,2,64,1536]{3,2,1,0:T(8,128)(2,1)}, bf16[4,2,64,1536]{3,2,1,0:T(8,128)(2,1)}, u32[]{:S(2)}, u32[]{:S(2)}) collective-permute-start(bf16[4,2,64,1536]{3,2,1,0:T(8,128)(2,1)} %get-tuple-element.35), channel_id=1, source_target_pairs={{0,252},{4,0},{8,4},{12,8},{16,12},{20,16},{24,20},{28,24},{32,28}... | collective-permute-start | bytes 4718600 | tf_op jit(solution)/shard_map/ppermute | solution.py:34
  10.6 22.9 %collective-permute-start.5 = (bf16[4,2,64,1536]{3,2,1,0:T(8,128)(2,1)}, bf16[4,2,64,1536]{3,2,1,0:T(8,128)(2,1)}, u32[]{:S(2)}, u32[]{:S(2)}) collective-permute-start(bf16[4,2,64,1536]{3,2,1,0:T(8,128)(2,1)} %get-tuple-element.36), channel_id=1, source_target_pairs={{0,4},{4,8},{8,12},{12,16},{16,20},{20,24},{24,28},{28,32},{32,36}... | collective-permute-start | bytes 4718600 | tf_op jit(solution)/shard_map/ppermute | solution.py:34
  13.7 30.8 %collective-permute-start.2 = (bf16[4,2,64,512]{3,2,1,0:T(8,128)(2,1)}, bf16[4,2,64,512]{3,2,1,0:T(8,128)(2,1)}, u32[]{:S(2)}, u32[]{:S(2)}) collective-permute-start(bf16[4,2,64,512]{3,2,1,0:T(8,128)(2,1)} %get-tuple-element.32), channel_id=1, source_target_pairs={{0,252},{4,0},{8,4},{12,8},{16,12},{20,16},{24,20},{28,24},{32,28}... | collective-permute-start | bytes 1572872 | tf_op jit(solution)/shard_map/ppermute | solution.py:34
  17.1 27.5 %collective-permute-start.3 = (bf16[4,2,64,512]{3,2,1,0:T(8,128)(2,1)}, bf16[4,2,64,512]{3,2,1,0:T(8,128)(2,1)}, u32[]{:S(2)}, u32[]{:S(2)}) collective-permute-start(bf16[4,2,64,512]{3,2,1,0:T(8,128)(2,1)} %get-tuple-element.33), channel_id=1, source_target_pairs={{0,4},{4,8},{8,12},{12,16},{16,20},{20,24},{24,28},{28,32},{32,36}... | collective-permute-start | bytes 1572872 | tf_op jit(solution)/shard_map/ppermute | solution.py:34
  17.8 32.5 %all-to-all-start = ((s32[64,8,128]{2,1,0:T(8,128)}), s32[64,8,128]{2,1,0:T(8,128)S(1)}, u32[]{:S(2)}, u32[]{:S(2)}) async-start(s32[64,8,128]{2,1,0:T(8,128)} %bitcast.6), calls=%async_computation | async-start | bytes 524288 | tf_op jit(solution)/shard_map/all_to_all | solution.py:231
  30.8 2.6 %copy-start.5 = (s32[16,2]{0,1:T(2,128)S(1)}, s32[16,2]{0,1:T(2,128)}, u32[]{:S(2)}) copy-start(s32[16,2]{0,1:T(2,128)} %param.5) | copy-start | bytes 388
  33.4 11.1 %copy-start = (bf16[4,2,128,512]{3,2,1,0:T(8,128)(2,1)S(1)}, bf16[4,2,128,512]{3,2,1,0:T(8,128)(2,1)}, u32[]{:S(2)}) copy-start(bf16[4,2,128,512]{3,2,1,0:T(8,128)(2,1)} %slice.50.own) | copy-start | bytes 3145732
  33.5 11.1 %copy-start.1 = (s32[16,32,128]{2,1,0:T(8,128)S(1)}, s32[16,32,128]{2,1,0:T(8,128)}, u32[]{:S(2)}) copy-start(s32[16,32,128]{2,1,0:T(8,128)} %refs_2_.1) | copy-start | bytes 786436
  33.5 11.1 %copy-start.3 = (s32[16,32,128]{2,1,0:T(8,128)S(1)}, s32[16,32,128]{2,1,0:T(8,128)}, u32[]{:S(2)}) copy-start(s32[16,32,128]{2,1,0:T(8,128)} %copy-done.2) | copy-start | bytes 786436
  50.3 19.9 %all-to-all-start.1 = ((s32[64,1,640]{2,1,0:T(1,128)}), s32[64,1,640]{2,1,0:T(1,128)S(1)}, u32[]{:S(2)}, u32[]{:S(2)}) async-start(s32[64,1,640]{2,1,0:T(1,128)} %bitcast.8), calls=%async_computation.1 | async-start | bytes 327680 | tf_op jit(solution)/shard_map/all_to_all | solution.py:344
  60.7 1.6 %collective-permute-start.6 = (s32[512,128]{1,0:T(8,128)S(1)}, s32[512,128]{1,0:T(8,128)S(1)}, u32[]{:S(2)}, u32[]{:S(2)}) collective-permute-start(s32[512,128]{1,0:T(8,128)S(1)} %bitcast.26), channel_id=1, source_target_pairs={{0,4},{4,0},{8,12},{12,8},{16,20},{20,16},{24,28},{28,24},{32,36},... | collective-permute-start | bytes 786440 | tf_op jit(solution)/shard_map/ppermute | solution.py:343
  71.2 4.7 %collective-permute-start.9 = (f32[8,256]{1,0:T(8,128)S(1)}, f32[8,256]{1,0:T(8,128)S(1)}, u32[]{:S(2)}, u32[]{:S(2)}) collective-permute-start(f32[8,256]{1,0:T(8,128)S(1)} %get-tuple-element.42), channel_id=1, source_target_pairs={{0,3},{1,0},{2,1},{3,2},{4,7},{5,4},{6,5},{7,6},{8,11},{9,8},{10,9... | collective-permute-start | bytes 24584 | tf_op jit(solution)/shard_map/ppermute | solution.py:34
  74.3 5.2 %collective-permute-start.8 = (f32[8,256]{1,0:T(8,128)S(1)}, f32[8,256]{1,0:T(8,128)S(1)}, u32[]{:S(2)}, u32[]{:S(2)}) collective-permute-start(f32[8,256]{1,0:T(8,128)S(1)} %get-tuple-element.42), channel_id=1, source_target_pairs={{0,2},{1,3},{2,0},{3,1},{4,6},{5,7},{6,4},{7,5},{8,10},{9,11},{10,... | collective-permute-start | bytes 24584 | tf_op jit(solution)/shard_map/ppermute | solution.py:34
  75.0 4.9 %collective-permute-start.7 = (f32[8,256]{1,0:T(8,128)S(1)}, f32[8,256]{1,0:T(8,128)S(1)}, u32[]{:S(2)}, u32[]{:S(2)}) collective-permute-start(f32[8,256]{1,0:T(8,128)S(1)} %get-tuple-element.42), channel_id=1, source_target_pairs={{0,1},{1,2},{2,3},{3,0},{4,5},{5,6},{6,7},{7,4},{8,9},{9,10},{10,1... | collective-permute-start | bytes 24584 | tf_op jit(solution)/shard_map/ppermute | solution.py:34

commit v9 on v8

--- a/solution.py
+++ b/solution.py
@@ -48,19 +48,32 @@
     return jnp.where(y < 0.0, -value, value)
 
 
-def phase_kernel(first_col, last, final, own, following, previous, *refs):
+def phase_kernel(first_col, last, sides, final, own, *refs):
     refs = list(refs)
-    earlier = refs.pop(0) if first_col else None
+    others = [refs.pop(0) for _ in sides]
+    earlier = [refs.pop(0) for _ in sides] if first_col else None
     if final:
-        combos, high_cycles, low_cycles, line, payload, images, high, low, picked, looked, cycles, sums, words = refs
+        combos, high_cycles, low_cycles, line, payload, held, arrived, images, high, low, picked = refs[:11]
+        looked, cycles, sums, words = refs[11:]
     else:
-        looked, images, high, low, picked = refs
-    group, _, rows, _ = following.shape
+        looked, held, arrived, images, high, low, picked = refs
+    group, _, rows, _ = others[0].shape
     steps, width, _ = picked.shape
     looks = rows // LOOK_R
     pair_count = group * group
     step_cols = width // LOOK_C
     tiles = width // LANES
+    copies = [
+        pltpu.make_async_copy(
+            other.at[:, :, :, pl.ds(step * width, width)],
+            held.at[at * steps + step],
+            arrived.at[at * steps + step],
+        )
+        for at, other in enumerate(others)
+        for step in range(steps)
+    ]
+    for copy in copies:
+        copy.start()
     for step in range(steps):
         shape = picked.shape[1:]
         of = lax.broadcasted_iota(jnp.int32, shape, 0) // LOOK_C + first_col + step * step_cols
@@ -75,18 +88,14 @@
                 lanes = pl.ds(pl.multiple_of(col + tile * LANES, LANES), LANES)
                 images[start + date, part, tile] = source[date, part, pl.ds(row, rows), lanes].astype(jnp.float32)
 
-    @pl.loop(0, 2 * steps)
+    @pl.loop(0, len(sides) * steps)
     def _(index):
-        half, step_at = index // steps, index % steps
+        at, step_at = index // steps, index % steps
+        half = at + sides[0]
         widen(own, half * group, pl.multiple_of(half * rows, rows), step_at * width)
-
-        @pl.when(half == 0)
-        def _():
-            widen(following, group, 0, step_at * width)
-
-        @pl.when(half == 1)
-        def _():
-            widen(previous, 0, 0, step_at * width)
+        for piece, copy in enumerate(copies):
+            pl.when(index == piece)(copy.wait)
+        widen(held.at[index], (1 - half) * group, 0, 0)
 
         @pl.loop(0, tiles)
         def _(tile):
@@ -95,9 +104,9 @@
                 totals = {}
                 for block in range(looks // 8):
                     for step in range(LOOK_R):
-                        at = pl.ds(block * 8 * LOOK_R + step, 8, stride=LOOK_R)
+                        lines = pl.ds(block * 8 * LOOK_R + step, 8, stride=LOOK_R)
                         seen = {
-                            image: [images[image, part, tile, at, :] for part in range(2)]
+                            image: [images[image, part, tile, lines, :] for part in range(2)]
                             for image in range(date, date + group + 2)
                         }
                         for first in range(date, date + 2):
@@ -123,13 +132,15 @@
         summed = jnp.dot(high[...], picked[step_at], preferred_element_type=jnp.float32)
         summed += jnp.dot(low[...], picked[step_at], preferred_element_type=jnp.float32)
 
-        @pl.when(step_at == 0)
-        def _():
-            looked[half] = summed if earlier is None else earlier[half] + summed
+        for place in range(len(sides)):
+
+            @pl.when(index == place * steps)
+            def _(place=place):
+                looked[place] = summed if earlier is None else earlier[place][0] + summed
 
         @pl.when(step_at > 0)
         def _():
-            looked[half] += summed
+            looked[at] += summed
 
     if not final:
         return
@@ -166,7 +177,7 @@
     payload[pl.ds(4, last // 2, stride=MESSAGE), :] = jnp.broadcast_to(full, (last // 2, LANES))
 
 
-def phases(start, stop, final, own, following, previous, earlier, *rest):
+def phases(start, stop, sides, final, own, others, earlier, *rest):
     group, _, height, _ = own.shape
     rows = height // 2
     looked_cols = LANES
@@ -175,10 +186,12 @@
     pair_count = group * group
     steps = (stop - start) // STEP
     vmem = pl.BlockSpec(memory_space=pltpu.VMEM)
-    in_specs = [vmem] * (3 + len(earlier))
-    looked_shape = (2, 2 * pair_count * looks, looked_cols)
+    in_specs = [vmem] + [pl.BlockSpec(memory_space=pl.ANY)] * len(others) + [vmem] * len(earlier)
+    looked_shape = (len(sides), 2 * pair_count * looks, looked_cols)
     out_shape = jax.ShapeDtypeStruct(looked_shape, jnp.float32)
     scratch = [
+        pltpu.VMEM((len(sides) * steps, group, 2, rows, STEP), jnp.bfloat16),
+        pltpu.SemaphoreType.DMA((len(sides) * steps,)),
         pltpu.VMEM((2 * group, 2, tiles, rows, LANES), jnp.float32),
         pltpu.VMEM((2 * pair_count * looks, STEP), jnp.bfloat16),
         pltpu.VMEM((2 * pair_count * looks, STEP), jnp.bfloat16),
@@ -194,19 +207,19 @@
             pltpu.VMEM((looked_cols, LANES), jnp.int32),
         ]
     return pl.pallas_call(
-        partial(phase_kernel, start // LOOK_C, stop // LOOK_C, final),
+        partial(phase_kernel, start // LOOK_C, stop // LOOK_C, sides, final),
         in_specs=in_specs,
         out_specs=vmem,
         out_shape=out_shape,
         scratch_shapes=scratch,
         compiler_params=pltpu.CompilerParams(vmem_limit_bytes=16 << 20),
         cost_estimate=pl.CostEstimate(
-            flops=8 * pair_count * height * (stop - start),
+            flops=8 * pair_count * rows * len(sides) * (stop - start),
             bytes_accessed=group * 4 * height * (stop - start) * 2,
             transcendentals=0,
         ),
         name="phases",
-    )(own, following, previous, *earlier, *rest)
+    )(own, *others, *earlier, *rest)
 
 
 def coded_inverse(inverse):
@@ -334,12 +347,17 @@
     owned = [late[:, :, :, start:stop] for start, stop in CHUNKS]
     owned, combos = lax.optimization_barrier((owned, combos))
     looked = ()
-    for (start, stop), own, (following, previous) in zip(CHUNKS, owned, others):
-        final = stop == width
-        rest = (combos, cycle_maps, low_cycles, line) if final else ()
-        looked = (phases(start, stop, final, own, following, previous, looked, *rest),)
-
-    payload, kept = lax.optimization_barrier((looked[0], kept))
+    for (start, stop), own, received in zip(CHUNKS, owned, others):
+        if stop < width:
+            upper = phases(start, stop, (0,), False, own, received[:1], looked[:1])
+            lower, upper = lax.optimization_barrier((received[1:], upper))
+            looked = [upper, phases(start, stop, (1,), False, own, lower, looked[1:])]
+        else:
+            payload = phases(
+                start, stop, (0, 1), True, own, received, looked, combos, cycle_maps, low_cycles, line
+            )
+
+    payload, kept = lax.optimization_barrier((payload, kept))
     swapped = lax.ppermute(kept, "date", [(at, at ^ 1) for at in range(devices)])
     received = lax.all_to_all(
         payload.reshape(devices, 1, -1), "date", split_axis=0, concat_axis=0, tiled=True

time: 81 us -> 81.1 us (level)
    pallas_call x2 -> x3, Pallas kernels: 16.7 us -> 16.8 us  [phases(): pl.pallas_call(partial(phase_kernel, start // LOOK_C, stop // LOOK_C, sid...]
where the time goes in v9:
time: 81.1 us; the launch traced here: 80.5 us
  starting transfers between devices  31.9 us (39%)
  Pallas kernels  17.8 us (22%)
  waiting for transfers between devices  17.2 us (21%)
  local copies, waits for them, and re-layouts  12.5 us (15%)
  other arithmetic  0.95 us (1%)
    pallas_call x3, Pallas kernels, phases(): pl.pallas_call(partial(phase_kernel, start // LOOK_C, stop // LOOK_C, sid...  16.8 us
    all_to_all x1, starting transfers between devices, sent_inverse(): lax.all_to_all(sent.reshape(devices, per, LANES), 'date', split_axis=0, c...  10.7 us
    ppermute x9, starting transfers between devices, passed_along(): return lax.ppermute(value, axis, pairs)  10.6 us
    all_to_all x1, starting transfers between devices, body(): lax.all_to_all(payload.reshape(devices, 1, -1), 'date', split_axis=0, con...  10.3 us
    ppermute x9, waiting for transfers between devices, passed_along(): return lax.ppermute(value, axis, pairs)  7.94 us
    all_to_all x1, waiting for transfers between devices, body(): lax.all_to_all(payload.reshape(devices, 1, -1), 'date', split_axis=0, con...  7.91 us
    slice x2, local copies, waits for them, and re-layouts, parts(): return (images[:, :, :rows, start:stop], images[:, :, rows:, start:stop])  6.21 us
    slice x2, local copies, waits for them, and re-layouts, body(): owned = [late[:, :, :, start:stop] for start, stop in CHUNKS]  4.5 us
  transfers between devices with their start and end apart: 12, of which 6 were waited for; matrix products, arithmetic and copies ran while one was open for 15% of the time, Pallas kernels for 21%

profile of v9, /device:TPU:6, one launch (start us, length us, event | category | flops | bytes accessed | tf_op | source)
XLA Modules:
  0.0 80.5 jit_solution(674259373186781202)
XLA Ops:
  0.0 0.0 collective-permute-start
  0.0 2.0 %collective-permute-start.1 = (s32[16,32,128]{2,1,0:T(8,128)}, s32[16,32,128]{2,1,0:T(8,128)S(1)}, u32[]{:S(2)}, u32[]{:S(2)}) collective-permute-start(s32[16,32,128]{2,1,0:T(8,128)} %refs_5_.1), channel_id=1, source_target_pairs={{0,4},{4,8},{8,12},{12,16},{16,20},{20,24},{24,28},{28,32},{32,36}... | collective-permute-start | bytes 786440 | tf_op jit(solution)/shard_map/ppermute | solution.py:34
  2.0 3.8 %fusion.9 = (bf16[4,2,64,1536]{3,2,1,0:T(8,128)(2,1)}, bf16[4,2,64,1536]{3,2,1,0:T(8,128)(2,1)}) fusion(bf16[4,2,128,2048]{3,2,1,0:T(8,128)(2,1)} %param.4), kind=kLoop, calls=%fused_computation.24 | loop fusion | bytes 6291456 | tf_op jit(solution)/shard_map/slice | solution.py:324
  5.9 1.2 %collective-permute-done = s32[16,2]{0,1:T(2,128)S(1)} collective-permute-done((s32[16,2]{0,1:T(2,128)}, s32[16,2]{0,1:T(2,128)S(1)}, u32[]{:S(2)}, u32[]{:S(2)}) %collective-permute-start) | collective-permute-done | bytes 160 | tf_op jit(solution)/shard_map/ppermute | solution.py:34
  7.0 2.9 %collective-permute-done.1.refs_6_ = s32[16,32,128]{2,1,0:T(8,128)S(1)} collective-permute-done((s32[16,32,128]{2,1,0:T(8,128)}, s32[16,32,128]{2,1,0:T(8,128)S(1)}, u32[]{:S(2)}, u32[]{:S(2)}) %collective-permute-start.1) | collective-permute-done | bytes 262176 | tf_op jit(solution)/shard_map/ppermute | solution.py:34
  9.9 0.7 copy-done.2
  10.6 0.0 collective-permute-start.5
  10.6 0.5 collective-permute-start.4
  11.1 0.0 copy-done.4
  11.1 0.1 abs_reduce_fusion
  11.2 0.1 convert_bitcast_fusion
  11.3 2.4 %fusion.8 = (bf16[4,2,64,512]{3,2,1,0:T(8,128)(2,1)}, bf16[4,2,64,512]{3,2,1,0:T(8,128)(2,1)}) fusion(bf16[4,2,128,2048]{3,2,1,0:T(8,128)(2,1)} %param.4), kind=kLoop, calls=%fused_computation.23 | loop fusion | bytes 2097152 | tf_op jit(solution)/shard_map/slice | solution.py:324
  13.7 3.3 %collective-permute-start.2 = (bf16[4,2,64,512]{3,2,1,0:T(8,128)(2,1)}, bf16[4,2,64,512]{3,2,1,0:T(8,128)(2,1)}, u32[]{:S(2)}, u32[]{:S(2)}) collective-permute-start(bf16[4,2,64,512]{3,2,1,0:T(8,128)(2,1)} %get-tuple-element.34), channel_id=1, source_target_pairs={{0,252},{4,0},{8,4},{12,8},{16,12},{20,16},{24,20},{28,24},{32,28}... | collective-permute-start | bytes 1572872 | tf_op jit(solution)/shard_map/ppermute | solution.py:34
  17.1 0.0 collective-permute-start.3
  17.1 0.7 broadcast_in_dim.18
  17.8 10.7 %all-to-all-start = ((s32[64,8,128]{2,1,0:T(8,128)}), s32[64,8,128]{2,1,0:T(8,128)S(1)}, u32[]{:S(2)}, u32[]{:S(2)}) async-start(s32[64,8,128]{2,1,0:T(8,128)} %bitcast.6), calls=%async_computation | async-start | bytes 524288 | tf_op jit(solution)/shard_map/all_to_all | solution.py:244
  28.5 2.3 %slice.50.own = bf16[4,2,128,512]{3,2,1,0:T(8,128)(2,1)} slice(bf16[4,2,128,2048]{3,2,1,0:T(8,128)(2,1)} %param.4), slice={[0:4], [0:2], [0:128], [1536:2048]} | slice | bytes 2097152 | tf_op jit(solution)/shard_map/slice | solution.py:347
  30.8 2.2 %slice.49.own = bf16[4,2,128,1536]{3,2,1,0:T(8,128)(2,1)S(1)} slice(bf16[4,2,128,2048]{3,2,1,0:T(8,128)(2,1)} %param.4), slice={[0:4], [0:2], [0:128], [0:1536]} | slice | bytes 6291456 | tf_op jit(solution)/shard_map/slice | solution.py:347
  33.0 0.1 reshape.58
  33.1 0.1 copy.8
  33.2 0.1 pad.4.clone
  33.3 0.1 broadcast_in_dim.15
  33.3 0.0 copy-done.5
  33.3 0.1 pad_add_fusion
  33.4 0.0 collective-permute-done.5.refs_0_
  33.5 5.4 %phases.3.refs_2_ = f32[1,512,128]{2,1,0:T(8,128)S(1)} custom-call(bf16[4,2,128,1536]{3,2,1,0:T(8,128)(2,1)S(1)} %slice.49.own, bf16[4,2,64,1536]{3,2,1,0:T(8,128)(2,1)} %collective-permute-done.5.refs_0_), custom_call_target="tpu_custom_call" | custom-call | flops 12582912 | bytes 6291456 | tf_op jit(solution)/shard_map/phases/pallas_call | solution.py:209
  38.8 0.0 copy-start.1
  38.9 0.0 collective-permute-done.4.refs_0_
  38.9 5.5 %phases.4.refs_3_ = f32[1,512,128]{2,1,0:T(8,128)S(1)} custom-call(bf16[4,2,128,1536]{3,2,1,0:T(8,128)(2,1)S(1)} %slice.49.own, bf16[4,2,64,1536]{3,2,1,0:T(8,128)(2,1)} %collective-permute-done.4.refs_0_), custom_call_target="tpu_custom_call" | custom-call | flops 12582912 | bytes 6291456 | tf_op jit(solution)/shard_map/phases/pallas_call | solution.py:209
  44.4 0.0 collective-permute-done.2.refs_0_
  44.4 0.0 collective-permute-done.3.refs_1_
  44.4 0.0 copy-done
  44.4 0.0 copy-done.1
  44.4 0.0 copy-done.3
  44.4 5.9 %phases.5 = s32[320,128]{1,0:T(8,128)} custom-call(bf16[4,2,128,512]{3,2,1,0:T(8,128)(2,1)S(1)} %copy-done, bf16[4,2,64,512]{3,2,1,0:T(8,128)(2,1)} %collective-permute-done.2.refs_0_, bf16[4,2,64,512]{3,2,1,0:T(8,128)(2,1)} %collective-permute-done.3.refs_1_, f32[1,512,128]{2,1,0:T(8,128)S(1)} %phases.3.refs_2_, f32[1,512,128]{2,1,0:T(8,128)S(1)} %phases.4.refs_3_, ...), custom_call_target="tpu_custom_call" | custom-call | flops 8388608 | bytes 2097152 | tf_op jit(solution)/shard_map/phases/pallas_call | solution.py:209
  50.4 0.0 all-to-all-done
  50.4 10.3 %all-to-all-start.1 = ((s32[64,1,640]{2,1,0:T(1,128)}), s32[64,1,640]{2,1,0:T(1,128)S(1)}, u32[]{:S(2)}, u32[]{:S(2)}) async-start(s32[64,1,640]{2,1,0:T(1,128)} %bitcast.8), calls=%async_computation.1 | async-start | bytes 327680 | tf_op jit(solution)/shard_map/all_to_all | solution.py:362
  60.7 0.2 collective-permute-start.6
  61.0 1.4 %collective-permute-done.6.swapped = s32[512,128]{1,0:T(8,128)S(1)} collective-permute-done((s32[512,128]{1,0:T(8,128)S(1)}, s32[512,128]{1,0:T(8,128)S(1)}, u32[]{:S(2)}, u32[]{:S(2)}) %collective-permute-start.6) | collective-permute-done | bytes 262176 | tf_op jit(solution)/shard_map/ppermute | solution.py:361
  62.3 7.9 %all-to-all-done.1 = s32[64,1,640]{2,1,0:T(1,128)S(1)} async-done(((s32[64,1,640]{2,1,0:T(1,128)}), s32[64,1,640]{2,1,0:T(1,128)S(1)}, u32[]{:S(2)}, u32[]{:S(2)}) %all-to-all-start.1) | async-done | bytes 163872 | tf_op jit(solution)/shard_map/all_to_all | solution.py:362
  70.3 1.1 %invert.1 = (f32[64,256]{1,0:T(8,128)S(1)}, f32[8,256]{1,0:T(8,128)S(1)}) custom-call(s32[1]{0:T(128)} %bitcast.side, s32[320,128]{1,0:T(8,128)S(1)} %bitcast.28, s32[512,128]{1,0:T(8,128)S(1)} %bitcast.27, s32[512,128]{1,0:T(8,128)S(1)} %collective-permute-done.6.swapped), custom_call_target="tpu_custom_call" | custom-call | tf_op jit(solution)/shard_map/invert/pallas_call | solution.py:298
  71.3 3.1 %collective-permute-start.9 = (f32[8,256]{1,0:T(8,128)S(1)}, f32[8,256]{1,0:T(8,128)S(1)}, u32[]{:S(2)}, u32[]{:S(2)}) collective-permute-start(f32[8,256]{1,0:T(8,128)S(1)} %get-tuple-element.46), channel_id=1, source_target_pairs={{0,3},{1,0},{2,1},{3,2},{4,7},{5,4},{6,5},{7,6},{8,11},{9,8},{10,9... | collective-permute-start | bytes 24584 | tf_op jit(solution)/shard_map/ppermute | solution.py:34
  74.4 0.6 collective-permute-start.8
  75.0 1.0 %collective-permute-start.7 = (f32[8,256]{1,0:T(8,128)S(1)}, f32[8,256]{1,0:T(8,128)S(1)}, u32[]{:S(2)}, u32[]{:S(2)}) collective-permute-start(f32[8,256]{1,0:T(8,128)S(1)} %get-tuple-element.46), channel_id=1, source_target_pairs={{0,1},{1,2},{2,3},{3,0},{4,5},{5,6},{6,7},{7,4},{8,9},{9,10},{10,1... | collective-permute-start | bytes 24584 | tf_op jit(solution)/shard_map/ppermute | solution.py:34
  76.0 0.0 collective-permute-done.9
  76.0 3.5 %collective-permute-done.8 = f32[8,256]{1,0:T(8,128)S(1)} collective-permute-done((f32[8,256]{1,0:T(8,128)S(1)}, f32[8,256]{1,0:T(8,128)S(1)}, u32[]{:S(2)}, u32[]{:S(2)}) %collective-permute-start.8) | collective-permute-done | bytes 8224 | tf_op jit(solution)/shard_map/ppermute | solution.py:34
  79.6 0.3 collective-permute-done.7
  79.9 0.6 subtract_subtract_fusion
  (13 shorter events, 0.1 us)
Async XLA Ops:
  0.0 11.1 %copy-start.4 = (f32[256,16]{0,1:T(8,128)S(1)}, f32[256,16]{0,1:T(8,128)}, u32[]{:S(2)}) copy-start(f32[256,16]{0,1:T(8,128)} %param.7) | copy-start | bytes 49156
  0.0 7.0 %collective-permute-start = (s32[16,2]{0,1:T(2,128)}, s32[16,2]{0,1:T(2,128)S(1)}, u32[]{:S(2)}, u32[]{:S(2)}) collective-permute-start(s32[16,2]{0,1:T(2,128)} %param.5), channel_id=1, source_target_pairs={{0,4},{4,8},{8,12},{12,16},{16,20},{20,24},{24,28},{28,32},{32,36}... | collective-permute-start | bytes 392 | tf_op jit(solution)/shard_map/ppermute | solution.py:34
  0.0 9.9 %collective-permute-start.1 = (s32[16,32,128]{2,1,0:T(8,128)}, s32[16,32,128]{2,1,0:T(8,128)S(1)}, u32[]{:S(2)}, u32[]{:S(2)}) collective-permute-start(s32[16,32,128]{2,1,0:T(8,128)} %refs_5_.1), channel_id=1, source_target_pairs={{0,4},{4,8},{8,12},{12,16},{16,20},{20,24},{24,28},{28,32},{32,36}... | collective-permute-start | bytes 786440 | tf_op jit(solution)/shard_map/ppermute | solution.py:34
  9.9 0.7 copy-start.2
  10.6 22.8 %collective-permute-start.5 = (bf16[4,2,64,1536]{3,2,1,0:T(8,128)(2,1)}, bf16[4,2,64,1536]{3,2,1,0:T(8,128)(2,1)}, u32[]{:S(2)}, u32[]{:S(2)}) collective-permute-start(bf16[4,2,64,1536]{3,2,1,0:T(8,128)(2,1)} %get-tuple-element.38), channel_id=1, source_target_pairs={{0,252},{4,0},{8,4},{12,8},{16,12},{20,16},{24,20},{28,24},{32,28}... | collective-permute-start | bytes 4718600 | tf_op jit(solution)/shard_map/ppermute | solution.py:34
  10.6 28.3 %collective-permute-start.4 = (bf16[4,2,64,1536]{3,2,1,0:T(8,128)(2,1)}, bf16[4,2,64,1536]{3,2,1,0:T(8,128)(2,1)}, u32[]{:S(2)}, u32[]{:S(2)}) collective-permute-start(bf16[4,2,64,1536]{3,2,1,0:T(8,128)(2,1)} %get-tuple-element.36), channel_id=1, source_target_pairs={{0,4},{4,8},{8,12},{12,16},{16,20},{20,24},{24,28},{28,32},{32,36}... | collective-permute-start | bytes 4718600 | tf_op jit(solution)/shard_map/ppermute | solution.py:34
  13.7 30.7 %collective-permute-start.2 = (bf16[4,2,64,512]{3,2,1,0:T(8,128)(2,1)}, bf16[4,2,64,512]{3,2,1,0:T(8,128)(2,1)}, u32[]{:S(2)}, u32[]{:S(2)}) collective-permute-start(bf16[4,2,64,512]{3,2,1,0:T(8,128)(2,1)} %get-tuple-element.34), channel_id=1, source_target_pairs={{0,252},{4,0},{8,4},{12,8},{16,12},{20,16},{24,20},{28,24},{32,28}... | collective-permute-start | bytes 1572872 | tf_op jit(solution)/shard_map/ppermute | solution.py:34
  17.1 27.3 %collective-permute-start.3 = (bf16[4,2,64,512]{3,2,1,0:T(8,128)(2,1)}, bf16[4,2,64,512]{3,2,1,0:T(8,128)(2,1)}, u32[]{:S(2)}, u32[]{:S(2)}) collective-permute-start(bf16[4,2,64,512]{3,2,1,0:T(8,128)(2,1)} %get-tuple-element.35), channel_id=1, source_target_pairs={{0,4},{4,8},{8,12},{12,16},{16,20},{20,24},{24,28},{28,32},{32,36}... | collective-permute-start | bytes 1572872 | tf_op jit(solution)/shard_map/ppermute | solution.py:34
  17.8 32.6 %all-to-all-start = ((s32[64,8,128]{2,1,0:T(8,128)}), s32[64,8,128]{2,1,0:T(8,128)S(1)}, u32[]{:S(2)}, u32[]{:S(2)}) async-start(s32[64,8,128]{2,1,0:T(8,128)} %bitcast.6), calls=%async_computation | async-start | bytes 524288 | tf_op jit(solution)/shard_map/all_to_all | solution.py:244
  30.8 2.6 %copy-start.5 = (s32[16,2]{0,1:T(2,128)S(1)}, s32[16,2]{0,1:T(2,128)}, u32[]{:S(2)}) copy-start(s32[16,2]{0,1:T(2,128)} %param.5) | copy-start | bytes 388
  38.8 5.6 %copy-start = (bf16[4,2,128,512]{3,2,1,0:T(8,128)(2,1)S(1)}, bf16[4,2,128,512]{3,2,1,0:T(8,128)(2,1)}, u32[]{:S(2)}) copy-start(bf16[4,2,128,512]{3,2,1,0:T(8,128)(2,1)} %slice.50.own) | copy-start | bytes 3145732
  38.8 5.6 %copy-start.1 = (s32[16,32,128]{2,1,0:T(8,128)S(1)}, s32[16,32,128]{2,1,0:T(8,128)}, u32[]{:S(2)}) copy-start(s32[16,32,128]{2,1,0:T(8,128)} %refs_5_.1) | copy-start | bytes 786436
  38.8 5.6 %copy-start.3 = (s32[16,32,128]{2,1,0:T(8,128)S(1)}, s32[16,32,128]{2,1,0:T(8,128)}, u32[]{:S(2)}) copy-start(s32[16,32,128]{2,1,0:T(8,128)} %copy-done.2) | copy-start | bytes 786436
  50.4 19.9 %all-to-all-start.1 = ((s32[64,1,640]{2,1,0:T(1,128)}), s32[64,1,640]{2,1,0:T(1,128)S(1)}, u32[]{:S(2)}, u32[]{:S(2)}) async-start(s32[64,1,640]{2,1,0:T(1,128)} %bitcast.8), calls=%async_computation.1 | async-start | bytes 327680 | tf_op jit(solution)/shard_map/all_to_all | solution.py:362
  60.7 1.6 %collective-permute-start.6 = (s32[512,128]{1,0:T(8,128)S(1)}, s32[512,128]{1,0:T(8,128)S(1)}, u32[]{:S(2)}, u32[]{:S(2)}) collective-permute-start(s32[512,128]{1,0:T(8,128)S(1)} %bitcast.26), channel_id=1, source_target_pairs={{0,4},{4,0},{8,12},{12,8},{16,20},{20,16},{24,28},{28,24},{32,36},... | collective-permute-start | bytes 786440 | tf_op jit(solution)/shard_map/ppermute | solution.py:361
  71.3 4.7 %collective-permute-start.9 = (f32[8,256]{1,0:T(8,128)S(1)}, f32[8,256]{1,0:T(8,128)S(1)}, u32[]{:S(2)}, u32[]{:S(2)}) collective-permute-start(f32[8,256]{1,0:T(8,128)S(1)} %get-tuple-element.46), channel_id=1, source_target_pairs={{0,3},{1,0},{2,1},{3,2},{4,7},{5,4},{6,5},{7,6},{8,11},{9,8},{10,9... | collective-permute-start | bytes 24584 | tf_op jit(solution)/shard_map/ppermute | solution.py:34
  74.4 5.2 %collective-permute-start.8 = (f32[8,256]{1,0:T(8,128)S(1)}, f32[8,256]{1,0:T(8,128)S(1)}, u32[]{:S(2)}, u32[]{:S(2)}) collective-permute-start(f32[8,256]{1,0:T(8,128)S(1)} %get-tuple-element.46), channel_id=1, source_target_pairs={{0,2},{1,3},{2,0},{3,1},{4,6},{5,7},{6,4},{7,5},{8,10},{9,11},{10,... | collective-permute-start | bytes 24584 | tf_op jit(solution)/shard_map/ppermute | solution.py:34
  75.0 4.9 %collective-permute-start.7 = (f32[8,256]{1,0:T(8,128)S(1)}, f32[8,256]{1,0:T(8,128)S(1)}, u32[]{:S(2)}, u32[]{:S(2)}) collective-permute-start(f32[8,256]{1,0:T(8,128)S(1)} %get-tuple-element.46), channel_id=1, source_target_pairs={{0,1},{1,2},{2,3},{3,0},{4,5},{5,6},{6,7},{7,4},{8,9},{9,10},{10,1... | collective-permute-start | bytes 24584 | tf_op jit(solution)/shard_map/ppermute | solution.py:34

commit v10 on v9

--- a/solution.py
+++ b/solution.py
@@ -53,6 +53,7 @@
     others = [refs.pop(0) for _ in sides]
     earlier = [refs.pop(0) for _ in sides] if first_col else None
     if final:
+        finished = refs.pop(0)
         combos, high_cycles, low_cycles, line, payload, held, arrived, images, high, low, picked = refs[:11]
         looked, cycles, sums, words = refs[11:]
     else:
@@ -74,6 +75,9 @@
     ]
     for copy in copies:
         copy.start()
+    shift = sides[0] if final else 0
+    if final:
+        looked[0] = finished[0]
     for step in range(steps):
         shape = picked.shape[1:]
         of = lax.broadcasted_iota(jnp.int32, shape, 0) // LOOK_C + first_col + step * step_cols
@@ -136,11 +140,11 @@
 
             @pl.when(index == place * steps)
             def _(place=place):
-                looked[place] = summed if earlier is None else earlier[place][0] + summed
+                looked[place + shift] = summed if earlier is None else earlier[place][0] + summed
 
         @pl.when(step_at > 0)
         def _():
-            looked[at] += summed
+            looked[at + shift] += summed
 
     if not final:
         return
@@ -198,10 +202,10 @@
         pltpu.VMEM((steps, STEP, looked_cols), jnp.bfloat16),
     ]
     if final:
-        in_specs += [pl.BlockSpec(memory_space=pltpu.SMEM)] + [vmem] * 3
+        in_specs += [vmem, pl.BlockSpec(memory_space=pltpu.SMEM)] + [vmem] * 3
         out_shape = jax.ShapeDtypeStruct((looked_cols // 2 * MESSAGE, LANES), jnp.int32)
         scratch += [
-            pltpu.VMEM(looked_shape, jnp.float32),
+            pltpu.VMEM((2, 2 * pair_count * looks, looked_cols), jnp.float32),
             pltpu.VMEM((2, pair_count * looks, looked_cols), jnp.float32),
             pltpu.VMEM((8, LANES), jnp.int32),
             pltpu.VMEM((looked_cols, LANES), jnp.int32),
@@ -346,16 +350,14 @@
     late, words = lax.optimization_barrier((left, words))
     owned = [late[:, :, :, start:stop] for start, stop in CHUNKS]
     owned, combos = lax.optimization_barrier((owned, combos))
-    looked = ()
+    looked = [(), ()]
     for (start, stop), own, received in zip(CHUNKS, owned, others):
-        if stop < width:
-            upper = phases(start, stop, (0,), False, own, received[:1], looked[:1])
-            lower, upper = lax.optimization_barrier((received[1:], upper))
-            looked = [upper, phases(start, stop, (1,), False, own, lower, looked[1:])]
-        else:
-            payload = phases(
-                start, stop, (0, 1), True, own, received, looked, combos, cycle_maps, low_cycles, line
-            )
+        received, before = lax.optimization_barrier((received, looked[1]))
+        upper = phases(start, stop, (0,), False, own, received[:1], looked[0])
+        lower, upper = lax.optimization_barrier((received[1:], upper))
+        rest = (upper, combos, cycle_maps, low_cycles, line) if stop == width else ()
+        looked = [(upper,), (phases(start, stop, (1,), stop == width, own, lower, before, *rest),)]
+    payload = looked[1][0]
 
     payload, kept = lax.optimization_barrier((payload, kept))
     swapped = lax.ppermute(kept, "date", [(at, at ^ 1) for at in range(devices)])

time: 81.1 us -> 82 us (1.011)
  Pallas kernels: 17.8 us -> 18.7 us
    pallas_call x3 -> x4, Pallas kernels: 16.8 us -> 17.6 us  [phases(): pl.pallas_call(partial(phase_kernel, start // LOOK_C, stop // LOOK_C, sid...]
  transfers between devices with their start and end apart: 12 -> 12, of which waited for: 6 -> 6; matrix products, arithmetic and copies ran while one was open for 15% -> 15% of each run, Pallas kernels for 21% -> 22%
where the time goes in v10:
time: 82 us; the launch traced here: 81.4 us
  starting transfers between devices  31.9 us (39%)
  Pallas kernels  18.7 us (23%)
  waiting for transfers between devices  17.2 us (21%)
  local copies, waits for them, and re-layouts  12.5 us (15%)
  other arithmetic  0.95 us (1%)
    pallas_call x4, Pallas kernels, phases(): pl.pallas_call(partial(phase_kernel, start // LOOK_C, stop // LOOK_C, sid...  17.6 us
    all_to_all x1, starting transfers between devices, sent_inverse(): lax.all_to_all(sent.reshape(devices, per, LANES), 'date', split_axis=0, c...  10.7 us
    ppermute x9, starting transfers between devices, passed_along(): return lax.ppermute(value, axis, pairs)  10.6 us
    all_to_all x1, starting transfers between devices, body(): lax.all_to_all(payload.reshape(devices, 1, -1), 'date', split_axis=0, con...  10.3 us
    ppermute x9, waiting for transfers between devices, passed_along(): return lax.ppermute(value, axis, pairs)  7.94 us
    all_to_all x1, waiting for transfers between devices, body(): lax.all_to_all(payload.reshape(devices, 1, -1), 'date', split_axis=0, con...  7.91 us
    slice x2, local copies, waits for them, and re-layouts, parts(): return (images[:, :, :rows, start:stop], images[:, :, rows:, start:stop])  6.21 us
    slice x2, local copies, waits for them, and re-layouts, body(): owned = [late[:, :, :, start:stop] for start, stop in CHUNKS]  4.5 us
  transfers between devices with their start and end apart: 12, of which 6 were waited for; matrix products, arithmetic and copies ran while one was open for 15% of the time, Pallas kernels for 22%

profile of v10, /device:TPU:6, one launch (start us, length us, event | category | flops | bytes accessed | tf_op | source)
XLA Modules:
  0.0 81.4 jit_solution(534909630451431958)
XLA Ops:
  0.0 0.0 collective-permute-start
  0.0 2.0 %collective-permute-start.1 = (s32[16,32,128]{2,1,0:T(8,128)}, s32[16,32,128]{2,1,0:T(8,128)S(1)}, u32[]{:S(2)}, u32[]{:S(2)}) collective-permute-start(s32[16,32,128]{2,1,0:T(8,128)} %refs_4_.1), channel_id=1, source_target_pairs={{0,4},{4,8},{8,12},{12,16},{16,20},{20,24},{24,28},{28,32},{32,36}... | collective-permute-start | bytes 786440 | tf_op jit(solution)/shard_map/ppermute | solution.py:34
  2.0 3.8 %fusion.9 = (bf16[4,2,64,1536]{3,2,1,0:T(8,128)(2,1)}, bf16[4,2,64,1536]{3,2,1,0:T(8,128)(2,1)}) fusion(bf16[4,2,128,2048]{3,2,1,0:T(8,128)(2,1)} %param.4), kind=kLoop, calls=%fused_computation.24 | loop fusion | bytes 6291456 | tf_op jit(solution)/shard_map/slice | solution.py:328
  5.9 1.2 %collective-permute-done = s32[16,2]{0,1:T(2,128)S(1)} collective-permute-done((s32[16,2]{0,1:T(2,128)}, s32[16,2]{0,1:T(2,128)S(1)}, u32[]{:S(2)}, u32[]{:S(2)}) %collective-permute-start) | collective-permute-done | bytes 160 | tf_op jit(solution)/shard_map/ppermute | solution.py:34
  7.0 2.9 %collective-permute-done.1.refs_5_ = s32[16,32,128]{2,1,0:T(8,128)S(1)} collective-permute-done((s32[16,32,128]{2,1,0:T(8,128)}, s32[16,32,128]{2,1,0:T(8,128)S(1)}, u32[]{:S(2)}, u32[]{:S(2)}) %collective-permute-start.1) | collective-permute-done | bytes 262176 | tf_op jit(solution)/shard_map/ppermute | solution.py:34
  9.9 0.7 copy-done.2
  10.6 0.0 collective-permute-start.4
  10.6 0.5 collective-permute-start.5
  11.1 0.0 copy-done.4
  11.1 0.1 abs_reduce_fusion
  11.2 0.1 convert_bitcast_fusion
  11.3 2.4 %fusion.8 = (bf16[4,2,64,512]{3,2,1,0:T(8,128)(2,1)}, bf16[4,2,64,512]{3,2,1,0:T(8,128)(2,1)}) fusion(bf16[4,2,128,2048]{3,2,1,0:T(8,128)(2,1)} %param.4), kind=kLoop, calls=%fused_computation.23 | loop fusion | bytes 2097152 | tf_op jit(solution)/shard_map/slice | solution.py:328
  13.7 3.3 %collective-permute-start.2 = (bf16[4,2,64,512]{3,2,1,0:T(8,128)(2,1)}, bf16[4,2,64,512]{3,2,1,0:T(8,128)(2,1)}, u32[]{:S(2)}, u32[]{:S(2)}) collective-permute-start(bf16[4,2,64,512]{3,2,1,0:T(8,128)(2,1)} %get-tuple-element.41), channel_id=1, source_target_pairs={{0,252},{4,0},{8,4},{12,8},{16,12},{20,16},{24,20},{28,24},{32,28}... | collective-permute-start | bytes 1572872 | tf_op jit(solution)/shard_map/ppermute | solution.py:34
  17.1 0.0 collective-permute-start.3
  17.1 0.7 broadcast_in_dim.18
  17.8 10.7 %all-to-all-start = ((s32[64,8,128]{2,1,0:T(8,128)}), s32[64,8,128]{2,1,0:T(8,128)S(1)}, u32[]{:S(2)}, u32[]{:S(2)}) async-start(s32[64,8,128]{2,1,0:T(8,128)} %bitcast.6), calls=%async_computation | async-start | bytes 524288 | tf_op jit(solution)/shard_map/all_to_all | solution.py:248
  28.5 2.3 %slice.50.own = bf16[4,2,128,512]{3,2,1,0:T(8,128)(2,1)} slice(bf16[4,2,128,2048]{3,2,1,0:T(8,128)(2,1)} %param.4), slice={[0:4], [0:2], [0:128], [1536:2048]} | slice | bytes 2097152 | tf_op jit(solution)/shard_map/slice | solution.py:351
  30.8 2.2 %slice.49.own = bf16[4,2,128,1536]{3,2,1,0:T(8,128)(2,1)S(1)} slice(bf16[4,2,128,2048]{3,2,1,0:T(8,128)(2,1)} %param.4), slice={[0:4], [0:2], [0:128], [0:1536]} | slice | bytes 6291456 | tf_op jit(solution)/shard_map/slice | solution.py:351
  33.0 0.1 reshape.58
  33.1 0.1 copy.8
  33.2 0.1 pad.4.clone
  33.3 0.1 broadcast_in_dim.15
  33.3 0.0 copy-done.5
  33.3 0.1 pad_add_fusion
  33.4 0.0 collective-permute-done.4.refs_0_
  33.5 0.0 collective-permute-done.5.refs_0_
  33.5 5.4 %phases.4.refs_1_ = f32[1,512,128]{2,1,0:T(8,128)S(1)} custom-call(bf16[4,2,128,1536]{3,2,1,0:T(8,128)(2,1)S(1)} %slice.49.own, bf16[4,2,64,1536]{3,2,1,0:T(8,128)(2,1)} %collective-permute-done.4.refs_0_), custom_call_target="tpu_custom_call" | custom-call | flops 12582912 | bytes 6291456 | tf_op jit(solution)/shard_map/phases/pallas_call | solution.py:213
  38.8 0.0 copy-start
  38.8 5.5 %phases.5.refs_1_ = f32[1,512,128]{2,1,0:T(8,128)S(1)} custom-call(bf16[4,2,128,1536]{3,2,1,0:T(8,128)(2,1)S(1)} %slice.49.own, bf16[4,2,64,1536]{3,2,1,0:T(8,128)(2,1)} %collective-permute-done.5.refs_0_), custom_call_target="tpu_custom_call" | custom-call | flops 12582912 | bytes 6291456 | tf_op jit(solution)/shard_map/phases/pallas_call | solution.py:213
  44.3 0.0 copy-start.1
  44.3 0.0 copy-start.3
  44.3 0.0 collective-permute-done.2.refs_0_
  44.4 0.0 collective-permute-done.3.refs_0_
  44.4 2.4 %phases.6.refs_2_ = f32[1,512,128]{2,1,0:T(8,128)S(1)} custom-call(bf16[4,2,128,512]{3,2,1,0:T(8,128)(2,1)S(1)} %copy-done, bf16[4,2,64,512]{3,2,1,0:T(8,128)(2,1)} %collective-permute-done.2.refs_0_, f32[1,512,128]{2,1,0:T(8,128)S(1)} %phases.4.refs_1_), custom_call_target="tpu_custom_call" | custom-call | flops 4194304 | bytes 2097152 | tf_op jit(solution)/shard_map/phases/pallas_call | solution.py:213
  46.8 4.4 %phases.7 = s32[320,128]{1,0:T(8,128)} custom-call(bf16[4,2,128,512]{3,2,1,0:T(8,128)(2,1)S(1)} %copy-done, bf16[4,2,64,512]{3,2,1,0:T(8,128)(2,1)} %collective-permute-done.3.refs_0_, f32[1,512,128]{2,1,0:T(8,128)S(1)} %phases.5.refs_1_, f32[1,512,128]{2,1,0:T(8,128)S(1)} %phases.6.refs_2_, s32[32]{0:T(128)S(1)} %fusion.6.refs_3_, ...), custom_call_target="tpu_custom_call" | custom-call | flops 4194304 | bytes 2097152 | tf_op jit(solution)/shard_map/phases/pallas_call | solution.py:213
  51.2 0.0 all-to-all-done
  51.2 10.3 %all-to-all-start.1 = ((s32[64,1,640]{2,1,0:T(1,128)}), s32[64,1,640]{2,1,0:T(1,128)S(1)}, u32[]{:S(2)}, u32[]{:S(2)}) async-start(s32[64,1,640]{2,1,0:T(1,128)} %bitcast.8), calls=%async_computation.1 | async-start | bytes 327680 | tf_op jit(solution)/shard_map/all_to_all | solution.py:364
  61.6 0.2 collective-permute-start.6
  61.8 1.4 %collective-permute-done.6.swapped = s32[512,128]{1,0:T(8,128)S(1)} collective-permute-done((s32[512,128]{1,0:T(8,128)S(1)}, s32[512,128]{1,0:T(8,128)S(1)}, u32[]{:S(2)}, u32[]{:S(2)}) %collective-permute-start.6) | collective-permute-done | bytes 262176 | tf_op jit(solution)/shard_map/ppermute | solution.py:363
  63.2 7.9 %all-to-all-done.1 = s32[64,1,640]{2,1,0:T(1,128)S(1)} async-done(((s32[64,1,640]{2,1,0:T(1,128)}), s32[64,1,640]{2,1,0:T(1,128)S(1)}, u32[]{:S(2)}, u32[]{:S(2)}) %all-to-all-start.1) | async-done | bytes 163872 | tf_op jit(solution)/shard_map/all_to_all | solution.py:364
  71.1 1.1 %invert.1 = (f32[64,256]{1,0:T(8,128)S(1)}, f32[8,256]{1,0:T(8,128)S(1)}) custom-call(s32[1]{0:T(128)} %bitcast.side, s32[320,128]{1,0:T(8,128)S(1)} %bitcast.28, s32[512,128]{1,0:T(8,128)S(1)} %bitcast.27, s32[512,128]{1,0:T(8,128)S(1)} %collective-permute-done.6.swapped), custom_call_target="tpu_custom_call" | custom-call | tf_op jit(solution)/shard_map/invert/pallas_call | solution.py:302
  72.2 3.1 %collective-permute-start.9 = (f32[8,256]{1,0:T(8,128)S(1)}, f32[8,256]{1,0:T(8,128)S(1)}, u32[]{:S(2)}, u32[]{:S(2)}) collective-permute-start(f32[8,256]{1,0:T(8,128)S(1)} %get-tuple-element.60), channel_id=1, source_target_pairs={{0,3},{1,0},{2,1},{3,2},{4,7},{5,4},{6,5},{7,6},{8,11},{9,8},{10,9... | collective-permute-start | bytes 24584 | tf_op jit(solution)/shard_map/ppermute | solution.py:34
  75.3 0.6 collective-permute-start.8
  75.9 1.0 %collective-permute-start.7 = (f32[8,256]{1,0:T(8,128)S(1)}, f32[8,256]{1,0:T(8,128)S(1)}, u32[]{:S(2)}, u32[]{:S(2)}) collective-permute-start(f32[8,256]{1,0:T(8,128)S(1)} %get-tuple-element.60), channel_id=1, source_target_pairs={{0,1},{1,2},{2,3},{3,0},{4,5},{5,6},{6,7},{7,4},{8,9},{9,10},{10,1... | collective-permute-start | bytes 24584 | tf_op jit(solution)/shard_map/ppermute | solution.py:34
  76.9 0.0 collective-permute-done.9
  76.9 3.5 %collective-permute-done.8 = f32[8,256]{1,0:T(8,128)S(1)} collective-permute-done((f32[8,256]{1,0:T(8,128)S(1)}, f32[8,256]{1,0:T(8,128)S(1)}, u32[]{:S(2)}, u32[]{:S(2)}) %collective-permute-start.8) | collective-permute-done | bytes 8224 | tf_op jit(solution)/shard_map/ppermute | solution.py:34
  80.4 0.3 collective-permute-done.7
  80.8 0.6 subtract_subtract_fusion
  (14 shorter events, 0.1 us)
Async XLA Ops:
  0.0 11.1 %copy-start.4 = (f32[256,16]{0,1:T(8,128)S(1)}, f32[256,16]{0,1:T(8,128)}, u32[]{:S(2)}) copy-start(f32[256,16]{0,1:T(8,128)} %param.7) | copy-start | bytes 49156
  0.0 7.0 %collective-permute-start = (s32[16,2]{0,1:T(2,128)}, s32[16,2]{0,1:T(2,128)S(1)}, u32[]{:S(2)}, u32[]{:S(2)}) collective-permute-start(s32[16,2]{0,1:T(2,128)} %param.5), channel_id=1, source_target_pairs={{0,4},{4,8},{8,12},{12,16},{16,20},{20,24},{24,28},{28,32},{32,36}... | collective-permute-start | bytes 392 | tf_op jit(solution)/shard_map/ppermute | solution.py:34
  0.0 9.9 %collective-permute-start.1 = (s32[16,32,128]{2,1,0:T(8,128)}, s32[16,32,128]{2,1,0:T(8,128)S(1)}, u32[]{:S(2)}, u32[]{:S(2)}) collective-permute-start(s32[16,32,128]{2,1,0:T(8,128)} %refs_4_.1), channel_id=1, source_target_pairs={{0,4},{4,8},{8,12},{12,16},{16,20},{20,24},{24,28},{28,32},{32,36}... | collective-permute-start | bytes 786440 | tf_op jit(solution)/shard_map/ppermute | solution.py:34
  9.9 0.7 copy-start.2
  10.6 22.8 %collective-permute-start.4 = (bf16[4,2,64,1536]{3,2,1,0:T(8,128)(2,1)}, bf16[4,2,64,1536]{3,2,1,0:T(8,128)(2,1)}, u32[]{:S(2)}, u32[]{:S(2)}) collective-permute-start(bf16[4,2,64,1536]{3,2,1,0:T(8,128)(2,1)} %get-tuple-element.44), channel_id=1, source_target_pairs={{0,252},{4,0},{8,4},{12,8},{16,12},{20,16},{24,20},{28,24},{32,28}... | collective-permute-start | bytes 4718600 | tf_op jit(solution)/shard_map/ppermute | solution.py:34
  10.6 22.9 %collective-permute-start.5 = (bf16[4,2,64,1536]{3,2,1,0:T(8,128)(2,1)}, bf16[4,2,64,1536]{3,2,1,0:T(8,128)(2,1)}, u32[]{:S(2)}, u32[]{:S(2)}) collective-permute-start(bf16[4,2,64,1536]{3,2,1,0:T(8,128)(2,1)} %get-tuple-element.45), channel_id=1, source_target_pairs={{0,4},{4,8},{8,12},{12,16},{16,20},{20,24},{24,28},{28,32},{32,36}... | collective-permute-start | bytes 4718600 | tf_op jit(solution)/shard_map/ppermute | solution.py:34
  13.7 30.6 %collective-permute-start.2 = (bf16[4,2,64,512]{3,2,1,0:T(8,128)(2,1)}, bf16[4,2,64,512]{3,2,1,0:T(8,128)(2,1)}, u32[]{:S(2)}, u32[]{:S(2)}) collective-permute-start(bf16[4,2,64,512]{3,2,1,0:T(8,128)(2,1)} %get-tuple-element.41), channel_id=1, source_target_pairs={{0,252},{4,0},{8,4},{12,8},{16,12},{20,16},{24,20},{28,24},{32,28}... | collective-permute-start | bytes 1572872 | tf_op jit(solution)/shard_map/ppermute | solution.py:34
  17.1 27.3 %collective-permute-start.3 = (bf16[4,2,64,512]{3,2,1,0:T(8,128)(2,1)}, bf16[4,2,64,512]{3,2,1,0:T(8,128)(2,1)}, u32[]{:S(2)}, u32[]{:S(2)}) collective-permute-start(bf16[4,2,64,512]{3,2,1,0:T(8,128)(2,1)} %get-tuple-element.42), channel_id=1, source_target_pairs={{0,4},{4,8},{8,12},{12,16},{16,20},{20,24},{24,28},{28,32},{32,36}... | collective-permute-start | bytes 1572872 | tf_op jit(solution)/shard_map/ppermute | solution.py:34
  17.8 33.5 %all-to-all-start = ((s32[64,8,128]{2,1,0:T(8,128)}), s32[64,8,128]{2,1,0:T(8,128)S(1)}, u32[]{:S(2)}, u32[]{:S(2)}) async-start(s32[64,8,128]{2,1,0:T(8,128)} %bitcast.6), calls=%async_computation | async-start | bytes 524288 | tf_op jit(solution)/shard_map/all_to_all | solution.py:248
  30.8 2.6 %copy-start.5 = (s32[16,2]{0,1:T(2,128)S(1)}, s32[16,2]{0,1:T(2,128)}, u32[]{:S(2)}) copy-start(s32[16,2]{0,1:T(2,128)} %param.5) | copy-start | bytes 388
  38.8 5.5 %copy-start = (bf16[4,2,128,512]{3,2,1,0:T(8,128)(2,1)S(1)}, bf16[4,2,128,512]{3,2,1,0:T(8,128)(2,1)}, u32[]{:S(2)}) copy-start(bf16[4,2,128,512]{3,2,1,0:T(8,128)(2,1)} %slice.50.own) | copy-start | bytes 3145732
  44.3 2.5 %copy-start.1 = (s32[16,32,128]{2,1,0:T(8,128)S(1)}, s32[16,32,128]{2,1,0:T(8,128)}, u32[]{:S(2)}) copy-start(s32[16,32,128]{2,1,0:T(8,128)} %refs_4_.1) | copy-start | bytes 786436
  44.3 2.5 %copy-start.3 = (s32[16,32,128]{2,1,0:T(8,128)S(1)}, s32[16,32,128]{2,1,0:T(8,128)}, u32[]{:S(2)}) copy-start(s32[16,32,128]{2,1,0:T(8,128)} %copy-done.2) | copy-start | bytes 786436
  51.2 19.9 %all-to-all-start.1 = ((s32[64,1,640]{2,1,0:T(1,128)}), s32[64,1,640]{2,1,0:T(1,128)S(1)}, u32[]{:S(2)}, u32[]{:S(2)}) async-start(s32[64,1,640]{2,1,0:T(1,128)} %bitcast.8), calls=%async_computation.1 | async-start | bytes 327680 | tf_op jit(solution)/shard_map/all_to_all | solution.py:364
  61.6 1.6 %collective-permute-start.6 = (s32[512,128]{1,0:T(8,128)S(1)}, s32[512,128]{1,0:T(8,128)S(1)}, u32[]{:S(2)}, u32[]{:S(2)}) collective-permute-start(s32[512,128]{1,0:T(8,128)S(1)} %bitcast.26), channel_id=1, source_target_pairs={{0,4},{4,0},{8,12},{12,8},{16,20},{20,16},{24,28},{28,24},{32,36},... | collective-permute-start | bytes 786440 | tf_op jit(solution)/shard_map/ppermute | solution.py:363
  72.2 4.7 %collective-permute-start.9 = (f32[8,256]{1,0:T(8,128)S(1)}, f32[8,256]{1,0:T(8,128)S(1)}, u32[]{:S(2)}, u32[]{:S(2)}) collective-permute-start(f32[8,256]{1,0:T(8,128)S(1)} %get-tuple-element.60), channel_id=1, source_target_pairs={{0,3},{1,0},{2,1},{3,2},{4,7},{5,4},{6,5},{7,6},{8,11},{9,8},{10,9... | collective-permute-start | bytes 24584 | tf_op jit(solution)/shard_map/ppermute | solution.py:34
  75.3 5.2 %collective-permute-start.8 = (f32[8,256]{1,0:T(8,128)S(1)}, f32[8,256]{1,0:T(8,128)S(1)}, u32[]{:S(2)}, u32[]{:S(2)}) collective-permute-start(f32[8,256]{1,0:T(8,128)S(1)} %get-tuple-element.60), channel_id=1, source_target_pairs={{0,2},{1,3},{2,0},{3,1},{4,6},{5,7},{6,4},{7,5},{8,10},{9,11},{10,... | collective-permute-start | bytes 24584 | tf_op jit(solution)/shard_map/ppermute | solution.py:34
  75.9 4.9 %collective-permute-start.7 = (f32[8,256]{1,0:T(8,128)S(1)}, f32[8,256]{1,0:T(8,128)S(1)}, u32[]{:S(2)}, u32[]{:S(2)}) collective-permute-start(f32[8,256]{1,0:T(8,128)S(1)} %get-tuple-element.60), channel_id=1, source_target_pairs={{0,1},{1,2},{2,3},{3,0},{4,5},{5,6},{6,7},{7,4},{8,9},{9,10},{10,1... | collective-permute-start | bytes 24584 | tf_op jit(solution)/shard_map/ppermute | solution.py:34

commit v11 on v10

--- a/solution.py
+++ b/solution.py
@@ -352,8 +352,10 @@
     owned, combos = lax.optimization_barrier((owned, combos))
     looked = [(), ()]
     for (start, stop), own, received in zip(CHUNKS, owned, others):
-        received, before = lax.optimization_barrier((received, looked[1]))
-        upper = phases(start, stop, (0,), False, own, received[:1], looked[0])
+        first, before = received[:1], looked[1]
+        if before:
+            first, before = lax.optimization_barrier((first, before))
+        upper = phases(start, stop, (0,), False, own, first, looked[0])
         lower, upper = lax.optimization_barrier((received[1:], upper))
         rest = (upper, combos, cycle_maps, low_cycles, line) if stop == width else ()
         looked = [(upper,), (phases(start, stop, (1,), stop == width, own, lower, before, *rest),)]

time: 82 us -> 82 us (level)
  no operation moved by 1% of the time
where the time goes in v11:
time: 82 us; the launch traced here: 81.4 us
  starting transfers between devices  31.9 us (39%)
  Pallas kernels  18.7 us (23%)
  waiting for transfers between devices  17.2 us (21%)
  local copies, waits for them, and re-layouts  12.4 us (15%)
  other arithmetic  0.95 us (1%)
    pallas_call x4, Pallas kernels, phases(): pl.pallas_call(partial(phase_kernel, start // LOOK_C, stop // LOOK_C, sid...  17.6 us
    all_to_all x1, starting transfers between devices, sent_inverse(): lax.all_to_all(sent.reshape(devices, per, LANES), 'date', split_axis=0, c...  10.7 us
    ppermute x9, starting transfers between devices, passed_along(): return lax.ppermute(value, axis, pairs)  10.6 us
    all_to_all x1, starting transfers between devices, body(): lax.all_to_all(payload.reshape(devices, 1, -1), 'date', split_axis=0, con...  10.3 us
    ppermute x9, waiting for transfers between devices, passed_along(): return lax.ppermute(value, axis, pairs)  7.94 us
    all_to_all x1, waiting for transfers between devices, body(): lax.all_to_all(payload.reshape(devices, 1, -1), 'date', split_axis=0, con...  7.91 us
    slice x2, local copies, waits for them, and re-layouts, parts(): return (images[:, :, :rows, start:stop], images[:, :, rows:, start:stop])  6.17 us
    slice x2, local copies, waits for them, and re-layouts, body(): owned = [late[:, :, :, start:stop] for start, stop in CHUNKS]  4.5 us
  transfers between devices with their start and end apart: 12, of which 6 were waited for; matrix products, arithmetic and copies ran while one was open for 15% of the time, Pallas kernels for 22%

profile of v11, /device:TPU:6, one launch (start us, length us, event | category | flops | bytes accessed | tf_op | source)
XLA Modules:
  0.0 81.4 jit_solution(16663232359834180423)
XLA Ops:
  0.0 0.0 collective-permute-start
  0.0 2.0 %collective-permute-start.1 = (s32[16,32,128]{2,1,0:T(8,128)}, s32[16,32,128]{2,1,0:T(8,128)S(1)}, u32[]{:S(2)}, u32[]{:S(2)}) collective-permute-start(s32[16,32,128]{2,1,0:T(8,128)} %refs_4_.1), channel_id=1, source_target_pairs={{0,4},{4,8},{8,12},{12,16},{16,20},{20,24},{24,28},{28,32},{32,36}... | collective-permute-start | bytes 786440 | tf_op jit(solution)/shard_map/ppermute | solution.py:34
  2.0 3.8 %fusion.9 = (bf16[4,2,64,1536]{3,2,1,0:T(8,128)(2,1)}, bf16[4,2,64,1536]{3,2,1,0:T(8,128)(2,1)}) fusion(bf16[4,2,128,2048]{3,2,1,0:T(8,128)(2,1)} %param.4), kind=kLoop, calls=%fused_computation.24 | loop fusion | bytes 6291456 | tf_op jit(solution)/shard_map/slice | solution.py:328
  5.9 1.2 %collective-permute-done = s32[16,2]{0,1:T(2,128)S(1)} collective-permute-done((s32[16,2]{0,1:T(2,128)}, s32[16,2]{0,1:T(2,128)S(1)}, u32[]{:S(2)}, u32[]{:S(2)}) %collective-permute-start) | collective-permute-done | bytes 160 | tf_op jit(solution)/shard_map/ppermute | solution.py:34
  7.0 2.9 %collective-permute-done.1.refs_5_ = s32[16,32,128]{2,1,0:T(8,128)S(1)} collective-permute-done((s32[16,32,128]{2,1,0:T(8,128)}, s32[16,32,128]{2,1,0:T(8,128)S(1)}, u32[]{:S(2)}, u32[]{:S(2)}) %collective-permute-start.1) | collective-permute-done | bytes 262176 | tf_op jit(solution)/shard_map/ppermute | solution.py:34
  9.9 0.7 copy-done.2
  10.6 0.0 collective-permute-start.5
  10.6 0.5 collective-permute-start.4
  11.1 0.0 copy-done.4
  11.1 0.1 abs_reduce_fusion
  11.2 0.1 convert_bitcast_fusion
  11.3 2.4 %fusion.8 = (bf16[4,2,64,512]{3,2,1,0:T(8,128)(2,1)}, bf16[4,2,64,512]{3,2,1,0:T(8,128)(2,1)}) fusion(bf16[4,2,128,2048]{3,2,1,0:T(8,128)(2,1)} %param.4), kind=kLoop, calls=%fused_computation.23 | loop fusion | bytes 2097152 | tf_op jit(solution)/shard_map/slice | solution.py:328
  13.7 3.3 %collective-permute-start.3 = (bf16[4,2,64,512]{3,2,1,0:T(8,128)(2,1)}, bf16[4,2,64,512]{3,2,1,0:T(8,128)(2,1)}, u32[]{:S(2)}, u32[]{:S(2)}) collective-permute-start(bf16[4,2,64,512]{3,2,1,0:T(8,128)(2,1)} %get-tuple-element.39), channel_id=1, source_target_pairs={{0,252},{4,0},{8,4},{12,8},{16,12},{20,16},{24,20},{28,24},{32,28}... | collective-permute-start | bytes 1572872 | tf_op jit(solution)/shard_map/ppermute | solution.py:34
  17.0 0.0 collective-permute-start.2
  17.0 0.7 broadcast_in_dim.18
  17.7 10.7 %all-to-all-start = ((s32[64,8,128]{2,1,0:T(8,128)}), s32[64,8,128]{2,1,0:T(8,128)S(1)}, u32[]{:S(2)}, u32[]{:S(2)}) async-start(s32[64,8,128]{2,1,0:T(8,128)} %bitcast.6), calls=%async_computation | async-start | bytes 524288 | tf_op jit(solution)/shard_map/all_to_all | solution.py:248
  28.5 2.3 %slice.50.own = bf16[4,2,128,512]{3,2,1,0:T(8,128)(2,1)} slice(bf16[4,2,128,2048]{3,2,1,0:T(8,128)(2,1)} %param.4), slice={[0:4], [0:2], [0:128], [1536:2048]} | slice | bytes 2097152 | tf_op jit(solution)/shard_map/slice | solution.py:351
  30.7 2.2 %slice.49.own = bf16[4,2,128,1536]{3,2,1,0:T(8,128)(2,1)S(1)} slice(bf16[4,2,128,2048]{3,2,1,0:T(8,128)(2,1)} %param.4), slice={[0:4], [0:2], [0:128], [0:1536]} | slice | bytes 6291456 | tf_op jit(solution)/shard_map/slice | solution.py:351
  33.0 0.1 reshape.58
  33.1 0.1 copy.8
  33.1 0.1 pad.4.clone
  33.2 0.1 broadcast_in_dim.15
  33.3 0.0 copy-done.5
  33.3 0.1 pad_add_fusion
  33.4 0.0 collective-permute-done.5.refs_0_
  33.4 5.4 %phases.4.refs_1_ = f32[1,512,128]{2,1,0:T(8,128)S(1)} custom-call(bf16[4,2,128,1536]{3,2,1,0:T(8,128)(2,1)S(1)} %slice.49.own, bf16[4,2,64,1536]{3,2,1,0:T(8,128)(2,1)} %collective-permute-done.5.refs_0_), custom_call_target="tpu_custom_call" | custom-call | flops 12582912 | bytes 6291456 | tf_op jit(solution)/shard_map/phases/pallas_call | solution.py:213
  38.8 0.0 collective-permute-done.4.refs_0_
  38.8 5.5 %phases.5.refs_1_ = f32[1,512,128]{2,1,0:T(8,128)S(1)} custom-call(bf16[4,2,128,1536]{3,2,1,0:T(8,128)(2,1)S(1)} %slice.49.own, bf16[4,2,64,1536]{3,2,1,0:T(8,128)(2,1)} %collective-permute-done.4.refs_0_), custom_call_target="tpu_custom_call" | custom-call | flops 12582912 | bytes 6291456 | tf_op jit(solution)/shard_map/phases/pallas_call | solution.py:213
  44.3 0.0 copy-start.1
  44.3 0.0 collective-permute-done.3.refs_0_
  44.3 2.4 %phases.6.refs_2_ = f32[1,512,128]{2,1,0:T(8,128)S(1)} custom-call(bf16[4,2,128,512]{3,2,1,0:T(8,128)(2,1)S(1)} %copy-done, bf16[4,2,64,512]{3,2,1,0:T(8,128)(2,1)} %collective-permute-done.3.refs_0_, f32[1,512,128]{2,1,0:T(8,128)S(1)} %phases.4.refs_1_), custom_call_target="tpu_custom_call" | custom-call | flops 4194304 | bytes 2097152 | tf_op jit(solution)/shard_map/phases/pallas_call | solution.py:213
  46.7 0.0 collective-permute-done.2.refs_0_
  46.7 0.0 copy-done.1
  46.7 0.0 copy-done.3
  46.8 4.4 %phases.7 = s32[320,128]{1,0:T(8,128)} custom-call(bf16[4,2,128,512]{3,2,1,0:T(8,128)(2,1)S(1)} %copy-done, bf16[4,2,64,512]{3,2,1,0:T(8,128)(2,1)} %collective-permute-done.2.refs_0_, f32[1,512,128]{2,1,0:T(8,128)S(1)} %phases.5.refs_1_, f32[1,512,128]{2,1,0:T(8,128)S(1)} %phases.6.refs_2_, s32[32]{0:T(128)S(1)} %fusion.6.refs_3_, ...), custom_call_target="tpu_custom_call" | custom-call | flops 4194304 | bytes 2097152 | tf_op jit(solution)/shard_map/phases/pallas_call | solution.py:213
  51.2 0.0 all-to-all-done
  51.2 10.3 %all-to-all-start.1 = ((s32[64,1,640]{2,1,0:T(1,128)}), s32[64,1,640]{2,1,0:T(1,128)S(1)}, u32[]{:S(2)}, u32[]{:S(2)}) async-start(s32[64,1,640]{2,1,0:T(1,128)} %bitcast.8), calls=%async_computation.1 | async-start | bytes 327680 | tf_op jit(solution)/shard_map/all_to_all | solution.py:366
  61.6 0.2 collective-permute-start.6
  61.8 1.4 %collective-permute-done.6.swapped = s32[512,128]{1,0:T(8,128)S(1)} collective-permute-done((s32[512,128]{1,0:T(8,128)S(1)}, s32[512,128]{1,0:T(8,128)S(1)}, u32[]{:S(2)}, u32[]{:S(2)}) %collective-permute-start.6) | collective-permute-done | bytes 262176 | tf_op jit(solution)/shard_map/ppermute | solution.py:365
  63.2 7.9 %all-to-all-done.1 = s32[64,1,640]{2,1,0:T(1,128)S(1)} async-done(((s32[64,1,640]{2,1,0:T(1,128)}), s32[64,1,640]{2,1,0:T(1,128)S(1)}, u32[]{:S(2)}, u32[]{:S(2)}) %all-to-all-start.1) | async-done | bytes 163872 | tf_op jit(solution)/shard_map/all_to_all | solution.py:366
  71.1 1.1 %invert.1 = (f32[64,256]{1,0:T(8,128)S(1)}, f32[8,256]{1,0:T(8,128)S(1)}) custom-call(s32[1]{0:T(128)} %bitcast.side, s32[320,128]{1,0:T(8,128)S(1)} %bitcast.28, s32[512,128]{1,0:T(8,128)S(1)} %bitcast.27, s32[512,128]{1,0:T(8,128)S(1)} %collective-permute-done.6.swapped), custom_call_target="tpu_custom_call" | custom-call | tf_op jit(solution)/shard_map/invert/pallas_call | solution.py:302
  72.1 3.1 %collective-permute-start.9 = (f32[8,256]{1,0:T(8,128)S(1)}, f32[8,256]{1,0:T(8,128)S(1)}, u32[]{:S(2)}, u32[]{:S(2)}) collective-permute-start(f32[8,256]{1,0:T(8,128)S(1)} %get-tuple-element.54), channel_id=1, source_target_pairs={{0,3},{1,0},{2,1},{3,2},{4,7},{5,4},{6,5},{7,6},{8,11},{9,8},{10,9... | collective-permute-start | bytes 24584 | tf_op jit(solution)/shard_map/ppermute | solution.py:34
  75.2 0.6 collective-permute-start.8
  75.9 1.0 %collective-permute-start.7 = (f32[8,256]{1,0:T(8,128)S(1)}, f32[8,256]{1,0:T(8,128)S(1)}, u32[]{:S(2)}, u32[]{:S(2)}) collective-permute-start(f32[8,256]{1,0:T(8,128)S(1)} %get-tuple-element.54), channel_id=1, source_target_pairs={{0,1},{1,2},{2,3},{3,0},{4,5},{5,6},{6,7},{7,4},{8,9},{9,10},{10,1... | collective-permute-start | bytes 24584 | tf_op jit(solution)/shard_map/ppermute | solution.py:34
  76.8 0.0 collective-permute-done.9
  76.8 3.5 %collective-permute-done.8 = f32[8,256]{1,0:T(8,128)S(1)} collective-permute-done((f32[8,256]{1,0:T(8,128)S(1)}, f32[8,256]{1,0:T(8,128)S(1)}, u32[]{:S(2)}, u32[]{:S(2)}) %collective-permute-start.8) | collective-permute-done | bytes 8224 | tf_op jit(solution)/shard_map/ppermute | solution.py:34
  80.4 0.3 collective-permute-done.7
  80.7 0.6 subtract_subtract_fusion
  (14 shorter events, 0.1 us)
Async XLA Ops:
  0.0 11.1 %copy-start.4 = (f32[256,16]{0,1:T(8,128)S(1)}, f32[256,16]{0,1:T(8,128)}, u32[]{:S(2)}) copy-start(f32[256,16]{0,1:T(8,128)} %param.7) | copy-start | bytes 49156
  0.0 7.0 %collective-permute-start = (s32[16,2]{0,1:T(2,128)}, s32[16,2]{0,1:T(2,128)S(1)}, u32[]{:S(2)}, u32[]{:S(2)}) collective-permute-start(s32[16,2]{0,1:T(2,128)} %param.5), channel_id=1, source_target_pairs={{0,4},{4,8},{8,12},{12,16},{16,20},{20,24},{24,28},{28,32},{32,36}... | collective-permute-start | bytes 392 | tf_op jit(solution)/shard_map/ppermute | solution.py:34
  0.0 9.9 %collective-permute-start.1 = (s32[16,32,128]{2,1,0:T(8,128)}, s32[16,32,128]{2,1,0:T(8,128)S(1)}, u32[]{:S(2)}, u32[]{:S(2)}) collective-permute-start(s32[16,32,128]{2,1,0:T(8,128)} %refs_4_.1), channel_id=1, source_target_pairs={{0,4},{4,8},{8,12},{12,16},{16,20},{20,24},{24,28},{28,32},{32,36}... | collective-permute-start | bytes 786440 | tf_op jit(solution)/shard_map/ppermute | solution.py:34
  9.9 0.7 copy-start.2
  10.6 22.8 %collective-permute-start.5 = (bf16[4,2,64,1536]{3,2,1,0:T(8,128)(2,1)}, bf16[4,2,64,1536]{3,2,1,0:T(8,128)(2,1)}, u32[]{:S(2)}, u32[]{:S(2)}) collective-permute-start(bf16[4,2,64,1536]{3,2,1,0:T(8,128)(2,1)} %get-tuple-element.42), channel_id=1, source_target_pairs={{0,252},{4,0},{8,4},{12,8},{16,12},{20,16},{24,20},{28,24},{32,28}... | collective-permute-start | bytes 4718600 | tf_op jit(solution)/shard_map/ppermute | solution.py:34
  10.6 28.2 %collective-permute-start.4 = (bf16[4,2,64,1536]{3,2,1,0:T(8,128)(2,1)}, bf16[4,2,64,1536]{3,2,1,0:T(8,128)(2,1)}, u32[]{:S(2)}, u32[]{:S(2)}) collective-permute-start(bf16[4,2,64,1536]{3,2,1,0:T(8,128)(2,1)} %get-tuple-element.41), channel_id=1, source_target_pairs={{0,4},{4,8},{8,12},{12,16},{16,20},{20,24},{24,28},{28,32},{32,36}... | collective-permute-start | bytes 4718600 | tf_op jit(solution)/shard_map/ppermute | solution.py:34
  13.7 30.6 %collective-permute-start.3 = (bf16[4,2,64,512]{3,2,1,0:T(8,128)(2,1)}, bf16[4,2,64,512]{3,2,1,0:T(8,128)(2,1)}, u32[]{:S(2)}, u32[]{:S(2)}) collective-permute-start(bf16[4,2,64,512]{3,2,1,0:T(8,128)(2,1)} %get-tuple-element.39), channel_id=1, source_target_pairs={{0,252},{4,0},{8,4},{12,8},{16,12},{20,16},{24,20},{28,24},{32,28}... | collective-permute-start | bytes 1572872 | tf_op jit(solution)/shard_map/ppermute | solution.py:34
  17.0 29.7 %collective-permute-start.2 = (bf16[4,2,64,512]{3,2,1,0:T(8,128)(2,1)}, bf16[4,2,64,512]{3,2,1,0:T(8,128)(2,1)}, u32[]{:S(2)}, u32[]{:S(2)}) collective-permute-start(bf16[4,2,64,512]{3,2,1,0:T(8,128)(2,1)} %get-tuple-element.38), channel_id=1, source_target_pairs={{0,4},{4,8},{8,12},{12,16},{16,20},{20,24},{24,28},{28,32},{32,36}... | collective-permute-start | bytes 1572872 | tf_op jit(solution)/shard_map/ppermute | solution.py:34
  17.7 33.5 %all-to-all-start = ((s32[64,8,128]{2,1,0:T(8,128)}), s32[64,8,128]{2,1,0:T(8,128)S(1)}, u32[]{:S(2)}, u32[]{:S(2)}) async-start(s32[64,8,128]{2,1,0:T(8,128)} %bitcast.6), calls=%async_computation | async-start | bytes 524288 | tf_op jit(solution)/shard_map/all_to_all | solution.py:248
  30.7 2.6 %copy-start.5 = (s32[16,2]{0,1:T(2,128)S(1)}, s32[16,2]{0,1:T(2,128)}, u32[]{:S(2)}) copy-start(s32[16,2]{0,1:T(2,128)} %param.5) | copy-start | bytes 388
  38.8 5.5 %copy-start = (bf16[4,2,128,512]{3,2,1,0:T(8,128)(2,1)S(1)}, bf16[4,2,128,512]{3,2,1,0:T(8,128)(2,1)}, u32[]{:S(2)}) copy-start(bf16[4,2,128,512]{3,2,1,0:T(8,128)(2,1)} %slice.50.own) | copy-start | bytes 3145732
  44.3 2.5 %copy-start.1 = (s32[16,32,128]{2,1,0:T(8,128)S(1)}, s32[16,32,128]{2,1,0:T(8,128)}, u32[]{:S(2)}) copy-start(s32[16,32,128]{2,1,0:T(8,128)} %refs_4_.1) | copy-start | bytes 786436
  44.3 2.5 %copy-start.3 = (s32[16,32,128]{2,1,0:T(8,128)S(1)}, s32[16,32,128]{2,1,0:T(8,128)}, u32[]{:S(2)}) copy-start(s32[16,32,128]{2,1,0:T(8,128)} %copy-done.2) | copy-start | bytes 786436
  51.2 19.9 %all-to-all-start.1 = ((s32[64,1,640]{2,1,0:T(1,128)}), s32[64,1,640]{2,1,0:T(1,128)S(1)}, u32[]{:S(2)}, u32[]{:S(2)}) async-start(s32[64,1,640]{2,1,0:T(1,128)} %bitcast.8), calls=%async_computation.1 | async-start | bytes 327680 | tf_op jit(solution)/shard_map/all_to_all | solution.py:366
  61.6 1.6 %collective-permute-start.6 = (s32[512,128]{1,0:T(8,128)S(1)}, s32[512,128]{1,0:T(8,128)S(1)}, u32[]{:S(2)}, u32[]{:S(2)}) collective-permute-start(s32[512,128]{1,0:T(8,128)S(1)} %bitcast.26), channel_id=1, source_target_pairs={{0,4},{4,0},{8,12},{12,8},{16,20},{20,16},{24,28},{28,24},{32,36},... | collective-permute-start | bytes 786440 | tf_op jit(solution)/shard_map/ppermute | solution.py:365
  72.1 4.7 %collective-permute-start.9 = (f32[8,256]{1,0:T(8,128)S(1)}, f32[8,256]{1,0:T(8,128)S(1)}, u32[]{:S(2)}, u32[]{:S(2)}) collective-permute-start(f32[8,256]{1,0:T(8,128)S(1)} %get-tuple-element.54), channel_id=1, source_target_pairs={{0,3},{1,0},{2,1},{3,2},{4,7},{5,4},{6,5},{7,6},{8,11},{9,8},{10,9... | collective-permute-start | bytes 24584 | tf_op jit(solution)/shard_map/ppermute | solution.py:34
  75.2 5.2 %collective-permute-start.8 = (f32[8,256]{1,0:T(8,128)S(1)}, f32[8,256]{1,0:T(8,128)S(1)}, u32[]{:S(2)}, u32[]{:S(2)}) collective-permute-start(f32[8,256]{1,0:T(8,128)S(1)} %get-tuple-element.54), channel_id=1, source_target_pairs={{0,2},{1,3},{2,0},{3,1},{4,6},{5,7},{6,4},{7,5},{8,10},{9,11},{10,... | collective-permute-start | bytes 24584 | tf_op jit(solution)/shard_map/ppermute | solution.py:34
  75.9 4.9 %collective-permute-start.7 = (f32[8,256]{1,0:T(8,128)S(1)}, f32[8,256]{1,0:T(8,128)S(1)}, u32[]{:S(2)}, u32[]{:S(2)}) collective-permute-start(f32[8,256]{1,0:T(8,128)S(1)} %get-tuple-element.54), channel_id=1, source_target_pairs={{0,1},{1,2},{2,3},{3,0},{4,5},{5,6},{6,7},{7,4},{8,9},{9,10},{10,1... | collective-permute-start | bytes 24584 | tf_op jit(solution)/shard_map/ppermute | solution.py:34
